TPU v7x, 128 devices: a whole 4x4x4 slice. The times are simulated.
128 devices in a mesh: dp: 8 (over x, core), expert: 16 (over z, y).
Axes of the slice: x: 4, y: 4, z: 4, core: 2. Of those that a mesh axis runs over, the one named last changes fastest.
Arguments:
- tokens: bfloat16 [16, 2048, 1024], P('expert', 'dp'), may hold values from -6 to 6
- cotangent: bfloat16 [16, 2048, 1024], P('expert', 'dp'), may hold values from -6 to 6
- lengths: int32 [16], P('expert'), may hold values from 1793 to 2048, as said below
- routes: int32 [16, 2048, 8], P('expert', 'dp'), may hold values from 0 to 31, all different within a row; in each aligned block of 256 rows (0 to 255, 256 to 511, ..., all dimensions but the last counted through in order) at most 80 rows name the same one
- attn_gain: bfloat16 [1024], replicated, may hold values from 0.099609375 to 1.8984375
- w_query: bfloat16 [1024, 1024], replicated, may hold values from -0.1875 to 0.1875
- w_key: bfloat16 [1024, 512], replicated, may hold values from -0.1875 to 0.1875
- w_value: bfloat16 [1024, 512], replicated, may hold values from -0.1875 to 0.1875
- query_gain: bfloat16 [1024], replicated, may hold values from 0.099609375 to 1.8984375
- key_gain: bfloat16 [512], replicated, may hold values from 0.099609375 to 1.8984375
- w_output: bfloat16 [1024, 1024], replicated, may hold values from -2 to 2
- ffn_gain: bfloat16 [1024], replicated, may hold values from 0.099609375 to 1.8984375
- w_router: bfloat16 [1024, 32], replicated, may hold values from -0.09375 to 0.09375
- w_gate: bfloat16 [32, 1024, 512], P('expert'), may hold values from -0.1875 to 0.1875
- w_up: bfloat16 [32, 1024, 512], P('expert'), may hold values from -0.1875 to 0.1875
- w_down: bfloat16 [32, 512, 1024], P('expert'), may hold values from -1 to 1
Outputs:
- mixed_out: bfloat16 [16, 2048, 1024], P('expert', 'dp')
- token_grad: bfloat16 [16, 2048, 1024], P('expert', 'dp')
- attn_gain_grad: float32 [1024], replicated
- w_query_grad: float32 [1024, 1024], replicated
- w_key_grad: float32 [1024, 512], replicated
- w_value_grad: float32 [1024, 512], replicated
- query_gain_grad: float32 [1024], replicated
- key_gain_grad: float32 [512], replicated
- w_output_grad: float32 [1024, 1024], replicated
- ffn_gain_grad: float32 [1024], replicated
- w_router_grad: float32 [1024, 32], replicated
- w_gate_grad: float32 [32, 1024, 512], P('expert')
- w_up_grad: float32 [32, 1024, 512], P('expert')
- w_down_grad: float32 [32, 512, 1024], P('expert')
Inputs may be any that keep to these rules, and one draw needn't show every extreme that they name: `lengths`: one of the 16 sequences is full; positions at or past a sequence's length are padding. `routes`: each row names 8 different experts; among the 256 rows of one device no expert is named by more than 80 rows, and in some devices' rows one expert is named by exactly 80.
All inputs are finite; a program needn't handle non-finite values.
Results may differ from a plain program's by a relative error of at most 0.025.
Values may be sent and summed in bfloat16 or wider, within the bound.
A program may use at most 192 MiB of HBM per device.

v0:
```python
import math

import jax
import jax.numpy as jnp
from jax import lax
from jax.sharding import PartitionSpec as P

HEADS = 16
KV_HEADS = 8
HEAD_DIM = 64
EXPERTS = 32
TOPK = 8
CAP = 80


epsilon = 1e-06
HIGHEST = lax.Precision.HIGHEST


def in_one_piece(arrays, axis, dim, along):
    widths = [a.shape[along] for a in arrays]
    both = jnp.concatenate(arrays, axis=along)
    whole = lax.all_gather(both, axis, axis=dim, tiled=True)
    return tuple(jnp.split(whole, [sum(widths[:k]) for k in range(1, len(widths))], axis=along))


def sent_together(arrays, axis, dim, along):
    widths = [a.shape[along] for a in arrays]
    both = jnp.concatenate(arrays, axis=along)
    whole = lax.psum_scatter(both, axis, scatter_dimension=dim, tiled=True)
    return tuple(jnp.split(whole, [sum(widths[:k]) for k in range(1, len(widths))], axis=along))


def together(arrays, axis):
    vector, at, finished = (jnp.concatenate([a.reshape(-1) for a in arrays]), 0, [])
    so_far = lax.psum(vector, axis)
    for a in arrays:
        finished.append(so_far[at : at + a.size].reshape(a.shape))
        at += a.size
    return tuple(finished)


def norm_rows(values, norm_gain):
    return (
        values * lax.rsqrt(jnp.mean(values * values, axis=-1, keepdims=True) + epsilon) * norm_gain
    )


def rope_tables(positions):
    steps_half = jnp.arange(HEAD_DIM // 2).astype(jnp.float32)
    inverse = jnp.exp(steps_half * (-2.0 * math.log(10000.0) / HEAD_DIM))
    angles = positions.astype(jnp.float32)[:, None] * inverse[None, :]
    return (jnp.cos(angles), jnp.sin(angles))


def rotate(values, cosine, sine_table):
    count_rows = values.shape[0]
    heads_view = values.reshape(count_rows, -1, HEAD_DIM)
    front_half = heads_view[..., : HEAD_DIM // 2]
    back_half = heads_view[..., HEAD_DIM // 2 :]
    cosine_rows = cosine[:, None, :]
    sine_rows = sine_table[:, None, :]
    turned = jnp.concatenate(
        [
            front_half * cosine_rows - back_half * sine_rows,
            back_half * cosine_rows + front_half * sine_rows,
        ],
        axis=-1,
    )
    return turned.reshape(count_rows, -1)


def contract_rows(left, right):
    return lax.dot_general(
        left, right, (((0,), (0,)), ((), ())), preferred_element_type=jnp.float32
    )


def times_transposed(left, right):
    return lax.dot_general(
        left, right, (((1,), (1,)), ((), ())), preferred_element_type=jnp.float32
    )


def masked_scores(query_pair, key_head, key_valid):
    scores = jnp.einsum(
        "trd,sd->rts", query_pair, key_head, preferred_element_type=jnp.float32
    ) * HEAD_DIM ** (-0.5)
    return jnp.where(key_valid[None], scores, -1e30)


def forward_head(operands, key_valid):
    query_pair, key_head, value_head = operands
    scores = masked_scores(query_pair, key_head, key_valid)
    top_score = jnp.max(scores, axis=-1, keepdims=True)
    log_total = top_score + jnp.log(jnp.sum(jnp.exp(scores - top_score), axis=-1, keepdims=True))
    probs = jnp.exp(scores - log_total).astype(jnp.bfloat16)
    mixed = jnp.einsum("rts,sd->trd", probs, value_head, preferred_element_type=jnp.float32)
    return (mixed, log_total[..., 0])


def backward_head(operands, key_valid):
    query_pair, key_head, value_head, grad_pair, log_total = operands
    scores = masked_scores(query_pair, key_head, key_valid)
    probs = jnp.exp(scores - log_total[..., None])
    grad_probs = jnp.einsum(
        "trd,sd->rts", grad_pair, value_head, preferred_element_type=jnp.float32
    )
    score_grad = (
        probs * (grad_probs - jnp.sum(probs * grad_probs, axis=-1, keepdims=True))
    ).astype(jnp.bfloat16)
    query_grad = jnp.einsum(
        "rts,sd->trd", score_grad, key_head, preferred_element_type=jnp.float32
    ) * HEAD_DIM ** (-0.5)
    key_grad = jnp.einsum(
        "rts,trd->sd", score_grad, query_pair, preferred_element_type=jnp.float32
    ) * HEAD_DIM ** (-0.5)
    value_grad = jnp.einsum(
        "rts,trd->sd", probs.astype(jnp.bfloat16), grad_pair, preferred_element_type=jnp.float32
    )
    return (query_grad, key_grad, value_grad)


def body(
    tokens,
    cotangent,
    lengths,
    routes,
    attn_gain,
    w_query,
    w_key,
    w_value,
    query_gain,
    key_gain,
    w_output,
    ffn_gain,
    w_router,
    w_gate,
    w_up,
    w_down,
):
    token_rows = tokens[0].astype(jnp.float32)
    tok_count = token_rows.shape[0]
    width = token_rows.shape[1]
    kv_width = w_key.shape[1]
    seq_total = tok_count * lax.axis_size("dp")
    query_pos = lax.axis_index("dp") * tok_count + jnp.arange(tok_count, dtype=jnp.int32)
    key_pos = jnp.arange(seq_total, dtype=jnp.int32)
    key_valid = (key_pos[None, :] <= query_pos[:, None]) & (key_pos[None, :] < lengths[0])
    cosine, sine_table = rope_tables(query_pos)
    normed_value, attn_pull = jax.vjp(norm_rows, token_rows, attn_gain.astype(jnp.float32))
    normed = normed_value.astype(jnp.bfloat16)
    query_raw = jnp.dot(normed, w_query, preferred_element_type=jnp.float32)
    key_raw = jnp.dot(normed, w_key, preferred_element_type=jnp.float32)
    value_raw = jnp.dot(normed, w_value, preferred_element_type=jnp.float32)

    def post_norm(query_in, key_in, gain_query, gain_key):
        return (
            rotate(norm_rows(query_in, gain_query), cosine, sine_table),
            rotate(norm_rows(key_in, gain_key), cosine, sine_table),
        )

    post_values, post_pull = jax.vjp(
        post_norm, query_raw, key_raw, query_gain.astype(jnp.float32), key_gain.astype(jnp.float32)
    )
    queries = post_values[0].astype(jnp.bfloat16)
    keys_own = post_values[1].astype(jnp.bfloat16)
    values_own = value_raw.astype(jnp.bfloat16)
    keys_full, values_full = in_one_piece((keys_own, values_own), "dp", 0, 1)
    query_groups = queries.reshape(tok_count, KV_HEADS, HEADS // KV_HEADS, HEAD_DIM).transpose(
        1, 0, 2, 3
    )
    key_groups = keys_full.reshape(seq_total, KV_HEADS, HEAD_DIM).transpose(1, 0, 2)
    value_groups = values_full.reshape(seq_total, KV_HEADS, HEAD_DIM).transpose(1, 0, 2)
    mixed_heads, log_totals = lax.map(
        lambda operands: forward_head(operands, key_valid), (query_groups, key_groups, value_groups)
    )
    attended = mixed_heads.transpose(1, 0, 2, 3).reshape(tok_count, width).astype(jnp.bfloat16)
    hidden_res = token_rows + jnp.dot(attended, w_output, preferred_element_type=jnp.float32)
    ffn_value, ffn_pull = jax.vjp(norm_rows, hidden_res, ffn_gain.astype(jnp.float32))
    ffn_in = ffn_value.astype(jnp.bfloat16)
    logits = jnp.dot(ffn_in, w_router, preferred_element_type=jnp.float32)
    route_rows = routes[0]
    choose = (route_rows[:, :, None] == jnp.arange(EXPERTS, dtype=jnp.int32)[None, None, :]).astype(
        jnp.float32
    )
    gates = jax.nn.softmax(jnp.einsum("tke,te->tk", choose, logits, precision=HIGHEST), axis=-1)
    pair_routes = route_rows.reshape(-1)
    member = (pair_routes[:, None] == jnp.arange(EXPERTS, dtype=jnp.int32)[None, :]).astype(
        jnp.int32
    )
    earlier = jnp.cumsum(member, axis=0) - member
    slots = jnp.sum(earlier * member, axis=-1)
    target = jnp.where(slots < CAP, pair_routes * CAP + slots, EXPERTS * CAP)
    groups = lax.axis_size("expert")
    local_count = w_gate.shape[0]

    def place_pairs(pair_values):
        filled = jnp.zeros((EXPERTS * CAP + 1, width), jnp.bfloat16).at[target].set(pair_values)
        return filled[: EXPERTS * CAP].reshape(groups, local_count, CAP, width)

    def collect_pairs(arrived_back):
        padded = jnp.concatenate(
            [arrived_back.reshape(EXPERTS * CAP, width), jnp.zeros((1, width), jnp.bfloat16)],
            axis=0,
        )
        return jnp.take(padded, target, axis=0).reshape(tok_count, TOPK, width)

    pair_rows = jnp.broadcast_to(ffn_in[:, None, :], (tok_count, TOPK, width)).reshape(-1, width)
    arrived_rows = lax.all_to_all(
        place_pairs(pair_rows), "expert", split_axis=0, concat_axis=0, tiled=True
    )
    gate_part = jnp.einsum(
        "slcd,ldf->slcf", arrived_rows, w_gate, preferred_element_type=jnp.float32
    )
    up_part = jnp.einsum("slcd,ldf->slcf", arrived_rows, w_up, preferred_element_type=jnp.float32)
    inner_part = (jax.nn.silu(gate_part) * up_part).astype(jnp.bfloat16)
    result_part = jnp.einsum(
        "slcf,lfd->slcd", inner_part, w_down, preferred_element_type=jnp.float32
    ).astype(jnp.bfloat16)
    returned = collect_pairs(
        lax.all_to_all(result_part, "expert", split_axis=0, concat_axis=0, tiled=True)
    )
    mixed_out = (hidden_res + jnp.sum(gates[:, :, None] * returned, axis=1)).astype(jnp.bfloat16)
    grad_out = cotangent[0].astype(jnp.float32)
    gate_grad = jnp.sum(grad_out[:, None, :] * returned, axis=-1)
    pair_grads = (gates[:, :, None] * grad_out[:, None, :]).astype(jnp.bfloat16).reshape(-1, width)
    grad_arrived = lax.all_to_all(
        place_pairs(pair_grads), "expert", split_axis=0, concat_axis=0, tiled=True
    )
    sigmoid_gate = jax.nn.sigmoid(gate_part)
    silu_gate = gate_part * sigmoid_gate
    inner = (silu_gate * up_part).astype(jnp.bfloat16)
    down_grad = jnp.einsum(
        "slcf,slcd->lfd", inner, grad_arrived, preferred_element_type=jnp.float32
    )
    inner_grad = jnp.einsum(
        "slcd,lfd->slcf", grad_arrived, w_down, preferred_element_type=jnp.float32
    )
    gate_pre_grad = (
        inner_grad * up_part * sigmoid_gate * (1.0 + gate_part * (1.0 - sigmoid_gate))
    ).astype(jnp.bfloat16)
    up_pre_grad = (inner_grad * silu_gate).astype(jnp.bfloat16)
    gate_w_grad = jnp.einsum(
        "slcd,slcf->ldf", arrived_rows, gate_pre_grad, preferred_element_type=jnp.float32
    )
    up_w_grad = jnp.einsum(
        "slcd,slcf->ldf", arrived_rows, up_pre_grad, preferred_element_type=jnp.float32
    )
    arrived_grad = jnp.einsum(
        "slcf,ldf->slcd", gate_pre_grad, w_gate, preferred_element_type=jnp.float32
    )
    arrived_grad = (
        arrived_grad
        + jnp.einsum("slcf,ldf->slcd", up_pre_grad, w_up, preferred_element_type=jnp.float32)
    ).astype(jnp.bfloat16)
    pair_in_grad = collect_pairs(
        lax.all_to_all(arrived_grad, "expert", split_axis=0, concat_axis=0, tiled=True)
    )
    gate_logit_grad = gates * (gate_grad - jnp.sum(gates * gate_grad, axis=-1, keepdims=True))
    logit_grad = jnp.einsum("tk,tke->te", gate_logit_grad, choose, precision=HIGHEST).astype(
        jnp.bfloat16
    )
    router_grad = contract_rows(ffn_in, logit_grad)
    ffn_in_grad = times_transposed(logit_grad, w_router) + jnp.sum(
        pair_in_grad, axis=1, dtype=jnp.float32
    )
    res_part, ffn_gain_grad = ffn_pull(ffn_in_grad)
    hidden_grad = grad_out + res_part
    branch_grad = hidden_grad.astype(jnp.bfloat16)
    output_w_grad = contract_rows(attended, branch_grad)
    attended_grad = times_transposed(branch_grad, w_output).astype(jnp.bfloat16)
    grad_groups = attended_grad.reshape(tok_count, KV_HEADS, HEADS // KV_HEADS, HEAD_DIM).transpose(
        1, 0, 2, 3
    )
    query_grad_heads, key_grad_heads, value_grad_heads = lax.map(
        lambda operands: backward_head(operands, key_valid),
        (query_groups, key_groups, value_groups, grad_groups, log_totals),
    )
    query_grad = query_grad_heads.transpose(1, 0, 2, 3).reshape(tok_count, width)
    key_grad_full = key_grad_heads.transpose(1, 0, 2).reshape(seq_total, kv_width)
    value_grad_full = value_grad_heads.transpose(1, 0, 2).reshape(seq_total, kv_width)
    key_grad, value_grad = tuple(
        (
            part.astype(jnp.float32)
            for part in sent_together(
                (key_grad_full.astype(jnp.bfloat16), value_grad_full.astype(jnp.bfloat16)),
                "dp",
                0,
                1,
            )
        )
    )
    query_raw_grad, key_raw_grad, query_gain_grad, key_gain_grad = post_pull((query_grad, key_grad))
    query_raw_low = query_raw_grad.astype(jnp.bfloat16)
    key_raw_low = key_raw_grad.astype(jnp.bfloat16)
    value_raw_low = value_grad.astype(jnp.bfloat16)
    query_w_grad = contract_rows(normed, query_raw_low)
    key_w_grad = contract_rows(normed, key_raw_low)
    value_w_grad = contract_rows(normed, value_raw_low)
    normed_grad = (
        times_transposed(query_raw_low, w_query)
        + times_transposed(key_raw_low, w_key)
        + times_transposed(value_raw_low, w_value)
    )
    token_part, attn_gain_grad = attn_pull(normed_grad)
    token_grad = (hidden_grad + token_part).astype(jnp.bfloat16)
    (
        attn_gain_sum,
        query_w_sum,
        key_w_sum,
        value_w_sum,
        query_gain_sum,
        key_gain_sum,
        output_w_sum,
        ffn_gain_sum,
        router_sum,
    ) = lax.psum(
        (
            attn_gain_grad,
            query_w_grad,
            key_w_grad,
            value_w_grad,
            query_gain_grad,
            key_gain_grad,
            output_w_grad,
            ffn_gain_grad,
            router_grad,
        ),
        ("dp", "expert"),
    )
    gate_w_sum, up_w_sum, down_w_sum = tuple(
        (
            part.astype(jnp.float32)
            for part in together(
                (
                    gate_w_grad.astype(jnp.bfloat16),
                    up_w_grad.astype(jnp.bfloat16),
                    down_grad.astype(jnp.bfloat16),
                ),
                "dp",
            )
        )
    )
    return (
        mixed_out[None],
        token_grad[None],
        attn_gain_sum,
        query_w_sum,
        key_w_sum,
        value_w_sum,
        query_gain_sum,
        key_gain_sum,
        output_w_sum,
        ffn_gain_sum,
        router_sum,
        gate_w_sum,
        up_w_sum,
        down_w_sum,
    )


def solution(mesh):
    return jax.shard_map(
        body,
        mesh=mesh,
        in_specs=(
            P("expert", "dp", None),
            P("expert", "dp", None),
            P("expert"),
            P("expert", "dp", None),
            P(),
            P(),
            P(),
            P(),
            P(),
            P(),
            P(),
            P(),
            P(),
            P("expert", None, None),
            P("expert", None, None),
            P("expert", None, None),
        ),
        out_specs=(
            P("expert", "dp", None),
            P("expert", "dp", None),
            P(),
            P(),
            P(),
            P(),
            P(),
            P(),
            P(),
            P(),
            P(),
            P("expert", None, None),
            P("expert", None, None),
            P("expert", None, None),
        ),
        check_vma=False,
    )
```

profile of v0, /device:TPU:1, one launch (start us, length us, event | category | flops | bytes accessed | tf_op | source)
XLA Modules:
  0.0 948.5 jit_solution(17040697998726867694)
XLA Ops:
  26.2 9.1 reduce-window.6
  38.7 15.1 %all-gather.2.cloned.1.call-done = bf16[2048,1024]{1,0:T(8,128)(2,1)} async-done(((bf16[256,1024]{1,0:T(8,128)(2,1)}), bf16[2048,1024]{1,0:T(8,128)(2,1)}) %all-gather.2.cloned.1.call-update) | async-done | bytes 4194320 | tf_op jit(solution)/shard_map/all_gather | solution.py:23
  66.1 40.7 %while.30 = (s32[]{:T(128)}, bf16[8,256,2,64]{1,3,2,0:T(8,128)(2,1)S(1)}, f32[8,2,256]{2,1,0:T(2,128)}, bf16[8,2048,64]{1,2,0:T(8,128)(2,1)}, bf16[8,2048,64]{1,...) while((s32[]{:T(128)}, ...), condition=%wide.region_6.7_spmd.clone.clone, body=%wide.region_3.6_spmd.clone.sunk.clone | while | flops 276823552 | bytes 14374485 | solution.py:175
  110.6 13.1 %scatter_custom_fusion = bf16[2561,1024]{1,0:T(8,128)(2,1)} fusion(s32[2048]{0:T(1024)S(1)} %bitcast.409, bf16[]{:T(256)} %constant.103.clone.1, bf16[256,1024]{1,0:T(8,128)(2,1)S(1)} %multiply_convert_fusion), kind=kCustom, calls=%fused_computation.107 | custom fusion | bytes 5769218 | tf_op jit(solution)/shard_map/scatter | solution.py:199
  126.3 68.0 %all_to_all.20 = bf16[16,2,80,1024]{3,2,1,0:T(8,128)(2,1)S(1)} all-to-all(bf16[16,2,80,1024]{3,2,1,0:T(8,128)(2,1)S(1)} %bitcast.377), channel_id=1, replica_groups=mesh['dp'=8,'expert'=16] {'expert'}, dimensions={0} | all-to-all | bytes 10485760 | tf_op jit(solution)/shard_map/all_to_all | solution.py:210
  197.4 5.1 fusion.60
  218.3 71.4 %all-to-all-done.1 = bf16[16,2,80,1024]{3,2,1,0:T(8,128)(2,1)} async-done(((bf16[16,2,80,1024]{3,2,1,0:T(8,128)(2,1)}), bf16[16,2,80,1024]{3,2,1,0:T(8,128)(2,1)}, u32[]{:S(2)}, u32[]{:S(2)}) %all-to-all-start.1) | async-done | bytes 5242912 | tf_op jit(solution)/shard_map/all_to_all | solution.py:222
  289.7 5.4 concatenate.26
  295.1 14.1 %gather_fusion = bf16[2048,1024]{1,0:T(8,128)(2,1)} fusion(bf16[2561,1024]{1,0:T(8,128)(2,1)} %concatenate.26, s32[2048]{0:T(1024)S(1)} %broadcast_clamp_fusion), kind=kCustom, calls=%fused_computation.clone | custom fusion | bytes 8396800 | tf_op jit(solution)/shard_map/jit(_take)/gather | solution.py:207
  314.1 13.9 %scatter_custom_fusion.1 = bf16[2561,1024]{1,0:T(8,128)(2,1)} fusion(s32[2048]{0:T(1024)} %bitcast.410, f32[2048]{0:T(1024)S(1)} %mul.508, f32[256,1024]{1,0:T(8,128)S(1)} %bitcast_convert_fusion.3, bf16[]{:T(256)} %constant.103.clone.1), kind=kCustom, calls=%fused_computation.102 | custom fusion | flops 4194304 | bytes 6302208 | tf_op jit(solution)/shard_map/scatter | solution.py:199
  330.5 64.5 %all_to_all.21 = bf16[16,2,80,1024]{3,2,1,0:T(8,128)(2,1)S(1)} all-to-all(bf16[16,2,80,1024]{3,2,1,0:T(8,128)(2,1)S(1)} %bitcast.376), channel_id=1, replica_groups=mesh['dp'=8,'expert'=16] {'expert'}, dimensions={0} | all-to-all | bytes 10485760 | tf_op jit(solution)/shard_map/all_to_all | solution.py:228
  395.0 10.4 %fusion.59 = (bf16[16,2,80,512]{3,2,0,1:T(8,128)(2,1)}, bf16[16,2,80,512]{3,2,0,1:T(8,128)(2,1)S(1)}) fusion(f32[2,16,80,512]{3,2,1,0:T(8,128)} %copy-done.77, f32[2,16,80,512]{3,2,1,0:T(8,128)} %get-tuple-element.249, bf16[2,512,1024]{2,1,0:T(8,128)(2,1)S(1)} %copy-done, bf16[16,2,80,1024]{3,2,1,0:T(8,128)(2,1)S(1)} %all_to_all.21), kind=kOutput, calls=%fused_computation.83 | convolution fusion | flops 2701393920 | bytes 23068672 | tf_op jit(solution)/shard_map/slcd,lfd->slcf/dot_general | solution.py:237
  423.2 6.3 bitcast_convert_fusion
  442.8 47.7 %all-to-all-done.3 = bf16[16,2,80,1024]{3,2,1,0:T(8,128)(2,1)} async-done(((bf16[16,2,80,1024]{3,2,1,0:T(8,128)(2,1)}), bf16[16,2,80,1024]{3,2,1,0:T(8,128)(2,1)}, u32[]{:S(2)}, u32[]{:S(2)}) %all-to-all-start.3) | async-done | bytes 5242912 | tf_op jit(solution)/shard_map/all_to_all | solution.py:258
  490.5 5.4 concatenate.27
  495.9 14.1 %gather_fusion.1 = bf16[2048,1024]{1,0:T(8,128)(2,1)} fusion(bf16[2561,1024]{1,0:T(8,128)(2,1)} %concatenate.27, s32[2048]{0:T(1024)S(1)} %copy-done.48), kind=kCustom, calls=%fused_computation.1.clone | custom fusion | bytes 8396800 | tf_op jit(solution)/shard_map/jit(_take)/gather | solution.py:207
  510.0 8.0 convert_reduce_fusion
  521.5 100.9 %while.31 = (s32[]{:T(128)}, f32[8,256,2,64]{1,3,2,0:T(8,128)}, bf16[8,2048,64]{1,2,0:T(8,128)(2,1)}, bf16[8,2048,64]{1,2,0:T(8,128)(2,1)}, bf16[8,2048,64]{1,2,...) while((s32[]{:T(128)}, f32[8,256,2,64]{1,3,2,0:T(8,128)}, ...), condition=%wide.region_22.24_spmd.clone.clone, body=%wide.region_20.23_spmd.clone.sunk.clone | while | flops 681737728 | bytes 34752624 | solution.py:276
  628.8 17.6 %pad_maximum_fusion = bf16[3145728]{0:T(1024)(128)(2,1)} fusion(bf16[1048576]{0:T(1024)(128)(2,1)S(1)} %bitcast.379, bf16[1048576]{0:T(1024)(128)(2,1)} %bitcast.381, bf16[1048576]{0:T(1024)(128)(2,1)} %bitcast.380), kind=kLoop, calls=%fused_computation.76 | loop fusion | flops 18874368 | bytes 12582912 | tf_op jit(solution)/shard_map/concatenate | solution.py:35
  671.4 80.6 %all-reduce.11.cloned.1.call-done = bf16[3145728]{0:T(1024)(128)(2,1)} async-done(((bf16[3145728]{0:T(1024)(128)(2,1)}), bf16[3145728]{0:T(1024)(128)(2,1)}) %all-reduce.11.cloned.1.call-update) | async-done | bytes 6291472 | tf_op jit(solution)/shard_map/psum | solution.py:36
  752.0 7.8 slice_convert_fusion
  764.7 5.2 reshape.407
  778.6 67.6 %all-reduce.6 = (f32[1024]{0:T(1024)}, f32[1024]{0:T(1024)}, f32[512]{0:T(512)}, f32[1024]{0:T(1024)}) all-reduce(f32[1024]{0:T(1024)S(1)} %get-tuple-element.162, f32[1024]{0:T(1024)S(1)} %get-tuple-element.160, f32[512]{0:T(512)S(1)} %get-tuple-element.164, ...), channel_id=1, replica_groups=mesh['dp'=8,'expert'=16] {'dp','expert'}, use_global_device_ids=true, to_apply=%region_28.30 | all-reduce | flops 3584 | bytes 28672 | tf_op jit(solution)/shard_map/psum | solution.py:318
  847.2 83.0 %all-reduce.13.cloned.1.call-done = (f32[1024,1024]{1,0:T(8,128)}, f32[1024,512]{1,0:T(8,128)}, f32[1024,512]{1,0:T(8,128)}, f32[1024,1024]{1,0:T(8,128)}, f32[1024,32]{0,1:T(8,128)}) async-done(((f32[1024,1024]{1,0:T(8,128)}, f32[1024,512]{1,0:T(8,128)}, f32[1024,512]{1,0:T(8,128)}, f32[1024,1024]{1,0:T(8,128)}, f32[1024,32]{0,1:T(8,128)}), (f32[1024,1024]{1,0:T(8,128)}, f32[1024,512]{1,0:T(8,128)}, ...) | async-done | bytes 12714000 | tf_op jit(solution)/shard_map/psum | solution.py:318
  (393 shorter events, 298.7 us)
Async XLA Ops:
  7.2 195.4 %copy-start = (bf16[2,512,1024]{2,1,0:T(8,128)(2,1)S(1)}, bf16[2,512,1024]{2,1,0:T(8,128)(2,1)}, u32[]{:S(2)}) copy-start(bf16[2,512,1024]{2,1,0:T(8,128)(2,1)} %param.37) | copy-start | bytes 6291460
  7.2 46.6 %all-gather.2.cloned.1.call-start = ((), (), s32[]{:S(2)}) async-start(), calls=%async_computation.5 | async-start | bytes 4718592 | tf_op jit(solution)/shard_map/all_gather | solution.py:23
  14.0 22.2 %copy-start.36 = (f32[256,32]{0,1:T(8,128)}, f32[256,32]{0,1:T(8,128)S(1)}, u32[]{:S(2)}) copy-start(f32[256,32]{0,1:T(8,128)S(1)} %get-tuple-element.240) | copy-start | bytes 98308
  14.0 22.2 %copy-start.38 = (f32[256,32]{0,1:T(8,128)}, f32[256,32]{0,1:T(8,128)S(1)}, u32[]{:S(2)}) copy-start(f32[256,32]{0,1:T(8,128)S(1)} %get-tuple-element.241) | copy-start | bytes 98308
  20.8 14.8 %copy-start.73 = (f32[256]{0:T(256)}, f32[256]{0:T(256)S(1)}, u32[]{:S(2)}) copy-start(f32[256]{0:T(256)S(1)} %get-tuple-element.244) | copy-start | bytes 3076
  20.8 14.8 %copy-start.58 = (f32[256]{0:T(256)}, f32[256]{0:T(256)S(1)}, u32[]{:S(2)}) copy-start(f32[256]{0:T(256)S(1)} %fusion.133) | copy-start | bytes 3076
  38.7 72.0 %copy-start.69 = (s32[2048,1]{0,1:T(1,128)}, s32[2048,1]{0,1:T(1,128)S(1)}, u32[]{:S(2)}) copy-start(s32[2048,1]{0,1:T(1,128)S(1)} %compare_select_fusion) | copy-start | bytes 24580
  106.9 16.9 %copy-start.15 = (bf16[8,256,2,64]{1,3,2,0:T(8,128)(2,1)}, bf16[8,256,2,64]{1,3,2,0:T(8,128)(2,1)S(1)}, u32[]{:S(2)}) copy-start(bf16[8,256,2,64]{1,3,2,0:T(8,128)(2,1)S(1)} %get-tuple-element.107) | copy-start | bytes 1572868
  109.5 14.3 %copy-start.67 = (f32[256]{0:T(256)}, f32[256]{0:T(256)S(1)}, u32[]{:S(2)}) copy-start(f32[256]{0:T(256)S(1)} %get-tuple-element.246) | copy-start | bytes 3076
  109.5 14.3 %copy-start.62 = (f32[256]{0:T(256)}, f32[256]{0:T(256)S(1)}, u32[]{:S(2)}) copy-start(f32[256]{0:T(256)S(1)} %fusion.134) | copy-start | bytes 3076
  126.3 68.0 %copy-start.28 = (bf16[2,1024,512]{2,1,0:T(8,128)(2,1)S(1)}, bf16[2,1024,512]{2,1,0:T(8,128)(2,1)}, u32[]{:S(2)}) copy-start(bf16[2,1024,512]{2,1,0:T(8,128)(2,1)} %param.35) | copy-start | bytes 6291460
  208.7 81.0 %all-to-all-start.1 = ((bf16[16,2,80,1024]{3,2,1,0:T(8,128)(2,1)}), bf16[16,2,80,1024]{3,2,1,0:T(8,128)(2,1)}, u32[]{:S(2)}, u32[]{:S(2)}) async-start(bf16[16,2,80,1024]{3,2,1,0:T(8,128)(2,1)} %copy.83), calls=%async_computation.1 | async-start | bytes 10485760 | tf_op jit(solution)/shard_map/all_to_all | solution.py:222
  213.8 81.3 %copy-start.45 = (s32[256,8]{1,0:T(8,128)}, s32[256,8]{1,0:T(8,128)S(1)}, u32[]{:S(2)}) copy-start(s32[256,8]{1,0:T(8,128)S(1)} %copy.75) | copy-start | bytes 24580
  213.8 95.4 %copy-start.56 = (pred[2048]{0:T(1024)(128)(4,1)}, pred[2048]{0:T(1024)(128)(4,1)S(1)}, u32[]{:S(2)}) copy-start(pred[2048]{0:T(1024)(128)(4,1)S(1)} %compare_and_fusion) | copy-start | bytes 6148
  213.8 81.2 %copy-start.47 = (s32[2048]{0:T(1024)}, s32[2048]{0:T(1024)S(1)}, u32[]{:S(2)}) copy-start(s32[2048]{0:T(1024)S(1)} %broadcast_clamp_fusion) | copy-start | bytes 24580
  217.6 77.5 %copy-start.64 = (f32[256]{0:T(256)}, f32[256]{0:T(256)S(1)}, u32[]{:S(2)}) copy-start(f32[256]{0:T(256)S(1)} %reduce_max.18) | copy-start | bytes 3076
  312.4 15.6 %copy-start.30 = (f32[256,8]{1,0:T(8,128)}, f32[256,8]{1,0:T(8,128)S(1)}, u32[]{:S(2)}) copy-start(f32[256,8]{1,0:T(8,128)S(1)} %reduce_sum.225) | copy-start | bytes 24580
  314.0 14.0 %copy-start.21 = (f32[256,8]{1,0:T(8,128)}, f32[256,8]{1,0:T(8,128)S(1)}, u32[]{:S(2)}) copy-start(f32[256,8]{1,0:T(8,128)S(1)} %get-tuple-element.218) | copy-start | bytes 24580
  416.2 74.2 %all-to-all-start.3 = ((bf16[16,2,80,1024]{3,2,1,0:T(8,128)(2,1)}), bf16[16,2,80,1024]{3,2,1,0:T(8,128)(2,1)}, u32[]{:S(2)}, u32[]{:S(2)}) async-start(bf16[16,2,80,1024]{3,2,1,0:T(8,128)(2,1)} %copy.85), calls=%async_computation.3 | async-start | bytes 10485760 | tf_op jit(solution)/shard_map/all_to_all | solution.py:258
  420.9 243.1 %reduce-scatter.2.cloned.1.call-start = ((), (), s32[]{:S(2)}) async-start(), calls=%async_computation.6 | async-start | bytes 4718592 | tf_op jit(solution)/shard_map/reduce_scatter | solution.py:30
  495.8 14.1 %copy-start.57 = (pred[2048]{0:T(1024)(128)(4,1)S(1)}, pred[2048]{0:T(1024)(128)(4,1)}, u32[]{:S(2)}) copy-start(pred[2048]{0:T(1024)(128)(4,1)} %copy-done.56) | copy-start | bytes 6148
  627.2 124.7 %all-reduce.11.cloned.1.call-start = ((), (), s32[]{:S(2)}) async-start(), calls=%async_computation.7 | async-start | bytes 12582912 | tf_op jit(solution)/shard_map/psum | solution.py:36
  646.4 283.8 %all-reduce.13.cloned.1.call-start = ((), (), s32[]{:S(2)}) async-start(), calls=%async_computation.8 | async-start | bytes 25427968 | tf_op jit(solution)/shard_map/psum | solution.py:318
  777.4 68.8 %copy-start.66 = (f32[256]{0:T(256)S(1)}, f32[256]{0:T(256)}, u32[]{:S(2)}) copy-start(f32[256]{0:T(256)} %copy-done.65) | copy-start | bytes 3076
  (65 other events, 345.2 us)
Sparse Core Ops, SparseCore 0:
  18.0 35.7 all-gather.1
  627.4 36.6 reduce-scatter.1
  666.4 85.5 all-reduce.10
  759.0 171.2 all-reduce.12
where the time goes:
time: 960 us; the launch traced here: 949 us
  waiting for transfers between devices  302 us (31%)
  blocking collectives  200 us (21%)
  matrix products  183 us (19%)
  local copies, waits for them, and re-layouts  129 us (13%)
  other arithmetic  108 us (11%)
  between operations  16.1 us (2%)
  starting transfers between devices  10.1 us (1%)
    psum x1, waiting for transfers between devices, body(): lax.psum((attn_gain_grad, query_w_grad, key_w_grad, value_w_grad, query_g...  83 us
    psum x1, waiting for transfers between devices, together(): so_far = lax.psum(vector, axis)  80.6 us
    all_to_all x1, waiting for transfers between devices, body(): lax.all_to_all(result_part, 'expert', split_axis=0, concat_axis=0, tiled=...  71.4 us
    all_to_all x1, blocking collectives, body(): lax.all_to_all(place_pairs(pair_rows), 'expert', split_axis=0, concat_axi...  68 us
    psum x1, blocking collectives, body(): lax.psum((attn_gain_grad, query_w_grad, key_w_grad, value_w_grad, query_g...  67.6 us
    all_to_all x1, blocking collectives, body(): lax.all_to_all(place_pairs(pair_grads), 'expert', split_axis=0, concat_ax...  64.5 us
    all_to_all x1, waiting for transfers between devices, body(): lax.all_to_all(arrived_grad, 'expert', split_axis=0, concat_axis=0, tiled...  47.7 us
    dot_general x16, matrix products, masked_scores(): jnp.einsum('trd,sd->rts', query_pair, key_head, preferred_element_type=jn...  33.1 us
  transfers between devices with their start and end apart: 6, of which 6 were waited for; matrix products, arithmetic and copies ran while one was open for 12% of the time, Pallas kernels for 0%

commit v1 on v0

--- a/solution.py
+++ b/solution.py
@@ -3,6 +3,8 @@
 import jax
 import jax.numpy as jnp
 from jax import lax
+from jax.experimental import pallas as pl
+from jax.experimental.pallas import tpu as pltpu
 from jax.sharding import PartitionSpec as P
 
 HEADS = 16
@@ -119,6 +121,445 @@
         "rts,trd->sd", probs.astype(jnp.bfloat16), grad_pair, preferred_element_type=jnp.float32
     )
     return (query_grad, key_grad, value_grad)
+
+
+RING = 4
+ROWS = 256
+EXTRA = 16
+FULL = ROWS + EXTRA
+GROUP = 4 * CAP
+MESH = pl.DeviceIdType.MESH
+
+
+def dot_nn(a, b):
+    return jnp.dot(a, b, preferred_element_type=jnp.float32)
+
+
+def dot_nt(a, b):
+    return lax.dot_general(a, b, (((1,), (1,)), ((), ())), preferred_element_type=jnp.float32)
+
+
+def dot_tn(a, b):
+    return lax.dot_general(a, b, (((0,), (0,)), ((), ())), preferred_element_type=jnp.float32)
+
+
+class Torus:
+    def __init__(self):
+        self.dp = lax.axis_index("dp")
+        expert = lax.axis_index("expert")
+        self.expert = expert
+        self.z, self.y = expert // RING, expert % RING
+
+    def block(self, dz, dy):
+        return ((self.z + dz + RING) % RING) * RING + (self.y + dy + RING) % RING
+
+    def near(self, axis, step):
+        return (self.dp, self.block(step, 0) if axis == "z" else self.block(0, step))
+
+    def along(self, axis, other, step):
+        return self.block(step, other) if axis == "z" else self.block(other, step)
+
+    def neighbours(self):
+        return [self.near(axis, step) for axis in "yz" for step in (1, -1)]
+
+
+class Gather:
+    def __init__(self, torus, buffer, send, recv, number, axis, other, low, size):
+        self.torus, self.buffer, self.send, self.recv = torus, buffer, send, recv
+        self.number, self.axis, self.other, self.low, self.size = number, axis, other, low, size
+
+    def copy(self, which, offset, start, size, step):
+        at = self.torus.along(self.axis, self.other, offset) * ROWS + start
+        rows = self.buffer.at[pl.ds(pl.multiple_of(at, 16), size)]
+        return pltpu.make_async_remote_copy(
+            src_ref=rows,
+            dst_ref=rows,
+            send_sem=self.send.at[self.number, which],
+            recv_sem=self.recv.at[self.number, which],
+            device_id=self.torus.near(self.axis, step),
+            device_id_type=MESH,
+        )
+
+    def first(self):
+        self.copy(0, 0, self.low, self.size, 1).start()
+        self.copy(1, 0, self.low, self.size, -1).start()
+
+    def second(self):
+        half = self.size // 2
+        self.copy(0, -1, self.low, self.size, 1).wait_recv()
+        self.copy(2, -1, self.low, half, 1).start()
+        self.copy(1, 1, self.low, self.size, -1).wait_recv()
+        self.copy(3, 1, self.low + half, half, -1).start()
+
+    def third(self):
+        half = self.size // 2
+        self.copy(2, 2, self.low, half, 1).wait_recv()
+        self.copy(3, 2, self.low + half, half, -1).wait_recv()
+
+    def drain(self):
+        half = self.size // 2
+        self.copy(0, 0, self.low, self.size, 1).wait_send()
+        self.copy(1, 0, self.low, self.size, -1).wait_send()
+        self.copy(2, -1, self.low, half, 1).wait_send()
+        self.copy(3, 1, self.low + half, half, -1).wait_send()
+
+
+class Scatter:
+    def __init__(self, torus, sums, landing, send, recv, number, base, axis, other, low, first, second):
+        self.torus, self.sums, self.landing, self.send, self.recv = torus, sums, landing, send, recv
+        self.number, self.axis, self.other = number, axis, other
+        self.low, self.parts = low, (first, second)
+        self.size = first + second
+        self.slots = (base, base + first, base + self.size, base + 2 * self.size)
+
+    def rows(self, which):
+        if which == 0:
+            return self.low, self.parts[0]
+        if which == 1:
+            return self.low + self.parts[0], self.parts[1]
+        return self.low, self.size
+
+    def at(self, offset):
+        return self.torus.along(self.axis, self.other, offset)
+
+    def copy(self, which):
+        start, size = self.rows(which)
+        offset = (2, 2, 1, -1)[which]
+        return pltpu.make_async_remote_copy(
+            src_ref=self.sums.at[self.at(offset), pl.ds(start, size)],
+            dst_ref=self.landing.at[pl.ds(self.slots[which], size)],
+            send_sem=self.send.at[self.number, which],
+            recv_sem=self.recv.at[self.number, which],
+            device_id=self.torus.near(self.axis, (1, -1, 1, -1)[which]),
+            device_id_type=MESH,
+        )
+
+    def add(self, which, offset):
+        start, size = self.rows(which)
+        block = self.at(offset)
+
+        @pl.loop(0, size // 16)
+        def _(k):
+            here = pl.ds(pl.multiple_of(start + k * 16, 16), 16)
+            there = pl.ds(pl.multiple_of(self.slots[which] + k * 16, 16), 16)
+            total = self.sums[block, here].astype(jnp.float32) + self.landing[there].astype(jnp.float32)
+            self.sums[block, here] = total.astype(jnp.bfloat16)
+
+    def first(self):
+        self.copy(0).start()
+        self.copy(1).start()
+
+    def second(self):
+        self.copy(0).wait_recv()
+        self.add(0, 1)
+        self.copy(2).start()
+        self.copy(1).wait_recv()
+        self.add(1, -1)
+        self.copy(3).start()
+
+    def third(self, result=None):
+        self.copy(2).wait_recv()
+        self.copy(3).wait_recv()
+        block = self.at(0)
+
+        @pl.loop(0, self.size // 16)
+        def _(k):
+            here = pl.ds(pl.multiple_of(self.low + k * 16, 16), 16)
+            left = pl.ds(pl.multiple_of(self.slots[2] + k * 16, 16), 16)
+            right = pl.ds(pl.multiple_of(self.slots[3] + k * 16, 16), 16)
+            total = (
+                self.sums[block, here].astype(jnp.float32)
+                + self.landing[left].astype(jnp.float32)
+                + self.landing[right].astype(jnp.float32)
+            )
+            if result is None:
+                self.sums[block, here] = total.astype(jnp.bfloat16)
+            else:
+                result[here] = total
+
+    def drain(self):
+        for which in range(4):
+            self.copy(which).wait_send()
+
+
+def moe_kernel(
+    ffn, cot, sel, mem, wr, w_gate, w_up, w_down,
+    ret, mixed, grad_gu, grad_d,
+    rows, sums, wgu, wd, held, pair, inner, dgu, mixing, back, cotv, gate_rows, grad_rows, stage,
+    ag_send, ag_recv, rs_send, rs_recv, w_sem, cot_sem, stage_sem, credit,
+):
+    torus = Torus()
+    barrier = pltpu.get_barrier_semaphore()
+    for device in torus.neighbours():
+        pl.semaphore_signal(barrier, inc=1, device_id=device, device_id_type=MESH)
+
+    weights = [
+        pltpu.make_async_copy(w_gate, wgu.at[:, :, pl.ds(0, 512)], w_sem.at[0]),
+        pltpu.make_async_copy(w_up, wgu.at[:, :, pl.ds(512, 512)], w_sem.at[1]),
+        pltpu.make_async_copy(w_down, wd, w_sem.at[2]),
+    ]
+    for copy in weights:
+        copy.start()
+
+    def group_z(g):
+        return (torus.z + g + (g // 2) * (1 - 2 * (g % 2))) % RING
+
+    def cot_copy(g):
+        return pltpu.make_async_copy(cot.at[pl.ds(group_z(g) * RING, RING)], cotv, cot_sem)
+
+    cot_copy(0).start()
+    rows[pl.ds(pl.multiple_of(torus.expert * ROWS, ROWS), ROWS)] = ffn[...]
+    pl.semaphore_wait(barrier, 4)
+
+    def gather(number, axis, other, low):
+        return Gather(torus, rows, ag_send, ag_recv, number, axis, other, low, ROWS // 2)
+
+    a_first = gather(0, "y", 0, 0)
+    b_first = gather(1, "z", 0, ROWS // 2)
+    a_second = {d: gather(2 + d % RING, "z", d, 0) for d in (0, 1, -1, 2)}
+    b_second = {d: gather(6 + d % RING, "y", d, ROWS // 2) for d in (0, 1, -1, 2)}
+    gathers = [a_first, b_first, *a_second.values(), *b_second.values()]
+
+    a_first.first()
+    b_first.first()
+    b_second[0].first()
+    a_second[0].first()
+    a_first.second()
+    b_first.second()
+    for d in (1, -1):
+        b_second[d].first()
+        a_second[d].first()
+    a_first.third()
+    b_first.third()
+    b_second[2].first()
+    a_second[2].first()
+    for copy in weights:
+        copy.wait()
+
+    def choice(source, e):
+        return lax.broadcasted_iota(jnp.int32, (CAP, ROWS), 0) == sel[source, pl.ds(e, 1), :]
+
+    def choices(source):
+        picked = [choice(source, e) for e in range(2)]
+        both = jnp.concatenate([p.astype(jnp.float32) for p in picked], axis=0)
+        return picked, both.astype(jnp.bfloat16)
+
+    def stage_copy(slot, target):
+        return pltpu.make_async_copy(stage.at[slot], target, stage_sem.at[slot])
+
+    expert_rows = lax.broadcasted_iota(jnp.int32, (EXPERTS, ROWS), 0)
+
+    @pl.loop(0, 4)
+    def _(g):
+        @pl.when(g == 0)
+        def _():
+            b_second[0].second()
+            a_second[0].second()
+            b_second[0].third()
+
+        @pl.when(g == 1)
+        def _():
+            for d in (1, -1):
+                b_second[d].second()
+                a_second[d].second()
+            a_second[2].second()
+            b_second[1].third()
+
+        @pl.when(g == 2)
+        def _():
+            b_second[2].second()
+            b_second[-1].third()
+
+        @pl.when(g == 3)
+        def _():
+            for d in (0, 1, -1, 2):
+                a_second[d].third()
+            b_second[2].third()
+
+        cot_copy(g).wait()
+        first_source = group_z(g) * RING
+
+        @pl.loop(0, 4)
+        def _(j):
+            source = first_source + j
+            block = rows[pl.ds(pl.multiple_of(source * ROWS, ROWS), ROWS)]
+            named = mem[source].astype(jnp.float32) > 0.5
+            logits = jnp.where(named, dot_nt(wr[...], block), -1e30)
+            weight = jnp.where(named, jnp.exp(logits - jnp.max(logits, axis=0, keepdims=True)), 0.0)
+            gates = weight / jnp.sum(weight, axis=0, keepdims=True)
+            picked, both = choices(source)
+            took = dot_nn(both, block).astype(jnp.bfloat16)
+            took_grad = dot_nn(both, cotv[j]).astype(jnp.bfloat16)
+            here = pl.ds(pl.multiple_of(j * CAP, 16), CAP)
+            there = pl.ds(pl.multiple_of(g * GROUP + j * CAP, 16), CAP)
+            for e in range(2):
+                own = jnp.sum(
+                    jnp.where(expert_rows == torus.expert * 2 + e, gates, 0.0), axis=0, keepdims=True
+                )
+                of_rows = jnp.sum(jnp.where(picked[e], own, 0.0), axis=1, keepdims=True)
+                gate_rows[e, here] = jnp.broadcast_to(of_rows, (CAP, 128))
+                held[e, there] = took[e * CAP : (e + 1) * CAP]
+                mixing[e, here] = took_grad[e * CAP : (e + 1) * CAP]
+
+        @pl.when(g < 3)
+        def _():
+            cot_copy(g + 1).start()
+
+        @pl.when(g == 3)
+        def _():
+            for one in gathers:
+                one.drain()
+            for device in torus.neighbours():
+                pl.semaphore_signal(credit, inc=1, device_id=device, device_id_type=MESH)
+
+        @pl.loop(0, 2)
+        def _(e):
+            there = pl.ds(pl.multiple_of(g * GROUP, 16), GROUP)
+            both = dot_nn(held[e, there], wgu[e])
+            gate, up = both[:, :512], both[:, 512:]
+            sig = jax.nn.sigmoid(gate)
+            silu = gate * sig
+            act = (silu * up).astype(jnp.bfloat16)
+            inner[e, there] = act
+            out = dot_nn(act, wd[e]).astype(jnp.bfloat16).astype(jnp.float32)
+            grad = mixing[e].astype(jnp.float32)
+            weight = gate_rows[e][:, :1]
+            grad_rows[e] = jnp.broadcast_to(jnp.sum(grad * out, axis=1, keepdims=True), (GROUP, 128))
+            pair[e, there] = (weight * grad).astype(jnp.bfloat16)
+            mixing[e] = (weight * out).astype(jnp.bfloat16)
+            inner_grad = dot_nt(pair[e, there], wd[e])
+            dgu[e, there, :512] = (inner_grad * up * sig * (1.0 + gate * (1.0 - sig))).astype(jnp.bfloat16)
+            dgu[e, there, 512:] = (inner_grad * silu).astype(jnp.bfloat16)
+            back[e] = dot_nt(dgu[e, there], wgu[e]).astype(jnp.bfloat16)
+
+        @pl.loop(0, 4)
+        def _(j):
+            source = first_source + j
+            picked, both = choices(source)
+            here = pl.ds(pl.multiple_of(j * CAP, 16), CAP)
+            part = dot_tn(both, jnp.concatenate([back[0, here], back[1, here]], axis=0))
+            sums[source, pl.ds(EXTRA, ROWS)] = part.astype(jnp.bfloat16)
+            grads = jnp.zeros((EXPERTS, ROWS), jnp.float32)
+            for e in range(2):
+                own = jnp.sum(
+                    jnp.where(picked[e], grad_rows[e, here][:, :1], 0.0), axis=0, keepdims=True
+                )
+                grads = grads + jnp.where(expert_rows == torus.expert * 2 + e, own, 0.0)
+            laid = jnp.concatenate([grads[8 * q : 8 * q + 8] for q in range(4)], axis=1)
+            sums[source, pl.ds(0, EXTRA)] = jnp.concatenate([laid, jnp.zeros_like(laid)], axis=0).astype(
+                jnp.bfloat16
+            )
+            slot = j % 2
+
+            @pl.when((g > 0) | (j > 1))
+            def _():
+                stage_copy(slot, mixed.at[source]).wait()
+
+            result = dot_tn(both, jnp.concatenate([mixing[0, here], mixing[1, here]], axis=0))
+            stage[slot] = result.astype(jnp.bfloat16)
+            stage_copy(slot, mixed.at[source]).start()
+
+    pl.semaphore_wait(credit, 4)
+
+    order = (2, 1, -1, 0)
+    a_lead = {}
+    b_lead = {}
+    for n, d in enumerate(order):
+        a_lead[d] = Scatter(
+            torus, sums, rows, rs_send, rs_recv, n, n * 384, "z", d, 0, 64, 64
+        )
+        b_lead[d] = Scatter(
+            torus, sums, rows, rs_send, rs_recv, 4 + n, 1920 + n * 432, "y", d, 128, 80, 64
+        )
+    a_last = Scatter(torus, sums, rows, rs_send, rs_recv, 8, 4 * 384, "y", 0, 0, 64, 64)
+    b_last = Scatter(torus, sums, rows, rs_send, rs_recv, 9, 1920 + 4 * 432, "z", 0, 128, 80, 64)
+
+    def write_grads(low, high):
+        @pl.loop(low, high)
+        def _(k):
+            slot = k % 2
+            e, c = k // 6, k % 6
+            stage_copy(slot, grad_d.at[0, pl.ds(0, 256)]).wait()
+
+            @pl.when(c < 4)
+            def _():
+                columns = pl.ds(pl.multiple_of(c * 256, 256), 256)
+                stage[slot] = dot_tn(held[e, :, columns], dgu[e]).astype(jnp.bfloat16)
+                stage_copy(slot, grad_gu.at[e, columns]).start()
+
+            @pl.when(c >= 4)
+            def _():
+                columns = pl.ds(pl.multiple_of((c - 4) * 256, 256), 256)
+                stage[slot] = dot_tn(inner[e, :, columns], pair[e]).astype(jnp.bfloat16)
+                stage_copy(slot, grad_d.at[e, columns]).start()
+
+    for d in order:
+        b_lead[d].first()
+        a_lead[d].first()
+    write_grads(0, 4)
+    for d in order:
+        b_lead[d].second()
+        a_lead[d].second()
+    write_grads(4, 12)
+    for slot in range(2):
+        stage_copy(slot, grad_d.at[0, pl.ds(0, 256)]).wait()
+    for d in order:
+        b_lead[d].third()
+        a_lead[d].third()
+        if d == 2:
+            b_last.first()
+            a_last.first()
+    b_last.second()
+    a_last.second()
+    b_last.third(ret)
+    a_last.third(ret)
+    for one in [*a_lead.values(), *b_lead.values(), a_last, b_last]:
+        one.drain()
+
+
+def moe(ffn_in, cot_all, sel, mem, router_rows, w_gate, w_up, w_down):
+    vmem, hbm = pl.BlockSpec(memory_space=pltpu.VMEM), pl.BlockSpec(memory_space=pl.ANY)
+    low, total = jnp.bfloat16, 4 * GROUP
+    return pl.pallas_call(
+        moe_kernel,
+        name="moe",
+        out_shape=(
+            jax.ShapeDtypeStruct((FULL, 1024), jnp.float32),
+            jax.ShapeDtypeStruct((16, ROWS, 1024), low),
+            jax.ShapeDtypeStruct((2, 1024, 1024), low),
+            jax.ShapeDtypeStruct((2, 512, 1024), low),
+        ),
+        in_specs=[vmem, hbm, vmem, vmem, vmem, hbm, hbm, hbm],
+        out_specs=(vmem, hbm, hbm, hbm),
+        scratch_shapes=[
+            pltpu.VMEM((16 * ROWS, 1024), low),
+            pltpu.VMEM((16, FULL, 1024), low),
+            pltpu.VMEM((2, 1024, 1024), low),
+            pltpu.VMEM((2, 512, 1024), low),
+            pltpu.VMEM((2, total, 1024), low),
+            pltpu.VMEM((2, total, 1024), low),
+            pltpu.VMEM((2, total, 512), low),
+            pltpu.VMEM((2, total, 1024), low),
+            pltpu.VMEM((2, GROUP, 1024), low),
+            pltpu.VMEM((2, GROUP, 1024), low),
+            pltpu.VMEM((4, ROWS, 1024), low),
+            pltpu.VMEM((2, GROUP, 128), jnp.float32),
+            pltpu.VMEM((2, GROUP, 128), jnp.float32),
+            pltpu.VMEM((2, ROWS, 1024), low),
+            pltpu.SemaphoreType.DMA((10, 4)),
+            pltpu.SemaphoreType.DMA((10, 4)),
+            pltpu.SemaphoreType.DMA((10, 4)),
+            pltpu.SemaphoreType.DMA((10, 4)),
+            pltpu.SemaphoreType.DMA((3,)),
+            pltpu.SemaphoreType.DMA,
+            pltpu.SemaphoreType.DMA((2,)),
+            pltpu.SemaphoreType.REGULAR,
+        ],
+        compiler_params=pltpu.CompilerParams(
+            collective_id=1, has_side_effects=True, vmem_limit_bytes=63 * 2**20
+        ),
+        cost_estimate=pl.CostEstimate(flops=50 * 10**9, bytes_accessed=40 * 10**6, transcendentals=2 * 10**6),
+    )(ffn_in, cot_all, sel, mem, router_rows, w_gate, w_up, w_down)
 
 
 def body(
@@ -139,6 +580,17 @@
     w_up,
     w_down,
 ):
+    local_experts = w_gate.shape[0]
+    cot_all = lax.all_gather(cotangent[0], "expert", axis=0)
+    routes_all = lax.all_gather(routes[0], "expert", axis=0)
+    member = (
+        (routes_all[:, :, :, None] == jnp.arange(EXPERTS, dtype=jnp.int32)).any(axis=2).astype(jnp.bfloat16)
+    )
+    mem = member.transpose(0, 2, 1)
+    before = jnp.triu(jnp.ones((ROWS, ROWS), jnp.bfloat16), 1)
+    own_mem = lax.dynamic_slice_in_dim(mem, lax.axis_index("expert") * local_experts, local_experts, 1)
+    slots = jnp.einsum("seu,ut->set", own_mem, before, preferred_element_type=jnp.float32).astype(jnp.int32)
+    sel = jnp.where((own_mem > 0) & (slots < CAP), slots, -1)
     token_rows = tokens[0].astype(jnp.float32)
     tok_count = token_rows.shape[0]
     width = token_rows.shape[1]
@@ -180,91 +632,24 @@
     ffn_value, ffn_pull = jax.vjp(norm_rows, hidden_res, ffn_gain.astype(jnp.float32))
     ffn_in = ffn_value.astype(jnp.bfloat16)
     logits = jnp.dot(ffn_in, w_router, preferred_element_type=jnp.float32)
-    route_rows = routes[0]
-    choose = (route_rows[:, :, None] == jnp.arange(EXPERTS, dtype=jnp.int32)[None, None, :]).astype(
-        jnp.float32
-    )
-    gates = jax.nn.softmax(jnp.einsum("tke,te->tk", choose, logits, precision=HIGHEST), axis=-1)
-    pair_routes = route_rows.reshape(-1)
-    member = (pair_routes[:, None] == jnp.arange(EXPERTS, dtype=jnp.int32)[None, :]).astype(
-        jnp.int32
-    )
-    earlier = jnp.cumsum(member, axis=0) - member
-    slots = jnp.sum(earlier * member, axis=-1)
-    target = jnp.where(slots < CAP, pair_routes * CAP + slots, EXPERTS * CAP)
-    groups = lax.axis_size("expert")
-    local_count = w_gate.shape[0]
-
-    def place_pairs(pair_values):
-        filled = jnp.zeros((EXPERTS * CAP + 1, width), jnp.bfloat16).at[target].set(pair_values)
-        return filled[: EXPERTS * CAP].reshape(groups, local_count, CAP, width)
-
-    def collect_pairs(arrived_back):
-        padded = jnp.concatenate(
-            [arrived_back.reshape(EXPERTS * CAP, width), jnp.zeros((1, width), jnp.bfloat16)],
-            axis=0,
-        )
-        return jnp.take(padded, target, axis=0).reshape(tok_count, TOPK, width)
-
-    pair_rows = jnp.broadcast_to(ffn_in[:, None, :], (tok_count, TOPK, width)).reshape(-1, width)
-    arrived_rows = lax.all_to_all(
-        place_pairs(pair_rows), "expert", split_axis=0, concat_axis=0, tiled=True
-    )
-    gate_part = jnp.einsum(
-        "slcd,ldf->slcf", arrived_rows, w_gate, preferred_element_type=jnp.float32
-    )
-    up_part = jnp.einsum("slcd,ldf->slcf", arrived_rows, w_up, preferred_element_type=jnp.float32)
-    inner_part = (jax.nn.silu(gate_part) * up_part).astype(jnp.bfloat16)
-    result_part = jnp.einsum(
-        "slcf,lfd->slcd", inner_part, w_down, preferred_element_type=jnp.float32
+    own_routes = (routes[0][:, :, None] == jnp.arange(EXPERTS, dtype=jnp.int32)).any(axis=1)
+    gates = jax.nn.softmax(jnp.where(own_routes, logits, -1e30), axis=-1)
+    gates = jnp.where(own_routes, gates, 0.0)
+    returned, mixed_parts, gate_up_w_grad, down_grad = moe(
+        ffn_in, cot_all, sel, mem, w_router.T, w_gate, w_up, w_down
+    )
+    mixed_sum = lax.psum_scatter(
+        mixed_parts.reshape(16 * ROWS, width), "expert", scatter_dimension=0, tiled=True
+    )
+    mixed_out = (hidden_res + mixed_sum.astype(jnp.float32)).astype(jnp.bfloat16)
+    grad_out = cotangent[0].astype(jnp.float32)
+    gate_grad = returned[:8].reshape(8, 4, ROWS).transpose(1, 0, 2).reshape(EXPERTS, ROWS).T
+    pair_sum = returned[EXTRA:]
+    logit_grad = (
+        gates * (gate_grad - jnp.sum(gates * gate_grad, axis=-1, keepdims=True))
     ).astype(jnp.bfloat16)
-    returned = collect_pairs(
-        lax.all_to_all(result_part, "expert", split_axis=0, concat_axis=0, tiled=True)
-    )
-    mixed_out = (hidden_res + jnp.sum(gates[:, :, None] * returned, axis=1)).astype(jnp.bfloat16)
-    grad_out = cotangent[0].astype(jnp.float32)
-    gate_grad = jnp.sum(grad_out[:, None, :] * returned, axis=-1)
-    pair_grads = (gates[:, :, None] * grad_out[:, None, :]).astype(jnp.bfloat16).reshape(-1, width)
-    grad_arrived = lax.all_to_all(
-        place_pairs(pair_grads), "expert", split_axis=0, concat_axis=0, tiled=True
-    )
-    sigmoid_gate = jax.nn.sigmoid(gate_part)
-    silu_gate = gate_part * sigmoid_gate
-    inner = (silu_gate * up_part).astype(jnp.bfloat16)
-    down_grad = jnp.einsum(
-        "slcf,slcd->lfd", inner, grad_arrived, preferred_element_type=jnp.float32
-    )
-    inner_grad = jnp.einsum(
-        "slcd,lfd->slcf", grad_arrived, w_down, preferred_element_type=jnp.float32
-    )
-    gate_pre_grad = (
-        inner_grad * up_part * sigmoid_gate * (1.0 + gate_part * (1.0 - sigmoid_gate))
-    ).astype(jnp.bfloat16)
-    up_pre_grad = (inner_grad * silu_gate).astype(jnp.bfloat16)
-    gate_w_grad = jnp.einsum(
-        "slcd,slcf->ldf", arrived_rows, gate_pre_grad, preferred_element_type=jnp.float32
-    )
-    up_w_grad = jnp.einsum(
-        "slcd,slcf->ldf", arrived_rows, up_pre_grad, preferred_element_type=jnp.float32
-    )
-    arrived_grad = jnp.einsum(
-        "slcf,ldf->slcd", gate_pre_grad, w_gate, preferred_element_type=jnp.float32
-    )
-    arrived_grad = (
-        arrived_grad
-        + jnp.einsum("slcf,ldf->slcd", up_pre_grad, w_up, preferred_element_type=jnp.float32)
-    ).astype(jnp.bfloat16)
-    pair_in_grad = collect_pairs(
-        lax.all_to_all(arrived_grad, "expert", split_axis=0, concat_axis=0, tiled=True)
-    )
-    gate_logit_grad = gates * (gate_grad - jnp.sum(gates * gate_grad, axis=-1, keepdims=True))
-    logit_grad = jnp.einsum("tk,tke->te", gate_logit_grad, choose, precision=HIGHEST).astype(
-        jnp.bfloat16
-    )
     router_grad = contract_rows(ffn_in, logit_grad)
-    ffn_in_grad = times_transposed(logit_grad, w_router) + jnp.sum(
-        pair_in_grad, axis=1, dtype=jnp.float32
-    )
+    ffn_in_grad = times_transposed(logit_grad, w_router) + pair_sum
     res_part, ffn_gain_grad = ffn_pull(ffn_in_grad)
     hidden_grad = grad_out + res_part
     branch_grad = hidden_grad.astype(jnp.bfloat16)
@@ -329,19 +714,10 @@
         ),
         ("dp", "expert"),
     )
-    gate_w_sum, up_w_sum, down_w_sum = tuple(
-        (
-            part.astype(jnp.float32)
-            for part in together(
-                (
-                    gate_w_grad.astype(jnp.bfloat16),
-                    up_w_grad.astype(jnp.bfloat16),
-                    down_grad.astype(jnp.bfloat16),
-                ),
-                "dp",
-            )
-        )
-    )
+    gate_up_sum, down_w_sum = lax.psum((gate_up_w_grad, down_grad), "dp")
+    gate_w_sum = gate_up_sum[:, :, :512].astype(jnp.float32)
+    up_w_sum = gate_up_sum[:, :, 512:].astype(jnp.float32)
+    down_w_sum = down_w_sum.astype(jnp.float32)
     return (
         mixed_out[None],
         token_grad[None],

time: 960 us -> 767 us (0.80)
  Pallas kernels: 0 us -> 132 us
  blocking collectives: 200 us -> 88.6 us
  local copies, waits for them, and re-layouts: 129 us -> 35.4 us
  matrix products: 183 us -> 123 us
  other arithmetic: 108 us -> 48.3 us
  waiting for transfers between devices: 302 us -> 321 us
    all_to_all x2 -> x0, blocking collectives: 132 us -> none  [the longest x1 68 us: body(): lax.all_to_all(place_pairs(pair_rows), 'expert', split_axis=0, concat_axi...]
    pallas_call x0 -> x1, Pallas kernels: none -> 132 us  [moe(): pl.pallas_call(moe_kernel, name='moe', out_shape=(jax.ShapeDtypeStruct((F...]
    all_to_all x2 -> x0, waiting for transfers between devices: 119 us -> none  [the longest x1 71.4 us: body(): lax.all_to_all(result_part, 'expert', split_axis=0, concat_axis=0, tiled=...]
    reduce_scatter x0 -> x1, waiting for transfers between devices: none -> 84.6 us  [body(): lax.psum_scatter(mixed_parts.reshape(16 * ROWS, width), 'expert', scatter...]
    dot_general x11 -> x1, matrix products: 44.2 us -> 0.14 us  [body(): jnp.einsum('seu,ut->set', own_mem, before, preferred_element_type=jnp.flo...]
    gather x2 -> x0, local copies, waits for them, and re-layouts: 28.2 us -> none  [collect_pairs(): return jnp.take(padded, target, axis=0).reshape(tok_count, TOPK, width)]
    all_gather x0 -> x1, waiting for transfers between devices: none -> 27.3 us  [body(): cot_all = lax.all_gather(cotangent[0], 'expert', axis=0)]
    all_gather x0 -> x1, blocking collectives: none -> 21.7 us  [body(): routes_all = lax.all_gather(routes[0], 'expert', axis=0)]
  transfers between devices with their start and end apart: 6 -> 6, of which waited for: 6 -> 6; matrix products, arithmetic and copies ran while one was open for 12% -> 11% of each run, Pallas kernels for 0% -> 0%
where the time goes in v1:
time: 767 us; the launch traced here: 765 us
  waiting for transfers between devices  321 us (42%)
  Pallas kernels  132 us (17%)
  matrix products  123 us (16%)
  blocking collectives  88.6 us (12%)
  other arithmetic  48.3 us (6%)
  local copies, waits for them, and re-layouts  35.4 us (5%)
  between operations  15.4 us (2%)
    pallas_call x1, Pallas kernels, moe(): pl.pallas_call(moe_kernel, name='moe', out_shape=(jax.ShapeDtypeStruct((F...  132 us
    psum x1, waiting for transfers between devices, body(): lax.psum((attn_gain_grad, query_w_grad, key_w_grad, value_w_grad, query_g...  98 us
    reduce_scatter x1, waiting for transfers between devices, body(): lax.psum_scatter(mixed_parts.reshape(16 * ROWS, width), 'expert', scatter...  84.6 us
    psum x1, waiting for transfers between devices, body(): gate_up_sum, down_w_sum = lax.psum((gate_up_w_grad, down_grad), 'dp')  80.8 us
    psum x1, blocking collectives, body(): lax.psum((attn_gain_grad, query_w_grad, key_w_grad, value_w_grad, query_g...  66.9 us
    dot_general x16, matrix products, masked_scores(): jnp.einsum('trd,sd->rts', query_pair, key_head, preferred_element_type=jn...  33.1 us
    all_gather x1, waiting for transfers between devices, body(): cot_all = lax.all_gather(cotangent[0], 'expert', axis=0)  27.3 us
    reduce_scatter x1, waiting for transfers between devices, sent_together(): whole = lax.psum_scatter(both, axis, scatter_dimension=dim, tiled=True)  23.2 us
  transfers between devices with their start and end apart: 6, of which 6 were waited for; matrix products, arithmetic and copies ran while one was open for 11% of the time, Pallas kernels for 0%

profile of v1, /device:TPU:1, one launch (start us, length us, event | category | flops | bytes accessed | tf_op | source)
XLA Modules:
  0.0 764.9 jit_solution(1128045094377457921)
XLA Ops:
  9.3 2.6 convolution_convert_fusion.1
  19.9 21.7 %all_gather.11 = s32[16,256,8]{1,2,0:T(8,128)S(1)} all-gather(s32[1,256,8]{1,2,0:T(8,128)S(1)} %copy-done.28), channel_id=1, replica_groups=mesh['dp'=8,'expert'=16] {'expert'}, dimensions={0}, use_global_device_ids=true | all-gather | bytes 139264 | tf_op jit(solution)/shard_map/all_gather | solution.py:585
  45.3 6.6 all-gather.3.cloned.1.call-done
  51.9 4.5 fusion.98
  56.4 2.9 copy.87
  59.3 3.9 copy.88
  63.3 28.6 %while.30 = (s32[]{:T(128)}, bf16[8,256,2,64]{1,3,2,0:T(8,128)(2,1)S(1)}, f32[8,2,256]{2,1,0:T(2,128)S(1)}, bf16[8,2048,64]{1,2,0:T(8,128)(2,1)S(1)}, bf16[8,204...) while((s32[]{:T(128)}, ...), condition=%wide.region_6.7_spmd.clone.clone, body=%wide.region_3.0_spmd.clone.sunk.clone | while | flops 276823552 | bytes 14373985 | solution.py:627
  91.9 3.4 multiply_reduce_fusion.4
  97.2 27.3 %all-gather.5.cloned.1.call-done.cot = bf16[16,256,1024]{2,1,0:T(8,128)(2,1)} async-done(((bf16[1,256,1024]{2,1,0:T(8,128)(2,1)}), bf16[16,256,1024]{2,1,0:T(8,128)(2,1)}) %all-gather.5.cloned.1.call-update) | async-done | bytes 8388624 | tf_op jit(solution)/shard_map/all_gather | solution.py:584
  124.5 131.6 %moe.1 = (f32[272,1024]{1,0:T(8,128)}, bf16[16,256,1024]{2,1,0:T(8,128)(2,1)}, bf16[2,1024,1024]{2,1,0:T(8,128)(2,1)}, bf16[2,512,1024]{2,1,0:T(8,128)(2,1)}) custom-call(bf16[256,1024]{1,0:T(8,128)(2,1)} %multiply_convert_fusion.ffn, bf16[16,256,1024]{2,1,0:T(8,128)(2,1)} %all-gather.5.cloned.1.call-done.cot, s32[16,2,256]{2,1,0:T(2,128)} %fusion.78.sel, ...), custom_call_target="tpu_custom_call" | custom-call | flops 49999998976 | bytes 40000000 | tf_op jit(solution)/shard_map/moe/pallas_call | solution.py:523
  258.3 2.6 multiply_reduce_fusion
  261.0 84.6 %reduce-scatter.3.cloned.1.call-done = bf16[256,1024]{1,0:T(8,128)(2,1)} async-done(((bf16[4096,1024]{1,0:T(8,128)(2,1)}), bf16[256,1024]{1,0:T(8,128)(2,1)}) %reduce-scatter.3.cloned.1.call-update) | async-done | bytes 524304 | tf_op jit(solution)/shard_map/reduce_scatter | solution.py:641
  345.6 2.8 fusion.56
  349.4 88.8 %while.31 = (s32[]{:T(128)}, f32[8,256,2,64]{1,3,2,0:T(8,128)}, bf16[8,2048,64]{1,2,0:T(8,128)(2,1)}, bf16[8,2048,64]{1,2,0:T(8,128)(2,1)}, bf16[8,2048,64]{1,2,...) while((s32[]{:T(128)}, f32[8,256,2,64]{1,3,2,0:T(8,128)}, ...), condition=%wide.region_17.18_spmd.clone.clone, body=%wide.region_15.17_spmd.clone.sunk.clone | while | flops 681737728 | bytes 34752632 | solution.py:661
  438.2 4.8 pad_maximum_fusion
  449.9 2.8 fusion.90
  452.7 2.7 fusion.65
  455.4 23.2 %reduce-scatter.5.cloned.1.call-done = bf16[256,1024]{0,1:T(8,128)(2,1)} async-done(((bf16[2048,1024]{0,1:T(8,128)(2,1)}), bf16[256,1024]{0,1:T(8,128)(2,1)}) %reduce-scatter.5.cloned.1.call-update) | async-done | bytes 524304 | tf_op jit(solution)/shard_map/reduce_scatter | solution.py:32
  486.0 80.8 %all-reduce.12.cloned.1.call-done = (bf16[2,1024,1024]{2,1,0:T(8,128)(2,1)}, bf16[2,512,1024]{2,1,0:T(8,128)(2,1)}) async-done(((bf16[2,1024,1024]{2,1,0:T(8,128)(2,1)}, bf16[2,512,1024]{2,1,0:T(8,128)(2,1)}), (bf16[2,1024,1024]{2,1,0:T(8,128)(2,1)}, bf16[2,512,1024]{2,1,0:T(8,128)(2,1)})) %all-reduce.12.cloned.1.call-update) | async-done | bytes 6291472 | tf_op jit(solution)/shard_map/psum | solution.py:717
  566.9 4.2 convert_element_type.178
  571.1 4.7 slice_convert_fusion
  579.1 66.9 %all-reduce.4 = (f32[1024]{0:T(1024)}, f32[1024]{0:T(1024)}, f32[512]{0:T(512)}, f32[1024]{0:T(1024)}) all-reduce(f32[1024]{0:T(1024)S(1)} %get-tuple-element.169, f32[1024]{0:T(1024)S(1)} %get-tuple-element.167, f32[512]{0:T(512)S(1)} %get-tuple-element.171, ...), channel_id=1, replica_groups=mesh['dp'=8,'expert'=16] {'dp','expert'}, use_global_device_ids=true, to_apply=%region_23.24 | all-reduce | flops 3584 | bytes 28672 | tf_op jit(solution)/shard_map/psum | solution.py:703
  647.1 98.0 %all-reduce.10.cloned.1.call-done = (f32[1024,1024]{1,0:T(8,128)}, f32[1024,512]{1,0:T(8,128)}, f32[1024,512]{1,0:T(8,128)}, f32[1024,1024]{1,0:T(8,128)}, f32[1024,32]{0,1:T(8,128)}) async-done(((f32[1024,1024]{1,0:T(8,128)}, f32[1024,512]{1,0:T(8,128)}, f32[1024,512]{1,0:T(8,128)}, f32[1024,1024]{1,0:T(8,128)}, f32[1024,32]{0,1:T(8,128)}), (f32[1024,1024]{1,0:T(8,128)}, f32[1024,512]{1,0:T(8,128)}, ...) | async-done | bytes 12714000 | tf_op jit(solution)/shard_map/psum | solution.py:703
  745.1 4.9 copy.143
  (263 shorter events, 161.3 us)
Async XLA Ops:
  7.2 4.7 copy-start
  7.2 4.7 copy-start.21
  7.2 44.7 %all-gather.3.cloned.1.call-start = ((), (), s32[]{:S(2)}) async-start(), calls=%async_computation.2 | async-start | bytes 4718592 | tf_op jit(solution)/shard_map/all_gather | solution.py:25
  9.3 3.2 copy-start.31
  9.3 3.2 copy-start.37
  13.8 3.1 copy-start.14
  16.0 108.5 %all-gather.5.cloned.1.call-start = ((), (), s32[]{:S(2)}) async-start(), calls=%async_computation.3 | async-start | bytes 8912896 | tf_op jit(solution)/shard_map/all_gather | solution.py:584
  16.8 328.8 %reduce-scatter.3.cloned.1.call-start = ((), (), s32[]{:S(2)}) async-start(), calls=%async_computation.4 | async-start | bytes 8912896 | tf_op jit(solution)/shard_map/reduce_scatter | solution.py:641
  91.9 3.4 copy-start.3
  91.9 3.4 copy-start.10
  256.2 222.4 %reduce-scatter.5.cloned.1.call-start = ((), (), s32[]{:S(2)}) async-start(), calls=%async_computation.5 | async-start | bytes 4718592 | tf_op jit(solution)/shard_map/reduce_scatter | solution.py:32
  345.6 2.8 copy-start.6
  443.0 123.8 %all-reduce.12.cloned.1.call-start = ((), (), s32[]{:S(2)}) async-start(), calls=%async_computation.7 | async-start | bytes 12582912 | tf_op jit(solution)/shard_map/psum | solution.py:717
  444.0 301.1 %all-reduce.10.cloned.1.call-start = ((), (), s32[]{:S(2)}) async-start(), calls=%async_computation.6 | async-start | bytes 25427968 | tf_op jit(solution)/shard_map/psum | solution.py:703
  449.8 2.9 copy-start.11
  479.6 2.2 copy-start.8
  479.6 2.2 copy-start.27
  479.6 2.4 copy-start.34
  566.9 4.2 copy-start.12
  571.1 4.7 copy-start.15
  578.4 67.6 %copy-start.32 = (f32[256]{0:T(256)S(1)}, f32[256]{0:T(256)}, u32[]{:S(2)}) copy-start(f32[256]{0:T(256)} %copy-done.31) | copy-start | bytes 3076
  745.1 4.9 copy-start.17
  750.1 2.3 copy-start.16
  752.4 2.9 copy-start.13
  (20 other events, 25.8 us)
Sparse Core Ops, SparseCore 0:
  16.2 35.7 all-gather.2
  54.0 70.4 all-gather.4
  256.3 89.2 reduce-scatter.2
  443.2 35.3 reduce-scatter.4
  480.9 85.8 all-reduce.11
  573.9 171.2 all-reduce.9

commit v2 on v1

--- a/solution.py
+++ b/solution.py
@@ -164,13 +164,14 @@
 
 
 class Gather:
-    def __init__(self, torus, buffer, send, recv, number, axis, other, low, size):
+    def __init__(self, torus, buffer, send, recv, number, axis, other, low, first, second, stride):
         self.torus, self.buffer, self.send, self.recv = torus, buffer, send, recv
-        self.number, self.axis, self.other, self.low, self.size = number, axis, other, low, size
-
-    def copy(self, which, offset, start, size, step):
-        at = self.torus.along(self.axis, self.other, offset) * ROWS + start
-        rows = self.buffer.at[pl.ds(pl.multiple_of(at, 16), size)]
+        self.number, self.axis, self.other, self.stride = number, axis, other, stride
+        self.whole, self.front, self.rear = (low, first + second), (low, first), (low + first, second)
+
+    def copy(self, which, offset, part, step):
+        at = self.torus.along(self.axis, self.other, offset) * self.stride + part[0]
+        rows = self.buffer.at[pl.ds(pl.multiple_of(at, 16), part[1])]
         return pltpu.make_async_remote_copy(
             src_ref=rows,
             dst_ref=rows,
@@ -181,27 +182,24 @@
         )
 
     def first(self):
-        self.copy(0, 0, self.low, self.size, 1).start()
-        self.copy(1, 0, self.low, self.size, -1).start()
+        self.copy(0, 0, self.whole, 1).start()
+        self.copy(1, 0, self.whole, -1).start()
 
     def second(self):
-        half = self.size // 2
-        self.copy(0, -1, self.low, self.size, 1).wait_recv()
-        self.copy(2, -1, self.low, half, 1).start()
-        self.copy(1, 1, self.low, self.size, -1).wait_recv()
-        self.copy(3, 1, self.low + half, half, -1).start()
+        self.copy(0, -1, self.whole, 1).wait_recv()
+        self.copy(2, -1, self.front, 1).start()
+        self.copy(1, 1, self.whole, -1).wait_recv()
+        self.copy(3, 1, self.rear, -1).start()
 
     def third(self):
-        half = self.size // 2
-        self.copy(2, 2, self.low, half, 1).wait_recv()
-        self.copy(3, 2, self.low + half, half, -1).wait_recv()
+        self.copy(2, 2, self.front, 1).wait_recv()
+        self.copy(3, 2, self.rear, -1).wait_recv()
 
     def drain(self):
-        half = self.size // 2
-        self.copy(0, 0, self.low, self.size, 1).wait_send()
-        self.copy(1, 0, self.low, self.size, -1).wait_send()
-        self.copy(2, -1, self.low, half, 1).wait_send()
-        self.copy(3, 1, self.low + half, half, -1).wait_send()
+        self.copy(0, 0, self.whole, 1).wait_send()
+        self.copy(1, 0, self.whole, -1).wait_send()
+        self.copy(2, -1, self.front, 1).wait_send()
+        self.copy(3, 1, self.rear, -1).wait_send()
 
 
 class Scatter:
@@ -283,9 +281,9 @@
 
 
 def moe_kernel(
-    ffn, cot, sel, mem, wr, w_gate, w_up, w_down,
+    ffn, cot, wr, w_gate, w_up, w_down,
     ret, mixed, grad_gu, grad_d,
-    rows, sums, wgu, wd, held, pair, inner, dgu, mixing, back, cotv, gate_rows, grad_rows, stage,
+    rows, sums, wgu, wd, held, pair, inner, dgu, mixing, back, cotv, before, chosen, gate_rows, grad_rows, stage,
     ag_send, ag_recv, rs_send, rs_recv, w_sem, cot_sem, stage_sem, credit,
 ):
     torus = Torus()
@@ -305,14 +303,14 @@
         return (torus.z + g + (g // 2) * (1 - 2 * (g % 2))) % RING
 
     def cot_copy(g):
-        return pltpu.make_async_copy(cot.at[pl.ds(group_z(g) * RING, RING)], cotv, cot_sem)
+        return pltpu.make_async_copy(cot.at[pl.ds(pl.multiple_of(group_z(g) * RING * FULL, 16), RING * FULL)], cotv, cot_sem)
 
     cot_copy(0).start()
     rows[pl.ds(pl.multiple_of(torus.expert * ROWS, ROWS), ROWS)] = ffn[...]
     pl.semaphore_wait(barrier, 4)
 
     def gather(number, axis, other, low):
-        return Gather(torus, rows, ag_send, ag_recv, number, axis, other, low, ROWS // 2)
+        return Gather(torus, rows, ag_send, ag_recv, number, axis, other, low, ROWS // 4, ROWS // 4, ROWS)
 
     a_first = gather(0, "y", 0, 0)
     b_first = gather(1, "z", 0, ROWS // 2)
@@ -336,13 +334,9 @@
     for copy in weights:
         copy.wait()
 
-    def choice(source, e):
-        return lax.broadcasted_iota(jnp.int32, (CAP, ROWS), 0) == sel[source, pl.ds(e, 1), :]
-
-    def choices(source):
-        picked = [choice(source, e) for e in range(2)]
-        both = jnp.concatenate([p.astype(jnp.float32) for p in picked], axis=0)
-        return picked, both.astype(jnp.bfloat16)
+    earlier = lax.broadcasted_iota(jnp.int32, (ROWS, ROWS), 0) < lax.broadcasted_iota(jnp.int32, (ROWS, ROWS), 1)
+    before[...] = jnp.where(earlier, 1.0, 0.0).astype(jnp.bfloat16)
+    slot_at = lax.broadcasted_iota(jnp.int32, (CAP, ROWS), 0).astype(jnp.float32)
 
     def stage_copy(slot, target):
         return pltpu.make_async_copy(stage.at[slot], target, stage_sem.at[slot])
@@ -383,20 +377,31 @@
         def _(j):
             source = first_source + j
             block = rows[pl.ds(pl.multiple_of(source * ROWS, ROWS), ROWS)]
-            named = mem[source].astype(jnp.float32) > 0.5
+            laid = cotv[pl.ds(pl.multiple_of(j * FULL, 16), EXTRA)].astype(jnp.float32)
+            member = jnp.concatenate([laid[:8, q * ROWS : (q + 1) * ROWS] for q in range(4)], axis=0)
+            named = member > 0.5
+            slots = dot_nn(member.astype(jnp.bfloat16), before[...])
+            slots = jnp.where(named, slots, -1.0)
             logits = jnp.where(named, dot_nt(wr[...], block), -1e30)
             weight = jnp.where(named, jnp.exp(logits - jnp.max(logits, axis=0, keepdims=True)), 0.0)
             gates = weight / jnp.sum(weight, axis=0, keepdims=True)
-            picked, both = choices(source)
+            picked = []
+            for e in range(2):
+                own = jnp.sum(
+                    jnp.where(expert_rows == torus.expert * 2 + e, slots, 0.0), axis=0, keepdims=True
+                )
+                picked.append(jnp.where(slot_at == own, 1.0, 0.0))
+            both = jnp.concatenate(picked, axis=0).astype(jnp.bfloat16)
+            chosen[j] = both
             took = dot_nn(both, block).astype(jnp.bfloat16)
-            took_grad = dot_nn(both, cotv[j]).astype(jnp.bfloat16)
+            took_grad = dot_nn(both, cotv[pl.ds(pl.multiple_of(j * FULL + EXTRA, 16), ROWS)]).astype(jnp.bfloat16)
             here = pl.ds(pl.multiple_of(j * CAP, 16), CAP)
             there = pl.ds(pl.multiple_of(g * GROUP + j * CAP, 16), CAP)
             for e in range(2):
                 own = jnp.sum(
                     jnp.where(expert_rows == torus.expert * 2 + e, gates, 0.0), axis=0, keepdims=True
                 )
-                of_rows = jnp.sum(jnp.where(picked[e], own, 0.0), axis=1, keepdims=True)
+                of_rows = jnp.sum(picked[e] * own, axis=1, keepdims=True)
                 gate_rows[e, here] = jnp.broadcast_to(of_rows, (CAP, 128))
                 held[e, there] = took[e * CAP : (e + 1) * CAP]
                 mixing[e, here] = took_grad[e * CAP : (e + 1) * CAP]
@@ -435,14 +440,15 @@
         @pl.loop(0, 4)
         def _(j):
             source = first_source + j
-            picked, both = choices(source)
+            both = chosen[j]
+            picked = both.astype(jnp.float32)
             here = pl.ds(pl.multiple_of(j * CAP, 16), CAP)
             part = dot_tn(both, jnp.concatenate([back[0, here], back[1, here]], axis=0))
             sums[source, pl.ds(EXTRA, ROWS)] = part.astype(jnp.bfloat16)
             grads = jnp.zeros((EXPERTS, ROWS), jnp.float32)
             for e in range(2):
                 own = jnp.sum(
-                    jnp.where(picked[e], grad_rows[e, here][:, :1], 0.0), axis=0, keepdims=True
+                    picked[e * CAP : (e + 1) * CAP] * grad_rows[e, here][:, :1], axis=0, keepdims=True
                 )
                 grads = grads + jnp.where(expert_rows == torus.expert * 2 + e, own, 0.0)
             laid = jnp.concatenate([grads[8 * q : 8 * q + 8] for q in range(4)], axis=1)
@@ -517,7 +523,7 @@
         one.drain()
 
 
-def moe(ffn_in, cot_all, sel, mem, router_rows, w_gate, w_up, w_down):
+def moe(ffn_in, cot_all, router_rows, w_gate, w_up, w_down):
     vmem, hbm = pl.BlockSpec(memory_space=pltpu.VMEM), pl.BlockSpec(memory_space=pl.ANY)
     low, total = jnp.bfloat16, 4 * GROUP
     return pl.pallas_call(
@@ -529,7 +535,7 @@
             jax.ShapeDtypeStruct((2, 1024, 1024), low),
             jax.ShapeDtypeStruct((2, 512, 1024), low),
         ),
-        in_specs=[vmem, hbm, vmem, vmem, vmem, hbm, hbm, hbm],
+        in_specs=[vmem, hbm, vmem, hbm, hbm, hbm],
         out_specs=(vmem, hbm, hbm, hbm),
         scratch_shapes=[
             pltpu.VMEM((16 * ROWS, 1024), low),
@@ -542,7 +548,9 @@
             pltpu.VMEM((2, total, 1024), low),
             pltpu.VMEM((2, GROUP, 1024), low),
             pltpu.VMEM((2, GROUP, 1024), low),
-            pltpu.VMEM((4, ROWS, 1024), low),
+            pltpu.VMEM((4 * FULL, 1024), low),
+            pltpu.VMEM((ROWS, ROWS), low),
+            pltpu.VMEM((4, 2 * CAP, ROWS), low),
             pltpu.VMEM((2, GROUP, 128), jnp.float32),
             pltpu.VMEM((2, GROUP, 128), jnp.float32),
             pltpu.VMEM((2, ROWS, 1024), low),
@@ -559,7 +567,522 @@
             collective_id=1, has_side_effects=True, vmem_limit_bytes=63 * 2**20
         ),
         cost_estimate=pl.CostEstimate(flops=50 * 10**9, bytes_accessed=40 * 10**6, transcendentals=2 * 10**6),
-    )(ffn_in, cot_all, sel, mem, router_rows, w_gate, w_up, w_down)
+    )(ffn_in, cot_all, router_rows, w_gate, w_up, w_down)
+
+
+def everywhere():
+    dp, expert = lax.axis_index("dp"), lax.axis_index("expert")
+    here = {"x": dp // 2, "core": dp % 2, "z": expert // RING, "y": expert % RING}
+
+    def device(axis, step):
+        there = dict(here)
+        size = 2 if axis == "core" else RING
+        there[axis] = (here[axis] + step + size) % size
+        return (there["x"] * 2 + there["core"], there["z"] * RING + there["y"])
+
+    return here, device
+
+
+def rms_scale(values):
+    return lax.rsqrt(jnp.mean(values * values, axis=-1, keepdims=True) + epsilon)
+
+
+def turned_rows(values, cosine, sine):
+    front, back = values[: HEAD_DIM // 2], values[HEAD_DIM // 2 :]
+    return jnp.concatenate([front * cosine - back * sine, back * cosine + front * sine], axis=0)
+
+
+def kv_order(here, step):
+    turn = step // 2
+    return (turn % 2) * (3 - turn // 2) + (1 - turn % 2) * (turn // 2)
+
+
+class Keys:
+    def __init__(self, here, device, blocks, send, recv):
+        self.here, self.device, self.blocks, self.send, self.recv = here, device, blocks, send, recv
+        self.lines = blocks.shape[1]
+
+    def copy(self, which):
+        half = self.lines // 2
+        offset, start, size, axis, step = (
+            (0, 0, self.lines, "core", 1),
+            (0, 0, self.lines, "x", 1),
+            (0, 0, self.lines, "x", -1),
+            (-1, 0, half, "x", 1),
+            (1, half, half, "x", -1),
+            (-1, 0, self.lines, "core", 1),
+            (1, 0, self.lines, "core", 1),
+            (2, 0, self.lines, "core", 1),
+        )[which]
+        block = (self.here["x"] + offset + RING) % RING * 2 + self.here["core"]
+        part = self.blocks.at[block, pl.ds(start, size)]
+        return pltpu.make_async_remote_copy(
+            src_ref=part,
+            dst_ref=part,
+            send_sem=self.send.at[which],
+            recv_sem=self.recv.at[which],
+            device_id=self.device(axis, step),
+            device_id_type=MESH,
+        )
+
+    def start(self, *which):
+        for one in which:
+            self.copy(one).start()
+
+    def arrive(self, *which):
+        for one in which:
+            self.copy(one).wait_recv()
+
+    def drain(self):
+        for one in range(8):
+            self.copy(one).wait_send()
+
+
+def forward_kernel(
+    tokens, cot, routes_t, length, cosine, sine, attn_gain, query_gain, key_gain, ffn_gain,
+    w_query, w_key, w_value, w_output,
+    ffn_in, hidden, mixed_t, queries, log_total, normed, query_raw, key_raw, kv_all, cot_all,
+    wq, wk, wv, wo, kv, turned, most, total, mixed, packed,
+    ag_send, ag_recv, kv_send, kv_recv, w_sem, kv_sem, own_sem,
+):
+    torus = Torus()
+    here, device = everywhere()
+    me = here["x"] * 2 + here["core"]
+    barrier = pltpu.get_barrier_semaphore()
+    peers = [*torus.neighbours(), device("core", 1), device("x", 1), device("x", -1)]
+    for peer in peers:
+        pl.semaphore_signal(barrier, inc=1, device_id=peer, device_id_type=MESH)
+    loads = [
+        pltpu.make_async_copy(source, target, w_sem.at[n])
+        for n, (source, target) in enumerate(((w_query, wq), (w_key, wk), (w_value, wv), (w_output, wo)))
+    ]
+    for load in loads:
+        load.start()
+
+    expert_rows = lax.broadcasted_iota(jnp.int32, (EXPERTS, ROWS), 0)
+    member = jnp.zeros((EXPERTS, ROWS), jnp.float32)
+    for k in range(TOPK):
+        member = member + jnp.where(expert_rows == routes_t[pl.ds(k, 1), :], 1.0, 0.0)
+    laid = jnp.concatenate([member[8 * q : 8 * q + 8] for q in range(4)], axis=1)
+    packed[...] = jnp.concatenate([laid, jnp.zeros_like(laid)], axis=0).astype(jnp.bfloat16)
+    first_row = pl.multiple_of(torus.expert * FULL, 16)
+    owns = [
+        pltpu.make_async_copy(packed, cot_all.at[pl.ds(first_row, EXTRA)], own_sem.at[0]),
+        pltpu.make_async_copy(cot, cot_all.at[pl.ds(pl.multiple_of(first_row + EXTRA, 16), ROWS)], own_sem.at[1]),
+    ]
+    for copy in owns:
+        copy.start()
+    for copy in owns:
+        copy.wait()
+    pl.semaphore_wait(barrier, len(peers))
+
+    def gather(number, axis, other, low, first, second):
+        return Gather(torus, cot_all, ag_send, ag_recv, number, axis, other, low, first, second, FULL)
+
+    a_first = gather(0, "y", 0, 0, 64, 64)
+    b_first = gather(1, "z", 0, 128, 80, 64)
+    a_second = {d: gather(2 + d % RING, "z", d, 0, 64, 64) for d in (0, 1, -1, 2)}
+    b_second = {d: gather(6 + d % RING, "y", d, 128, 80, 64) for d in (0, 1, -1, 2)}
+    gathers = [a_first, b_first, *a_second.values(), *b_second.values()]
+    a_first.first()
+    b_first.first()
+    b_second[0].first()
+    a_second[0].first()
+
+    @pl.loop(0, 4)
+    def _(n):
+        at = pl.ds(pl.multiple_of(n * 64, 64), 64)
+        rows = tokens[at].astype(jnp.float32)
+        normed[at] = (rows * rms_scale(rows) * attn_gain[...].astype(jnp.float32)).astype(jnp.bfloat16)
+
+    for load in loads:
+        load.wait()
+
+    keys = Keys(here, device, kv, kv_send, kv_recv)
+    key_raw[...] = dot_nn(normed[...], wk[...])
+    scaled = key_raw[...]
+    scaled = (scaled * rms_scale(scaled) * key_gain[...].astype(jnp.float32)).T
+    for j in range(KV_HEADS):
+        head = turned_rows(scaled[j * 64 : j * 64 + 64], cosine[...], sine[...])
+        kv[me, pl.ds(j * 64, 64)] = head.astype(jnp.bfloat16)
+    kv[me, pl.ds(512, 512)] = dot_nn(normed[...], wv[...]).T.astype(jnp.bfloat16)
+    keys.start(0, 1, 2)
+    query_raw[...] = dot_nn(normed[...], wq[...])
+    scaled = query_raw[...]
+    turned[...] = (scaled * rms_scale(scaled) * query_gain[...].astype(jnp.float32)).T
+
+    @pl.loop(0, KV_HEADS)
+    def _(j):
+        for r in range(2):
+            head = turned[pl.ds(pl.multiple_of(j * 128 + r * 64, 64), 64)]
+            head = turned_rows(head, cosine[...], sine[...])
+            queries[j, :, r * ROWS : (r + 1) * ROWS] = (head * HEAD_DIM**-0.5).astype(jnp.bfloat16)
+
+    a_first.second()
+    b_first.second()
+    for d in (1, -1):
+        b_second[d].first()
+        a_second[d].first()
+
+    key_at = lax.broadcasted_iota(jnp.int32, (ROWS, 2 * ROWS), 0)
+    query_at = lax.broadcasted_iota(jnp.int32, (ROWS, 2 * ROWS), 1) % ROWS
+    valid = (key_at <= query_at) & (key_at + me * ROWS < length[...])
+
+    @pl.loop(0, KV_HEADS)
+    def _(j):
+        key_head = kv[me, pl.ds(pl.multiple_of(j * 64, 64), 64)]
+        value_head = kv[me, pl.ds(pl.multiple_of(512 + j * 64, 64), 64)]
+        scores = jnp.where(valid, dot_tn(key_head, queries[j]), -1e30)
+        top = jnp.max(scores, axis=0, keepdims=True)
+        probs = jnp.exp(scores - top)
+        most[j] = top
+        total[j] = jnp.sum(probs, axis=0, keepdims=True)
+        mixed[j] = dot_nn(value_head, probs.astype(jnp.bfloat16))
+
+    @pl.loop(1, 8)
+    def _(step):
+        @pl.when(step == 1)
+        def _():
+            a_first.third()
+            b_first.third()
+            b_second[2].first()
+            a_second[2].first()
+            keys.arrive(0)
+
+        @pl.when(step == 2)
+        def _():
+            keys.arrive(1)
+            keys.start(3, 5)
+            keys.arrive(2)
+            keys.start(4, 6)
+            b_second[0].second()
+            a_second[0].second()
+
+        @pl.when(step == 3)
+        def _():
+            keys.arrive(5)
+            for d in (1, -1):
+                b_second[d].second()
+                a_second[d].second()
+
+        @pl.when(step == 5)
+        def _():
+            keys.arrive(3, 4)
+            keys.start(7)
+            keys.arrive(6)
+            b_second[2].second()
+            a_second[2].second()
+
+        @pl.when(step == 7)
+        def _():
+            keys.arrive(7)
+
+        block = (here["x"] + kv_order(here, step) + RING) % RING * 2 + (here["core"] + step) % 2
+
+        @pl.when(block < me)
+        def _():
+            @pl.loop(0, KV_HEADS)
+            def _(j):
+                key_head = kv[block, pl.ds(pl.multiple_of(j * 64, 64), 64)]
+                value_head = kv[block, pl.ds(pl.multiple_of(512 + j * 64, 64), 64)]
+                scores = dot_tn(key_head, queries[j])
+                before = most[j]
+                top = jnp.maximum(before, jnp.max(scores, axis=0, keepdims=True))
+                probs = jnp.exp(scores - top)
+                less = jnp.exp(before - top)
+                most[j] = top
+                total[j] = total[j] * less + jnp.sum(probs, axis=0, keepdims=True)
+                mixed[j] = mixed[j] * less + dot_nn(value_head, probs.astype(jnp.bfloat16))
+
+    save = pltpu.make_async_copy(kv, kv_all, kv_sem)
+    save.start()
+
+    @pl.loop(0, KV_HEADS)
+    def _(j):
+        share = total[j]
+        log_total[j] = most[j] + jnp.log(share)
+        head = (mixed[j] / share).astype(jnp.bfloat16)
+        for r in range(2):
+            mixed_t[pl.ds(pl.multiple_of(j * 128 + r * 64, 64), 64), :] = head[:, r * ROWS : (r + 1) * ROWS]
+
+    hidden[...] = dot_tn(mixed_t[...], wo[...])
+
+    @pl.loop(0, 4)
+    def _(n):
+        at = pl.ds(pl.multiple_of(n * 64, 64), 64)
+        rows = hidden[at] + tokens[at].astype(jnp.float32)
+        hidden[at] = rows
+        ffn_in[at] = (rows * rms_scale(rows) * ffn_gain[...].astype(jnp.float32)).astype(jnp.bfloat16)
+
+    for d in (0, 1, -1, 2):
+        a_second[d].third()
+        b_second[d].third()
+    save.wait()
+    keys.drain()
+    for one in gathers:
+        one.drain()
+
+
+def forward(tokens, cot, routes_t, length, cosine, sine, gains, weights):
+    vmem, hbm = pl.BlockSpec(memory_space=pltpu.VMEM), pl.BlockSpec(memory_space=pl.ANY)
+    low, wide = jnp.bfloat16, jnp.float32
+    shape = jax.ShapeDtypeStruct
+    return pl.pallas_call(
+        forward_kernel,
+        name="forward",
+        out_shape=(
+            shape((ROWS, 1024), low),
+            shape((ROWS, 1024), wide),
+            shape((1024, ROWS), low),
+            shape((KV_HEADS, HEAD_DIM, 2 * ROWS), low),
+            shape((KV_HEADS, 1, 2 * ROWS), wide),
+            shape((ROWS, 1024), low),
+            shape((ROWS, 1024), wide),
+            shape((ROWS, 512), wide),
+            shape((8, 1024, ROWS), low),
+            shape((16 * FULL, 1024), low),
+        ),
+        in_specs=[vmem] * 10 + [hbm] * 4,
+        out_specs=(vmem,) * 8 + (hbm, hbm),
+        scratch_shapes=[
+            pltpu.VMEM((1024, 1024), low),
+            pltpu.VMEM((1024, 512), low),
+            pltpu.VMEM((1024, 512), low),
+            pltpu.VMEM((1024, 1024), low),
+            pltpu.VMEM((8, 1024, ROWS), low),
+            pltpu.VMEM((1024, ROWS), wide),
+            pltpu.VMEM((KV_HEADS, 1, 2 * ROWS), wide),
+            pltpu.VMEM((KV_HEADS, 1, 2 * ROWS), wide),
+            pltpu.VMEM((KV_HEADS, HEAD_DIM, 2 * ROWS), wide),
+            pltpu.VMEM((EXTRA, 1024), low),
+            pltpu.SemaphoreType.DMA((10, 4)),
+            pltpu.SemaphoreType.DMA((10, 4)),
+            pltpu.SemaphoreType.DMA((8,)),
+            pltpu.SemaphoreType.DMA((8,)),
+            pltpu.SemaphoreType.DMA((4,)),
+            pltpu.SemaphoreType.DMA,
+            pltpu.SemaphoreType.DMA((2,)),
+        ],
+        compiler_params=pltpu.CompilerParams(
+            collective_id=3, has_side_effects=True, vmem_limit_bytes=56 * 2**20
+        ),
+    )(tokens, cot, routes_t, length, cosine, sine, *gains, *weights)
+
+
+ORDERS = (("x", "y", "z"), ("y", "z", "x"), ("z", "x", "y"))
+
+
+class Total:
+    def __init__(self, here, device, buffer, final, landing, work, send, recv, number, half, start, rows, base, order):
+        self.here, self.device, self.buffer, self.final = here, device, buffer, final
+        self.landing, self.work = landing, work
+        self.send, self.recv, self.number, self.order = send, recv, number, order
+        self.half, self.start, self.rows, self.base = half, start, rows, base
+
+    def own(self):
+        return self.here["core"] * self.half + self.start
+
+    def copy(self, which, source, target, axis, step):
+        return pltpu.make_async_remote_copy(
+            src_ref=source,
+            dst_ref=target,
+            send_sem=self.send.at[self.number, which],
+            recv_sem=self.recv.at[self.number, which],
+            device_id=self.device(axis, step),
+            device_id_type=MESH,
+        )
+
+    def part(self, ref, at, size):
+        return ref.at[pl.ds(pl.multiple_of(at, 16), size)]
+
+    def copies(self, stage):
+        r, own = self.rows, self.own()
+        a, b, c = self.order
+        ia, ib = self.here[a], self.here[b]
+        second = own + ia * (r // 4)
+        third = second + ib * (r // 16)
+        land1, land2, land3 = self.base + r, self.base + r + 3 * (r // 4), self.base + r + 3 * (r // 4) + 3 * (r // 16)
+        if stage == 0:
+            there = (1 - self.here["core"]) * self.half + self.start
+            return [self.copy(0, self.part(self.buffer, there, r), self.part(self.landing, self.base, r), "core", 1)]
+        if stage == 6:
+            whole = self.part(self.final, own, r)
+            return [self.copy(16, whole, whole, "core", 1)]
+        found = []
+        for d in (1, 2, 3):
+            if stage == 1:
+                source = self.part(self.buffer, own + (ia + d) % RING * (r // 4), r // 4)
+                target, axis = self.part(self.landing, land1 + (d - 1) * (r // 4), r // 4), a
+            elif stage == 2:
+                source = self.part(self.buffer, second + (ib + d) % RING * (r // 16), r // 16)
+                target, axis = self.part(self.landing, land2 + (d - 1) * (r // 16), r // 16), b
+            elif stage == 3:
+                source = self.work.at[self.number, pl.ds(0, r // 16)]
+                target, axis = self.part(self.landing, land3 + (d - 1) * (r // 16), r // 16), c
+            elif stage == 4:
+                source = self.part(self.final, third, r // 16)
+                target, axis = source, b
+            else:
+                source = self.part(self.final, second, r // 4)
+                target, axis = source, a
+            found.append(self.copy(1 + (stage - 1) * 3 + d - 1, source, target, axis, d))
+        return found
+
+    def begin(self, stage):
+        for copy in self.copies(stage):
+            copy.start()
+
+    def add(self, target, start, size, lands):
+        @pl.loop(0, size // 16)
+        def _(k):
+            here = pl.ds(pl.multiple_of(start + k * 16, 16), 16)
+            total = self.buffer[here].astype(jnp.float32)
+            for land in lands:
+                total = total + self.landing[pl.ds(pl.multiple_of(land + k * 16, 16), 16)].astype(jnp.float32)
+            if target is None:
+                self.buffer[here] = total.astype(jnp.bfloat16)
+            else:
+                target[pl.ds(pl.multiple_of(k * 16, 16), 16)] = total.astype(jnp.bfloat16)
+
+    def finish(self, stage):
+        for copy in self.copies(stage):
+            copy.wait_recv()
+        r, own = self.rows, self.own()
+        a, b, _ = self.order
+        second = own + self.here[a] * (r // 4)
+        third = second + self.here[b] * (r // 16)
+        land1, land2, land3 = self.base + r, self.base + r + 3 * (r // 4), self.base + r + 3 * (r // 4) + 3 * (r // 16)
+        if stage == 0:
+            self.add(None, own, r, [self.base])
+        elif stage == 1:
+            self.add(None, second, r // 4, [land1 + d * (r // 4) for d in range(3)])
+        elif stage == 2:
+            self.add(self.work.at[self.number], third, r // 16, [land2 + d * (r // 16) for d in range(3)])
+        elif stage == 3:
+            r16 = r // 16
+
+            @pl.loop(0, r16 // 16)
+            def _(k):
+                total = self.work[self.number, pl.ds(pl.multiple_of(k * 16, 16), 16)].astype(jnp.float32)
+                for d in range(3):
+                    at = land3 + d * r16 + k * 16
+                    total = total + self.landing[pl.ds(pl.multiple_of(at, 16), 16)].astype(jnp.float32)
+                self.final[pl.ds(pl.multiple_of(third + k * 16, 16), 16)] = total.astype(jnp.bfloat16)
+
+    def drain(self):
+        for stage in range(7):
+            for copy in self.copies(stage):
+                copy.wait_send()
+
+
+class Small:
+    STAGES = (("core", (1,)), ("x", (1, 2, 3)), ("y", (1, 2, 3)), ("z", (1, 2, 3)))
+
+    def __init__(self, device, value, landing, send, recv):
+        self.device, self.value, self.landing, self.send, self.recv = device, value, landing, send, recv
+
+    def copies(self, stage):
+        axis, steps = self.STAGES[stage]
+        first = sum(len(s) for _, s in self.STAGES[:stage])
+        return [
+            pltpu.make_async_remote_copy(
+                src_ref=self.value.at[stage],
+                dst_ref=self.landing.at[first + n],
+                send_sem=self.send.at[first + n],
+                recv_sem=self.recv.at[first + n],
+                device_id=self.device(axis, step),
+                device_id_type=MESH,
+            )
+            for n, step in enumerate(steps)
+        ]
+
+    def begin(self, stage):
+        for copy in self.copies(stage):
+            copy.start()
+
+    def finish(self, stage):
+        for copy in self.copies(stage):
+            copy.wait_recv()
+        first = sum(len(s) for _, s in self.STAGES[:stage])
+        total = self.value[stage]
+        for n in range(len(self.STAGES[stage][1])):
+            total = total + self.landing[first + n]
+        self.value[stage + 1] = total
+
+    def drain(self):
+        for stage in range(4):
+            for copy in self.copies(stage):
+                copy.wait_send()
+
+
+def total_kernel(parts, small, whole, small_whole, held, landing, work, values, small_landing, send, recv, small_send, small_recv, load_sem):
+    here, device = everywhere()
+    barrier = pltpu.get_barrier_semaphore()
+    peers = [device("core", 1)] + [device(axis, d) for axis in "xyz" for d in (1, 2, 3)]
+    for peer in peers:
+        pl.semaphore_signal(barrier, inc=1, device_id=peer, device_id_type=MESH)
+    load = pltpu.make_async_copy(parts, held, load_sem)
+    load.start()
+    values[0] = small[...]
+    load.wait()
+    pl.semaphore_wait(barrier, len(peers))
+    half = whole.shape[0] // 2
+    rows = half // 3
+    room = rows + 3 * (rows // 4) + 6 * (rows // 16)
+    streams = [
+        Total(here, device, held, whole, landing, work, send, recv, s, half, s * rows, rows, s * room, ORDERS[s])
+        for s in range(3)
+    ]
+    few = Small(device, values, small_landing, small_send, small_recv)
+    for one in streams:
+        one.begin(0)
+    few.begin(0)
+    for stage in range(7):
+        for one in streams:
+            one.finish(stage)
+            if stage < 6:
+                one.begin(stage + 1)
+        if stage < 4:
+            few.finish(stage)
+            if stage < 3:
+                few.begin(stage + 1)
+    small_whole[...] = values[4]
+    for one in streams:
+        one.drain()
+    few.drain()
+
+
+def total_everywhere(parts, small):
+    vmem, hbm = pl.BlockSpec(memory_space=pltpu.VMEM), pl.BlockSpec(memory_space=pl.ANY)
+    low = jnp.bfloat16
+    rows, width = parts.shape
+    third = rows // 6
+    room = third + 3 * (third // 4) + 6 * (third // 16)
+    return pl.pallas_call(
+        total_kernel,
+        name="total",
+        out_shape=(
+            jax.ShapeDtypeStruct(parts.shape, low),
+            jax.ShapeDtypeStruct(small.shape, jnp.float32),
+        ),
+        in_specs=[hbm, vmem],
+        out_specs=(vmem, vmem),
+        scratch_shapes=[
+            pltpu.VMEM((rows, width), low),
+            pltpu.VMEM((3 * room, width), low),
+            pltpu.VMEM((3, third // 16, width), low),
+            pltpu.VMEM((5, *small.shape), jnp.float32),
+            pltpu.VMEM((10, *small.shape), jnp.float32),
+            pltpu.SemaphoreType.DMA((3, 17)),
+            pltpu.SemaphoreType.DMA((3, 17)),
+            pltpu.SemaphoreType.DMA((10,)),
+            pltpu.SemaphoreType.DMA((10,)),
+            pltpu.SemaphoreType.DMA,
+        ],
+        compiler_params=pltpu.CompilerParams(
+            collective_id=2, has_side_effects=True, vmem_limit_bytes=56 * 2**20
+        ),
+    )(parts, small)
 
 
 def body(
@@ -580,17 +1103,6 @@
     w_up,
     w_down,
 ):
-    local_experts = w_gate.shape[0]
-    cot_all = lax.all_gather(cotangent[0], "expert", axis=0)
-    routes_all = lax.all_gather(routes[0], "expert", axis=0)
-    member = (
-        (routes_all[:, :, :, None] == jnp.arange(EXPERTS, dtype=jnp.int32)).any(axis=2).astype(jnp.bfloat16)
-    )
-    mem = member.transpose(0, 2, 1)
-    before = jnp.triu(jnp.ones((ROWS, ROWS), jnp.bfloat16), 1)
-    own_mem = lax.dynamic_slice_in_dim(mem, lax.axis_index("expert") * local_experts, local_experts, 1)
-    slots = jnp.einsum("seu,ut->set", own_mem, before, preferred_element_type=jnp.float32).astype(jnp.int32)
-    sel = jnp.where((own_mem > 0) & (slots < CAP), slots, -1)
     token_rows = tokens[0].astype(jnp.float32)
     tok_count = token_rows.shape[0]
     width = token_rows.shape[1]
@@ -600,11 +1112,17 @@
     key_pos = jnp.arange(seq_total, dtype=jnp.int32)
     key_valid = (key_pos[None, :] <= query_pos[:, None]) & (key_pos[None, :] < lengths[0])
     cosine, sine_table = rope_tables(query_pos)
-    normed_value, attn_pull = jax.vjp(norm_rows, token_rows, attn_gain.astype(jnp.float32))
-    normed = normed_value.astype(jnp.bfloat16)
-    query_raw = jnp.dot(normed, w_query, preferred_element_type=jnp.float32)
-    key_raw = jnp.dot(normed, w_key, preferred_element_type=jnp.float32)
-    value_raw = jnp.dot(normed, w_value, preferred_element_type=jnp.float32)
+    ffn_in, hidden_res, mixed_t, queries_t, log_totals, normed, query_raw, key_raw, kv_all, cot_all = forward(
+        tokens[0],
+        cotangent[0],
+        routes[0].T,
+        lengths.reshape(1, 1),
+        cosine.T,
+        sine_table.T,
+        [gain.reshape(1, -1) for gain in (attn_gain, query_gain, key_gain, ffn_gain)],
+        (w_query, w_key, w_value, w_output),
+    )
+    _, attn_pull = jax.vjp(norm_rows, token_rows, attn_gain.astype(jnp.float32))
 
     def post_norm(query_in, key_in, gain_query, gain_key):
         return (
@@ -612,31 +1130,21 @@
             rotate(norm_rows(key_in, gain_key), cosine, sine_table),
         )
 
-    post_values, post_pull = jax.vjp(
+    _, post_pull = jax.vjp(
         post_norm, query_raw, key_raw, query_gain.astype(jnp.float32), key_gain.astype(jnp.float32)
     )
-    queries = post_values[0].astype(jnp.bfloat16)
-    keys_own = post_values[1].astype(jnp.bfloat16)
-    values_own = value_raw.astype(jnp.bfloat16)
-    keys_full, values_full = in_one_piece((keys_own, values_own), "dp", 0, 1)
-    query_groups = queries.reshape(tok_count, KV_HEADS, HEADS // KV_HEADS, HEAD_DIM).transpose(
-        1, 0, 2, 3
-    )
-    key_groups = keys_full.reshape(seq_total, KV_HEADS, HEAD_DIM).transpose(1, 0, 2)
-    value_groups = values_full.reshape(seq_total, KV_HEADS, HEAD_DIM).transpose(1, 0, 2)
-    mixed_heads, log_totals = lax.map(
-        lambda operands: forward_head(operands, key_valid), (query_groups, key_groups, value_groups)
-    )
-    attended = mixed_heads.transpose(1, 0, 2, 3).reshape(tok_count, width).astype(jnp.bfloat16)
-    hidden_res = token_rows + jnp.dot(attended, w_output, preferred_element_type=jnp.float32)
-    ffn_value, ffn_pull = jax.vjp(norm_rows, hidden_res, ffn_gain.astype(jnp.float32))
-    ffn_in = ffn_value.astype(jnp.bfloat16)
+    query_groups = queries_t.reshape(KV_HEADS, HEAD_DIM, 2, tok_count).transpose(0, 3, 2, 1) * 8
+    key_groups = kv_all[:, :512].reshape(8, KV_HEADS, HEAD_DIM, ROWS).transpose(1, 0, 3, 2).reshape(KV_HEADS, seq_total, HEAD_DIM)
+    value_groups = kv_all[:, 512:].reshape(8, KV_HEADS, HEAD_DIM, ROWS).transpose(1, 0, 3, 2).reshape(KV_HEADS, seq_total, HEAD_DIM)
+    log_totals = log_totals.reshape(KV_HEADS, 2, tok_count)
+    attended = mixed_t.T
+    _, ffn_pull = jax.vjp(norm_rows, hidden_res, ffn_gain.astype(jnp.float32))
     logits = jnp.dot(ffn_in, w_router, preferred_element_type=jnp.float32)
     own_routes = (routes[0][:, :, None] == jnp.arange(EXPERTS, dtype=jnp.int32)).any(axis=1)
     gates = jax.nn.softmax(jnp.where(own_routes, logits, -1e30), axis=-1)
     gates = jnp.where(own_routes, gates, 0.0)
     returned, mixed_parts, gate_up_w_grad, down_grad = moe(
-        ffn_in, cot_all, sel, mem, w_router.T, w_gate, w_up, w_down
+        ffn_in, cot_all, w_router.T, w_gate, w_up, w_down
     )
     mixed_sum = lax.psum_scatter(
         mixed_parts.reshape(16 * ROWS, width), "expert", scatter_dimension=0, tiled=True
@@ -690,30 +1198,33 @@
     )
     token_part, attn_gain_grad = attn_pull(normed_grad)
     token_grad = (hidden_grad + token_part).astype(jnp.bfloat16)
-    (
-        attn_gain_sum,
-        query_w_sum,
-        key_w_sum,
-        value_w_sum,
-        query_gain_sum,
-        key_gain_sum,
-        output_w_sum,
-        ffn_gain_sum,
-        router_sum,
-    ) = lax.psum(
-        (
-            attn_gain_grad,
-            query_w_grad,
-            key_w_grad,
-            value_w_grad,
-            query_gain_grad,
-            key_gain_grad,
-            output_w_grad,
-            ffn_gain_grad,
-            router_grad,
-        ),
-        ("dp", "expert"),
-    )
+    weight_parts = [
+        query_w_grad[:, :512],
+        query_w_grad[:, 512:],
+        key_w_grad,
+        value_w_grad,
+        output_w_grad[:, :512],
+        output_w_grad[:, 512:],
+    ]
+    small_parts = [
+        router_grad.reshape(32, 1024),
+        attn_gain_grad.reshape(1, 1024),
+        query_gain_grad.reshape(1, 1024),
+        jnp.pad(key_gain_grad, (0, 512)).reshape(1, 1024),
+        ffn_gain_grad.reshape(1, 1024),
+        jnp.zeros((4, 1024), jnp.float32),
+    ]
+    weight_sums, small_sums = total_everywhere(
+        jnp.concatenate([part.astype(jnp.bfloat16) for part in weight_parts], axis=0),
+        jnp.concatenate(small_parts, axis=0),
+    )
+    weight_sums = weight_sums.astype(jnp.float32)
+    query_w_sum = jnp.concatenate([weight_sums[:1024], weight_sums[1024:2048]], axis=1)
+    key_w_sum, value_w_sum = weight_sums[2048:3072], weight_sums[3072:4096]
+    output_w_sum = jnp.concatenate([weight_sums[4096:5120], weight_sums[5120:]], axis=1)
+    router_sum = small_sums[:32].reshape(1024, 32)
+    attn_gain_sum, query_gain_sum, ffn_gain_sum = small_sums[32], small_sums[33], small_sums[35]
+    key_gain_sum = small_sums[34, :512]
     gate_up_sum, down_w_sum = lax.psum((gate_up_w_grad, down_grad), "dp")
     gate_w_sum = gate_up_sum[:, :, :512].astype(jnp.float32)
     up_w_sum = gate_up_sum[:, :, 512:].astype(jnp.float32)

time: 767 us -> 549 us (0.72)
  waiting for transfers between devices: 321 us -> 89 us
  Pallas kernels: 132 us -> 266 us
  blocking collectives: 88.6 us -> 0 us
  matrix products: 123 us -> 90.9 us
    pallas_call x0 -> x2, Pallas kernels: none -> 135 us  [the longest x1 75 us: total_everywhere(): pl.pallas_call(total_kernel, name='total', out_shape=(jax.ShapeDtypeStruc...]
    psum x1 -> x0, waiting for transfers between devices: 98 us -> none  [body(): lax.psum((attn_gain_grad, query_w_grad, key_w_grad, value_w_grad, query_g...]
    psum x1, waiting for transfers between devices: 80.8 us -> 0.03 us  [body(): gate_up_sum, down_w_sum = lax.psum((gate_up_w_grad, down_grad), 'dp')]
    psum x1 -> x0, blocking collectives: 66.9 us -> none  [body(): lax.psum((attn_gain_grad, query_w_grad, key_w_grad, value_w_grad, query_g...]
    all_gather x2 -> x0, waiting for transfers between devices: 33.9 us -> none  [the longest x1 27.3 us: body(): cot_all = lax.all_gather(cotangent[0], 'expert', axis=0)]
    all_gather x1 -> x0, blocking collectives: 21.7 us -> none  [body(): routes_all = lax.all_gather(routes[0], 'expert', axis=0)]
    slice x0 -> x5, local copies, waits for them, and re-layouts: none -> 15.5 us  [the longest x1 7.93 us: body(): weight_sums[4096:5120]]
    dot_general x16 -> x8, matrix products: 33.1 us -> 18.6 us  [masked_scores(): jnp.einsum('trd,sd->rts', query_pair, key_head, preferred_element_type=jn...]
  transfers between devices with their start and end apart: 6 -> 3, of which waited for: 6 -> 2; matrix products, arithmetic and copies ran while one was open for 11% -> 24% of each run, Pallas kernels for 0% -> 0%
where the time goes in v2:
time: 549 us; the launch traced here: 547 us
  Pallas kernels  266 us (48%)
  matrix products  90.9 us (17%)
  waiting for transfers between devices  89 us (16%)
  local copies, waits for them, and re-layouts  43 us (8%)
  other arithmetic  40.8 us (7%)
  between operations  16.6 us (3%)
    pallas_call x1, Pallas kernels, moe(): pl.pallas_call(moe_kernel, name='moe', out_shape=(jax.ShapeDtypeStruct((F...  131 us
    reduce_scatter x1, waiting for transfers between devices, body(): lax.psum_scatter(mixed_parts.reshape(16 * ROWS, width), 'expert', scatter...  76.3 us
    pallas_call x1, Pallas kernels, total_everywhere(): pl.pallas_call(total_kernel, name='total', out_shape=(jax.ShapeDtypeStruc...  75 us
    pallas_call x1, Pallas kernels, forward(): pl.pallas_call(forward_kernel, name='forward', out_shape=(shape((ROWS, 10...  59.9 us
    dot_general x8, matrix products, masked_scores(): jnp.einsum('trd,sd->rts', query_pair, key_head, preferred_element_type=jn...  18.6 us
    dot_general x8, matrix products, backward_head(): jnp.einsum('rts,trd->sd', probs.astype(jnp.bfloat16), grad_pair, preferre...  18.4 us
    dot_general x8, matrix products, backward_head(): jnp.einsum('rts,trd->sd', score_grad, query_pair, preferred_element_type=...  18.4 us
    dot_general x8, matrix products, backward_head(): jnp.einsum('trd,sd->rts', grad_pair, value_head, preferred_element_type=j...  13.4 us
  transfers between devices with their start and end apart: 3, of which 2 were waited for; matrix products, arithmetic and copies ran while one was open for 24% of the time, Pallas kernels for 0%

profile of v2, /device:TPU:1, one launch (start us, length us, event | category | flops | bytes accessed | tf_op | source)
XLA Modules:
  0.0 546.7 jit_solution(17998506243298188244)
XLA Ops:
  14.7 59.9 %forward.1 = (bf16[256,1024]{1,0:T(8,128)(2,1)}, f32[256,1024]{1,0:T(8,128)}, bf16[1024,256]{1,0:T(8,128)(2,1)}, bf16[8,64,512]{2,1,0:T(8,128)(2,1)}, f32[8,1,51...) custom-call(bf16[256,1024]{1,0:T(8,128)(2,1)} %bitcast.185, ...), custom_call_target="tpu_custom_call" | custom-call | tf_op jit(solution)/shard_map/forward/pallas_call | solution.py:830
  74.6 130.9 %moe.1 = (f32[272,1024]{1,0:T(8,128)}, bf16[16,256,1024]{2,1,0:T(8,128)(2,1)}, bf16[2,1024,1024]{2,1,0:T(8,128)(2,1)}, bf16[2,512,1024]{2,1,0:T(8,128)(2,1)}) custom-call(bf16[256,1024]{1,0:T(8,128)(2,1)} %get-tuple-element.85.ffn, bf16[4352,1024]{1,0:T(8,128)(2,1)} %get-tuple-element.86.cot, bf16[32,1024]{1,0:T(8,128)(2,1)} %bitcast.202, ...), custom_call_target="tpu_custom_call" | custom-call | flops 49999998976 | bytes 40000000 | tf_op jit(solution)/shard_map/moe/pallas_call | solution.py:529
  209.1 3.9 fusion.61
  215.0 3.2 copy.76
  218.2 76.3 %reduce-scatter.3.cloned.1.call-done = bf16[256,1024]{1,0:T(8,128)(2,1)} async-done(((bf16[4096,1024]{1,0:T(8,128)(2,1)}), bf16[256,1024]{1,0:T(8,128)(2,1)}) %reduce-scatter.3.cloned.1.call-update) | async-done | bytes 524304 | tf_op jit(solution)/shard_map/reduce_scatter | solution.py:1149
  294.6 3.1 fusion.38
  301.3 87.0 %while.15 = (s32[]{:T(128)}, f32[8,256,2,64]{1,3,2,0:T(8,128)}, bf16[8,2048,64]{1,2,0:T(8,128)(2,1)}, bf16[8,2048,64]{1,2,0:T(8,128)(2,1)}, bf16[8,2048,64]{1,2,...) while((s32[]{:T(128)}, f32[8,256,2,64]{1,3,2,0:T(8,128)}, ...), condition=%wide.region_9.10_spmd.clone, body=%wide.region_7.0_spmd.clone.sunk | while | flops 681737728 | bytes 34752640 | solution.py:1169
  303.5 2.3 fusion.113
  309.9 2.3 fusion.117
  314.4 2.3 fusion.113
  325.2 2.3 fusion.113
  336.1 2.3 fusion.113
  347.0 2.3 fusion.113
  357.9 2.3 fusion.113
  368.8 2.3 fusion.113
  379.6 2.3 fusion.113
  388.3 4.8 pad_maximum_fusion
  398.2 4.2 convert_element_type.136
  402.4 4.7 slice_convert_fusion
  416.4 12.1 %reduce-scatter.5.cloned.1.call-done = bf16[256,1024]{0,1:T(8,128)(2,1)} async-done(((bf16[2048,1024]{0,1:T(8,128)(2,1)}), bf16[256,1024]{0,1:T(8,128)(2,1)}) %reduce-scatter.5.cloned.1.call-update) | async-done | bytes 524304 | tf_op jit(solution)/shard_map/reduce_scatter | solution.py:32
  443.1 75.0 %total.1 = (bf16[6144,512]{1,0:T(8,128)(2,1)}, f32[40,1024]{1,0:T(8,128)}) custom-call(bf16[6144,512]{1,0:T(8,128)(2,1)} %slice_dynamic-update-slice_fusion.parts, f32[40,1024]{1,0:T(8,128)} %concatenate.17.small), custom_call_target="tpu_custom_call" | custom-call | tf_op jit(solution)/shard_map/total/pallas_call | solution.py:1061
  521.8 7.9 %fusion.60 = (f32[1024,512]{1,0:T(8,128)}, f32[1024,512]{1,0:T(8,128)}, f32[1024,512]{1,0:T(8,128)}, f32[1024,512]{1,0:T(8,128)}, f32[1024,512]{1,0:T(8,128)}, /*index=5*/f32[1024,512]{1,0:T(8,128)}) fusion(bf16[6144,512]{1,0:T(8,128)(2,1)} %get-tuple-element.100), kind=kLoop, calls=%fused_computation.131 | loop fusion | bytes 25165824 | tf_op jit(solution)/shard_map/slice | solution.py:1224
  532.5 4.3 pad_maximum_fusion.1
  536.8 2.4 pad_maximum_fusion.2
  (198 shorter events, 116.1 us)
Async XLA Ops:
  8.0 286.5 %reduce-scatter.3.cloned.1.call-start = ((), (), s32[]{:S(2)}) async-start(), calls=%async_computation.2 | async-start | bytes 8912896 | tf_op jit(solution)/shard_map/reduce_scatter | solution.py:1149
  205.5 192.7 %all-reduce.8.cloned.1.call-start = ((), (), s32[]{:S(2)}) async-start(), calls=%async_computation.4 | async-start | bytes 12582912 | tf_op jit(solution)/shard_map/psum | solution.py:1228
  205.6 1.7 copy-start.15
  205.6 1.7 copy-start.23
  206.1 222.4 %reduce-scatter.5.cloned.1.call-start = ((), (), s32[]{:S(2)}) async-start(), calls=%async_computation.3 | async-start | bytes 4718592 | tf_op jit(solution)/shard_map/reduce_scatter | solution.py:32
  213.3 1.7 copy-start.25
  294.6 3.1 copy-start.5
  393.2 4.3 copy-start.10
  393.8 3.8 copy-start.2
  393.8 3.9 copy-start
  398.2 4.2 copy-start.11
  402.4 4.7 copy-start.17
  411.7 2.2 copy-start.6
  413.9 1.7 copy-start.18
  432.5 3.0 copy-start.12
  432.5 3.0 copy-start.14
  434.0 1.9 copy-start.22
  435.4 2.1 copy-start.19
  439.0 2.2 copy-start.3
  439.0 2.2 copy-start.13
  521.8 8.9 %copy-start.4 = (bf16[1,256,1024]{2,1,0:T(8,128)(2,1)S(1)}, bf16[1,256,1024]{2,1,0:T(8,128)(2,1)}, u32[]{:S(2)}) copy-start(bf16[1,256,1024]{2,1,0:T(8,128)(2,1)} %param.18) | copy-start | bytes 1572868
  530.8 1.8 copy-start.9
  532.5 4.3 copy-start.7
  532.5 4.3 copy-start.8
  (9 other events, 9.3 us)
Sparse Core Ops, SparseCore 0:
  205.6 88.8 reduce-scatter.2
Sparse Core Ops, SparseCore 1:
  208.5 89.3 all-reduce.7
  393.3 35.2 reduce-scatter.4

commit v3 on v2

--- a/solution.py
+++ b/solution.py
@@ -16,36 +16,6 @@
 
 
 epsilon = 1e-06
-HIGHEST = lax.Precision.HIGHEST
-
-
-def in_one_piece(arrays, axis, dim, along):
-    widths = [a.shape[along] for a in arrays]
-    both = jnp.concatenate(arrays, axis=along)
-    whole = lax.all_gather(both, axis, axis=dim, tiled=True)
-    return tuple(jnp.split(whole, [sum(widths[:k]) for k in range(1, len(widths))], axis=along))
-
-
-def sent_together(arrays, axis, dim, along):
-    widths = [a.shape[along] for a in arrays]
-    both = jnp.concatenate(arrays, axis=along)
-    whole = lax.psum_scatter(both, axis, scatter_dimension=dim, tiled=True)
-    return tuple(jnp.split(whole, [sum(widths[:k]) for k in range(1, len(widths))], axis=along))
-
-
-def together(arrays, axis):
-    vector, at, finished = (jnp.concatenate([a.reshape(-1) for a in arrays]), 0, [])
-    so_far = lax.psum(vector, axis)
-    for a in arrays:
-        finished.append(so_far[at : at + a.size].reshape(a.shape))
-        at += a.size
-    return tuple(finished)
-
-
-def norm_rows(values, norm_gain):
-    return (
-        values * lax.rsqrt(jnp.mean(values * values, axis=-1, keepdims=True) + epsilon) * norm_gain
-    )
 
 
 def rope_tables(positions):
@@ -53,74 +23,6 @@
     inverse = jnp.exp(steps_half * (-2.0 * math.log(10000.0) / HEAD_DIM))
     angles = positions.astype(jnp.float32)[:, None] * inverse[None, :]
     return (jnp.cos(angles), jnp.sin(angles))
-
-
-def rotate(values, cosine, sine_table):
-    count_rows = values.shape[0]
-    heads_view = values.reshape(count_rows, -1, HEAD_DIM)
-    front_half = heads_view[..., : HEAD_DIM // 2]
-    back_half = heads_view[..., HEAD_DIM // 2 :]
-    cosine_rows = cosine[:, None, :]
-    sine_rows = sine_table[:, None, :]
-    turned = jnp.concatenate(
-        [
-            front_half * cosine_rows - back_half * sine_rows,
-            back_half * cosine_rows + front_half * sine_rows,
-        ],
-        axis=-1,
-    )
-    return turned.reshape(count_rows, -1)
-
-
-def contract_rows(left, right):
-    return lax.dot_general(
-        left, right, (((0,), (0,)), ((), ())), preferred_element_type=jnp.float32
-    )
-
-
-def times_transposed(left, right):
-    return lax.dot_general(
-        left, right, (((1,), (1,)), ((), ())), preferred_element_type=jnp.float32
-    )
-
-
-def masked_scores(query_pair, key_head, key_valid):
-    scores = jnp.einsum(
-        "trd,sd->rts", query_pair, key_head, preferred_element_type=jnp.float32
-    ) * HEAD_DIM ** (-0.5)
-    return jnp.where(key_valid[None], scores, -1e30)
-
-
-def forward_head(operands, key_valid):
-    query_pair, key_head, value_head = operands
-    scores = masked_scores(query_pair, key_head, key_valid)
-    top_score = jnp.max(scores, axis=-1, keepdims=True)
-    log_total = top_score + jnp.log(jnp.sum(jnp.exp(scores - top_score), axis=-1, keepdims=True))
-    probs = jnp.exp(scores - log_total).astype(jnp.bfloat16)
-    mixed = jnp.einsum("rts,sd->trd", probs, value_head, preferred_element_type=jnp.float32)
-    return (mixed, log_total[..., 0])
-
-
-def backward_head(operands, key_valid):
-    query_pair, key_head, value_head, grad_pair, log_total = operands
-    scores = masked_scores(query_pair, key_head, key_valid)
-    probs = jnp.exp(scores - log_total[..., None])
-    grad_probs = jnp.einsum(
-        "trd,sd->rts", grad_pair, value_head, preferred_element_type=jnp.float32
-    )
-    score_grad = (
-        probs * (grad_probs - jnp.sum(probs * grad_probs, axis=-1, keepdims=True))
-    ).astype(jnp.bfloat16)
-    query_grad = jnp.einsum(
-        "rts,sd->trd", score_grad, key_head, preferred_element_type=jnp.float32
-    ) * HEAD_DIM ** (-0.5)
-    key_grad = jnp.einsum(
-        "rts,trd->sd", score_grad, query_pair, preferred_element_type=jnp.float32
-    ) * HEAD_DIM ** (-0.5)
-    value_grad = jnp.einsum(
-        "rts,trd->sd", probs.astype(jnp.bfloat16), grad_pair, preferred_element_type=jnp.float32
-    )
-    return (query_grad, key_grad, value_grad)
 
 
 RING = 4
@@ -933,16 +835,18 @@
             copy.start()
 
     def add(self, target, start, size, lands):
-        @pl.loop(0, size // 16)
+        step = 64 if size % 64 == 0 else 16
+
+        @pl.loop(0, size // step)
         def _(k):
-            here = pl.ds(pl.multiple_of(start + k * 16, 16), 16)
+            here = pl.ds(pl.multiple_of(start + k * step, 16), step)
             total = self.buffer[here].astype(jnp.float32)
             for land in lands:
-                total = total + self.landing[pl.ds(pl.multiple_of(land + k * 16, 16), 16)].astype(jnp.float32)
+                total = total + self.landing[pl.ds(pl.multiple_of(land + k * step, 16), step)].astype(jnp.float32)
             if target is None:
                 self.buffer[here] = total.astype(jnp.bfloat16)
             else:
-                target[pl.ds(pl.multiple_of(k * 16, 16), 16)] = total.astype(jnp.bfloat16)
+                target[pl.ds(pl.multiple_of(k * step, 16), step)] = total.astype(jnp.bfloat16)
 
     def finish(self, stage):
         for copy in self.copies(stage):
@@ -1026,13 +930,12 @@
     values[0] = small[...]
     load.wait()
     pl.semaphore_wait(barrier, len(peers))
-    half = whole.shape[0] // 2
-    rows = half // 3
-    room = rows + 3 * (rows // 4) + 6 * (rows // 16)
-    streams = [
-        Total(here, device, held, whole, landing, work, send, recv, s, half, s * rows, rows, s * room, ORDERS[s])
-        for s in range(3)
-    ]
+    half, base, streams = whole.shape[0] // 2, 0, []
+    for s, (start, rows) in enumerate(EARLY):
+        streams.append(
+            Total(here, device, held, whole, landing, work, send, recv, s, half, start, rows, base, ORDERS[s])
+        )
+        base += rows + 3 * (rows // 4) + 6 * (rows // 16)
     few = Small(device, values, small_landing, small_send, small_recv)
     for one in streams:
         one.begin(0)
@@ -1056,8 +959,7 @@
     vmem, hbm = pl.BlockSpec(memory_space=pltpu.VMEM), pl.BlockSpec(memory_space=pl.ANY)
     low = jnp.bfloat16
     rows, width = parts.shape
-    third = rows // 6
-    room = third + 3 * (third // 4) + 6 * (third // 16)
+    room = sum(count + 3 * (count // 4) + 6 * (count // 16) for _, count in EARLY)
     return pl.pallas_call(
         total_kernel,
         name="total",
@@ -1069,8 +971,8 @@
         out_specs=(vmem, vmem),
         scratch_shapes=[
             pltpu.VMEM((rows, width), low),
-            pltpu.VMEM((3 * room, width), low),
-            pltpu.VMEM((3, third // 16, width), low),
+            pltpu.VMEM((room, width), low),
+            pltpu.VMEM((3, 48, width), low),
             pltpu.VMEM((5, *small.shape), jnp.float32),
             pltpu.VMEM((10, *small.shape), jnp.float32),
             pltpu.SemaphoreType.DMA((3, 17)),
@@ -1083,6 +985,407 @@
             collective_id=2, has_side_effects=True, vmem_limit_bytes=56 * 2**20
         ),
     )(parts, small)
+
+
+class Line:
+    def __init__(self, here, device):
+        self.here, self.device = here, device
+
+    def along(self, axis, other, step):
+        return (self.here["x"] + step + RING) % RING
+
+    def near(self, axis, step):
+        return self.device("x", step)
+
+
+def rms_back(values, gain, grad):
+    scale = rms_scale(values)
+    lifted = gain * grad
+    inner = jnp.mean(values * lifted, axis=-1, keepdims=True)
+    return scale * lifted - values * (scale * scale * scale) * inner, jnp.sum(
+        grad * values * scale, axis=0, keepdims=True
+    )
+
+
+def turned_back(grads, cosine, sine):
+    front, back = grads[: HEAD_DIM // 2], grads[HEAD_DIM // 2 :]
+    return jnp.concatenate([front * cosine + back * sine, back * cosine - front * sine], axis=0)
+
+
+EARLY = ((0, 768), (768, 768), (1536, 512))
+
+
+def backward_kernel(
+    returned, hidden, ffn_in, cot, tokens, normed, query_raw, key_raw, mixed_t, queries, log_total,
+    routes_t, length, cosine, sine, attn_gain, query_gain, key_gain, ffn_gain, router_rows,
+    mixed_parts, kv_all, w_query, w_key, w_value, w_output,
+    mixed_out, token_grad, late, early_small, late_small, output_sum,
+    sums, rows, wq, wk, wv, wo, kv, hidden_grad, result, branch, grads, delta, query_grad, turned,
+    for_mate, from_mate, kv_sums, kv_rows, kv_grad, raw_grad, key_low, value_low,
+    held, final, landing, work, values, small_rows,
+    rs_send, rs_recv, mate_send, mate_recv, kv_send, kv_recv, ar_send, ar_recv, small_send, small_recv, load_sem, stage_sem,
+):
+    torus = Torus()
+    here, device = everywhere()
+    me = here["x"] * 2 + here["core"]
+    barrier = pltpu.get_barrier_semaphore()
+    peers = [device("core", 1)] + [device(axis, d) for axis in "xyz" for d in (1, 2, 3)]
+    for peer in peers:
+        pl.semaphore_signal(barrier, inc=1, device_id=peer, device_id_type=MESH)
+    loads = [
+        pltpu.make_async_copy(source, target, load_sem.at[n])
+        for n, (source, target) in enumerate(
+            ((w_output, wo), (mixed_parts, sums), (kv_all, kv), (w_query, wq), (w_key, wk), (w_value, wv))
+        )
+    ]
+    for load in loads:
+        load.start()
+
+    expert_rows = lax.broadcasted_iota(jnp.int32, (EXPERTS, ROWS), 0)
+    member = jnp.zeros((EXPERTS, ROWS), jnp.float32)
+    for k in range(TOPK):
+        member = member + jnp.where(expert_rows == routes_t[pl.ds(k, 1), :], 1.0, 0.0)
+    named = member > 0.5
+    logits = jnp.where(named, dot_nt(router_rows[...], ffn_in[...]), -1e30)
+    weight = jnp.where(named, jnp.exp(logits - jnp.max(logits, axis=0, keepdims=True)), 0.0)
+    gates = weight / jnp.sum(weight, axis=0, keepdims=True)
+    gate_grad = jnp.concatenate([returned[:8, q * ROWS : (q + 1) * ROWS] for q in range(4)], axis=0)
+    logit_grad = (gates * (gate_grad - jnp.sum(gates * gate_grad, axis=0, keepdims=True))).astype(jnp.bfloat16)
+    result[...] = dot_tn(logit_grad, router_rows[...])
+    values[0, :EXPERTS] = dot_nn(logit_grad, ffn_in[...])
+
+    def ffn_part(n, gain_grad):
+        at = pl.ds(pl.multiple_of(n * 64, 64), 64)
+        grad = result[at] + returned[pl.ds(pl.multiple_of(n * 64 + EXTRA, 16), 64)]
+        part, more = rms_back(hidden[at], ffn_gain[...].astype(jnp.float32), grad)
+        part = part + cot[at].astype(jnp.float32)
+        hidden_grad[at] = part
+        branch[at] = part.astype(jnp.bfloat16)
+        return gain_grad + more
+
+    gain_grad = lax.fori_loop(0, 4, ffn_part, jnp.zeros((1, 1024), jnp.float32))
+    values[0, EXPERTS:] = jnp.concatenate([gain_grad, jnp.zeros((7, 1024), jnp.float32)], axis=0)
+
+    loads[0].wait()
+    turned[...] = dot_nt(wo[...], branch[...])
+
+    @pl.loop(0, KV_HEADS)
+    def _(j):
+        for r in range(2):
+            at = pl.ds(pl.multiple_of(j * 128 + r * 64, 64), 64)
+            low = turned[at].astype(jnp.bfloat16)
+            grads[j, :, r * ROWS : (r + 1) * ROWS] = low
+            delta[j, :, r * ROWS : (r + 1) * ROWS] = jnp.sum(
+                low.astype(jnp.float32) * mixed_t[at].astype(jnp.float32), axis=0, keepdims=True
+            )
+        query_grad[j] = jnp.zeros((HEAD_DIM, 2 * ROWS), jnp.float32)
+
+    @pl.loop(0, 4)
+    def _(n):
+        at = pl.ds(pl.multiple_of(n * 256, 256), 256)
+        part = dot_nn(mixed_t[at], branch[...]).astype(jnp.bfloat16)
+        for q in range(4):
+            held[pl.ds(pl.multiple_of(q * 1024 + n * 256, 256), 256)] = part[:, q * 256 : (q + 1) * 256]
+
+    for load in loads[1:]:
+        load.wait()
+    pl.semaphore_wait(barrier, len(peers))
+
+    half, base, early = 2048, 0, []
+    for s, (start, count) in enumerate(EARLY):
+        early.append(
+            Total(here, device, held, final, landing, work, ar_send, ar_recv, s, half, start, count, base, ORDERS[s])
+        )
+        base += count + 3 * (count // 4) + 6 * (count // 16)
+    few = Small(device, values, small_rows, small_send, small_recv)
+    order = (2, 1, -1, 0)
+    leads = []
+    for n, d in enumerate(order):
+        leads.append(Scatter(torus, sums, rows, rs_send, rs_recv, n, n * 384, "z", d, 0, 64, 64))
+        leads.append(Scatter(torus, sums, rows, rs_send, rs_recv, 4 + n, (5 + n) * 384, "y", d, 128, 64, 64))
+    lasts = [
+        Scatter(torus, sums, rows, rs_send, rs_recv, 8, 4 * 384, "y", 0, 0, 64, 64),
+        Scatter(torus, sums, rows, rs_send, rs_recv, 9, 9 * 384, "z", 0, 128, 64, 64),
+    ]
+    ring = Scatter(Line(here, device), kv_sums, kv_rows, kv_send, kv_recv, 0, 0, "x", 0, 0, 512, 512)
+
+    for one in early:
+        one.begin(0)
+    few.begin(0)
+    for one in leads:
+        one.first()
+
+    def early_step(stage):
+        for one in early:
+            one.finish(stage)
+            if stage < 6:
+                one.begin(stage + 1)
+        if stage < 4:
+            few.finish(stage)
+            if stage < 3:
+                few.begin(stage + 1)
+
+    def mate_copy(turn, at):
+        return pltpu.make_async_remote_copy(
+            src_ref=for_mate.at[at],
+            dst_ref=from_mate.at[at],
+            send_sem=mate_send.at[turn],
+            recv_sem=mate_recv.at[turn],
+            device_id=device("core", 1),
+            device_id_type=MESH,
+        )
+
+    key_at = lax.broadcasted_iota(jnp.int32, (ROWS, 2 * ROWS), 0)
+    query_at = lax.broadcasted_iota(jnp.int32, (ROWS, 2 * ROWS), 1) % ROWS
+    valid = (key_at <= query_at) & (key_at + me * ROWS < length[...])
+
+    def block_grads(block, target, at, masked):
+        @pl.loop(0, KV_HEADS)
+        def _(j):
+            key_lines = pl.ds(pl.multiple_of(j * 64, 64), 64)
+            value_lines = pl.ds(pl.multiple_of(512 + j * 64, 64), 64)
+            key_head, value_head = kv[block, key_lines], kv[block, value_lines]
+            probs = jnp.exp(dot_tn(key_head, queries[j]) - log_total[j])
+            if masked:
+                probs = jnp.where(valid, probs, 0.0)
+            probs_grad = dot_tn(value_head, grads[j])
+            score_grad = (probs * (probs_grad - delta[j])).astype(jnp.bfloat16)
+            target[at, key_lines] = dot_nt(queries[j], score_grad).astype(jnp.bfloat16)
+            target[at, value_lines] = dot_nt(grads[j], probs.astype(jnp.bfloat16)).astype(jnp.bfloat16)
+            query_grad[j] += dot_nn(key_head, score_grad)
+
+    def from_other(turn, at):
+        mate_copy(turn, at).wait_recv()
+
+        @pl.loop(0, 16)
+        def _(n):
+            lines = pl.ds(pl.multiple_of(n * 64, 64), 64)
+            total = kv_sums[at, lines].astype(jnp.float32) + from_mate[at, lines].astype(jnp.float32)
+            kv_sums[at, lines] = total.astype(jnp.bfloat16)
+
+    def turn_x(turn):
+        offset = (1 - turn % 2) * (2 + turn // 2) + (turn % 2) * (1 - turn // 2)
+        return (here["x"] + offset + RING) % RING
+
+    @pl.loop(0, 4)
+    def _(turn):
+        @pl.when(turn == 1)
+        def _():
+            early_step(0)
+            for one in leads:
+                one.second()
+
+        @pl.when(turn == 2)
+        def _():
+            early_step(2)
+
+        @pl.when(turn == 3)
+        def _():
+            early_step(4)
+            for one in leads[:2]:
+                one.third()
+            for one in lasts:
+                one.first()
+
+        at = turn_x(turn)
+        other = at * 2 + 1 - here["core"]
+
+        @pl.when(other < me)
+        def _():
+            block_grads(other, for_mate, at, False)
+
+        @pl.when(other >= me)
+        def _():
+            for_mate[at] = jnp.zeros((1024, ROWS), jnp.bfloat16)
+
+        mate_copy(turn, at).start()
+
+        @pl.when(turn == 1)
+        def _():
+            early_step(1)
+
+        @pl.when(turn == 2)
+        def _():
+            early_step(3)
+
+        @pl.when(turn == 3)
+        def _():
+            early_step(5)
+            for one in leads[2:]:
+                one.third()
+            for one in lasts:
+                one.second()
+
+        own = at * 2 + here["core"]
+
+        @pl.when(own < me)
+        def _():
+            block_grads(own, kv_sums, at, False)
+
+        @pl.when(own > me)
+        def _():
+            kv_sums[at] = jnp.zeros((1024, ROWS), jnp.bfloat16)
+
+        @pl.when(own == me)
+        def _():
+            block_grads(own, kv_sums, at, True)
+
+        from_other(turn, at)
+
+        @pl.when(turn == 0)
+        def _():
+            ring.first()
+
+        @pl.when(turn == 2)
+        def _():
+            ring.second()
+
+    @pl.loop(0, KV_HEADS)
+    def _(j):
+        for r in range(2):
+            head = query_grad[j, :, r * ROWS : (r + 1) * ROWS] * HEAD_DIM**-0.5
+            turned[pl.ds(pl.multiple_of(j * 128 + r * 64, 64), 64)] = turned_back(head, cosine[...], sine[...])
+
+    result[...] = turned[...].T
+
+    def query_part(n, gain_grad):
+        at = pl.ds(pl.multiple_of(n * 64, 64), 64)
+        part, more = rms_back(query_raw[at], query_gain[...].astype(jnp.float32), result[at])
+        raw_grad[at] = part.astype(jnp.bfloat16)
+        return gain_grad + more
+
+    query_gain_grad = lax.fori_loop(0, 4, query_part, jnp.zeros((1, 1024), jnp.float32))
+
+    @pl.loop(0, 4)
+    def _(n):
+        columns = pl.ds(pl.multiple_of(n * 256, 256), 256)
+        part = dot_tn(normed[:, columns], raw_grad[...]).astype(jnp.bfloat16)
+        for q in range(2):
+            late[pl.ds(pl.multiple_of(q * 1024 + n * 256, 256), 256)] = part[:, q * 512 : (q + 1) * 512]
+
+    result[...] = dot_nt(raw_grad[...], wq[...])
+    early_step(6)
+    ring.third(kv_grad)
+
+    for j in range(KV_HEADS):
+        turned[j * 64 : j * 64 + 64] = turned_back(kv_grad[j * 64 : j * 64 + 64], cosine[...], sine[...])
+    part, key_gain_grad = rms_back(key_raw[...], key_gain[...].astype(jnp.float32), turned[:512].T)
+    key_low[...] = part.astype(jnp.bfloat16)
+    value_low[...] = kv_grad[512:].T.astype(jnp.bfloat16)
+
+    @pl.loop(0, 4)
+    def _(n):
+        columns = pl.ds(pl.multiple_of(n * 256, 256), 256)
+        here_rows = normed[:, columns]
+        late[pl.ds(pl.multiple_of(2048 + n * 256, 256), 256)] = dot_tn(here_rows, key_low[...]).astype(jnp.bfloat16)
+        late[pl.ds(pl.multiple_of(3072 + n * 256, 256), 256)] = dot_tn(here_rows, value_low[...]).astype(jnp.bfloat16)
+
+    result[...] += dot_nt(key_low[...], wk[...]) + dot_nt(value_low[...], wv[...])
+
+    def token_part(n, gain_grad):
+        at = pl.ds(pl.multiple_of(n * 64, 64), 64)
+        part, more = rms_back(tokens[at].astype(jnp.float32), attn_gain[...].astype(jnp.float32), result[at])
+        token_grad[at] = (hidden_grad[at] + part).astype(jnp.bfloat16)
+        return gain_grad + more
+
+    attn_gain_grad = lax.fori_loop(0, 4, token_part, jnp.zeros((1, 1024), jnp.float32))
+    key_wide = jnp.concatenate([key_gain_grad, jnp.zeros((1, 512), jnp.float32)], axis=1)
+    late_small[...] = jnp.concatenate(
+        [attn_gain_grad, query_gain_grad, key_wide, jnp.zeros((5, 1024), jnp.float32)], axis=0
+    )
+
+    stages = (turned, kv_grad)
+    for q in range(4):
+        slot = q % 2
+        out = pltpu.make_async_copy(stages[slot], output_sum.at[:, pl.ds(q * 256, 256)], stage_sem.at[slot])
+        if q >= 2:
+            out.wait()
+        stages[slot][...] = final[q * 1024 : (q + 1) * 1024].astype(jnp.float32)
+        out.start()
+    early_small[...] = values[4]
+
+    for one in lasts:
+        one.third(result)
+
+    @pl.loop(0, 4)
+    def _(n):
+        at = pl.ds(pl.multiple_of(n * 64, 64), 64)
+        mixed_out[at] = (hidden[at] + result[at]).astype(jnp.bfloat16)
+
+    for slot in range(2):
+        pltpu.make_async_copy(stages[slot], output_sum.at[:, pl.ds(0, 256)], stage_sem.at[slot]).wait()
+    for one in [*leads, *lasts, ring, *early, few]:
+        one.drain()
+    for turn in range(4):
+        mate_copy(turn, 0).wait_send()
+
+
+def backward(smalls, larges):
+    vmem, hbm = pl.BlockSpec(memory_space=pltpu.VMEM), pl.BlockSpec(memory_space=pl.ANY)
+    low, wide = jnp.bfloat16, jnp.float32
+    shape = jax.ShapeDtypeStruct
+    dma = pltpu.SemaphoreType.DMA
+    room = sum(count + 3 * (count // 4) + 6 * (count // 16) for _, count in EARLY)
+    return pl.pallas_call(
+        backward_kernel,
+        name="backward",
+        out_shape=(
+            shape((ROWS, 1024), low),
+            shape((ROWS, 1024), low),
+            shape((4096, 512), low),
+            shape((40, 1024), wide),
+            shape((8, 1024), wide),
+            shape((1024, 1024), wide),
+        ),
+        in_specs=[vmem] * len(smalls) + [hbm] * len(larges),
+        out_specs=(vmem,) * 5 + (hbm,),
+        scratch_shapes=[
+            pltpu.VMEM((16, ROWS, 1024), low),
+            pltpu.VMEM((10 * 384, 1024), low),
+            pltpu.VMEM((1024, 1024), low),
+            pltpu.VMEM((1024, 512), low),
+            pltpu.VMEM((1024, 512), low),
+            pltpu.VMEM((1024, 1024), low),
+            pltpu.VMEM((8, 1024, ROWS), low),
+            pltpu.VMEM((ROWS, 1024), wide),
+            pltpu.VMEM((ROWS, 1024), wide),
+            pltpu.VMEM((ROWS, 1024), low),
+            pltpu.VMEM((KV_HEADS, HEAD_DIM, 2 * ROWS), low),
+            pltpu.VMEM((KV_HEADS, 1, 2 * ROWS), wide),
+            pltpu.VMEM((KV_HEADS, HEAD_DIM, 2 * ROWS), wide),
+            pltpu.VMEM((1024, ROWS), wide),
+            pltpu.VMEM((4, 1024, ROWS), low),
+            pltpu.VMEM((4, 1024, ROWS), low),
+            pltpu.VMEM((4, 1024, ROWS), low),
+            pltpu.VMEM((3072, ROWS), low),
+            pltpu.VMEM((1024, ROWS), wide),
+            pltpu.VMEM((ROWS, 1024), low),
+            pltpu.VMEM((ROWS, 512), low),
+            pltpu.VMEM((ROWS, 512), low),
+            pltpu.VMEM((4096, 256), low),
+            pltpu.VMEM((4096, 256), low),
+            pltpu.VMEM((room, 256), low),
+            pltpu.VMEM((3, 48, 256), low),
+            pltpu.VMEM((5, 40, 1024), wide),
+            pltpu.VMEM((10, 40, 1024), wide),
+            dma((10, 4)),
+            dma((10, 4)),
+            dma((4,)),
+            dma((4,)),
+            dma((1, 4)),
+            dma((1, 4)),
+            dma((3, 17)),
+            dma((3, 17)),
+            dma((10,)),
+            dma((10,)),
+            dma((6,)),
+            dma((2,)),
+        ],
+        compiler_params=pltpu.CompilerParams(
+            collective_id=4, has_side_effects=True, vmem_limit_bytes=63 * 2**20
+        ),
+        cost_estimate=pl.CostEstimate(flops=100 * 10**9, bytes_accessed=60 * 10**6, transcendentals=8 * 10**6),
+    )(*smalls, *larges)
 
 
 def body(
@@ -1103,129 +1406,32 @@
     w_up,
     w_down,
 ):
-    token_rows = tokens[0].astype(jnp.float32)
-    tok_count = token_rows.shape[0]
-    width = token_rows.shape[1]
-    kv_width = w_key.shape[1]
-    seq_total = tok_count * lax.axis_size("dp")
-    query_pos = lax.axis_index("dp") * tok_count + jnp.arange(tok_count, dtype=jnp.int32)
-    key_pos = jnp.arange(seq_total, dtype=jnp.int32)
-    key_valid = (key_pos[None, :] <= query_pos[:, None]) & (key_pos[None, :] < lengths[0])
+    query_pos = lax.axis_index("dp") * ROWS + jnp.arange(ROWS, dtype=jnp.int32)
     cosine, sine_table = rope_tables(query_pos)
-    ffn_in, hidden_res, mixed_t, queries_t, log_totals, normed, query_raw, key_raw, kv_all, cot_all = forward(
-        tokens[0],
-        cotangent[0],
-        routes[0].T,
-        lengths.reshape(1, 1),
-        cosine.T,
-        sine_table.T,
-        [gain.reshape(1, -1) for gain in (attn_gain, query_gain, key_gain, ffn_gain)],
-        (w_query, w_key, w_value, w_output),
+    cosine, sine_table = cosine.T, sine_table.T
+    routes_t, length = routes[0].T, lengths.reshape(1, 1)
+    gains = [gain.reshape(1, -1) for gain in (attn_gain, query_gain, key_gain, ffn_gain)]
+    weights = (w_query, w_key, w_value, w_output)
+    router_rows = w_router.T
+    ffn_in, hidden, mixed_t, queries, log_total, normed, query_raw, key_raw, kv_all, cot_all = forward(
+        tokens[0], cotangent[0], routes_t, length, cosine, sine_table, gains, weights
     )
-    _, attn_pull = jax.vjp(norm_rows, token_rows, attn_gain.astype(jnp.float32))
-
-    def post_norm(query_in, key_in, gain_query, gain_key):
-        return (
-            rotate(norm_rows(query_in, gain_query), cosine, sine_table),
-            rotate(norm_rows(key_in, gain_key), cosine, sine_table),
-        )
-
-    _, post_pull = jax.vjp(
-        post_norm, query_raw, key_raw, query_gain.astype(jnp.float32), key_gain.astype(jnp.float32)
+    returned, mixed_parts, gate_up_w_grad, down_grad = moe(ffn_in, cot_all, router_rows, w_gate, w_up, w_down)
+    gate_up_sum, down_w_sum = lax.psum((gate_up_w_grad, down_grad), "dp")
+    mixed_out, token_grad, late, early_small, late_small, output_w_sum = backward(
+        (
+            returned, hidden, ffn_in, cotangent[0], tokens[0], normed, query_raw, key_raw, mixed_t, queries,
+            log_total, routes_t, length, cosine, sine_table, *gains, router_rows,
+        ),
+        (mixed_parts, kv_all, *weights),
     )
-    query_groups = queries_t.reshape(KV_HEADS, HEAD_DIM, 2, tok_count).transpose(0, 3, 2, 1) * 8
-    key_groups = kv_all[:, :512].reshape(8, KV_HEADS, HEAD_DIM, ROWS).transpose(1, 0, 3, 2).reshape(KV_HEADS, seq_total, HEAD_DIM)
-    value_groups = kv_all[:, 512:].reshape(8, KV_HEADS, HEAD_DIM, ROWS).transpose(1, 0, 3, 2).reshape(KV_HEADS, seq_total, HEAD_DIM)
-    log_totals = log_totals.reshape(KV_HEADS, 2, tok_count)
-    attended = mixed_t.T
-    _, ffn_pull = jax.vjp(norm_rows, hidden_res, ffn_gain.astype(jnp.float32))
-    logits = jnp.dot(ffn_in, w_router, preferred_element_type=jnp.float32)
-    own_routes = (routes[0][:, :, None] == jnp.arange(EXPERTS, dtype=jnp.int32)).any(axis=1)
-    gates = jax.nn.softmax(jnp.where(own_routes, logits, -1e30), axis=-1)
-    gates = jnp.where(own_routes, gates, 0.0)
-    returned, mixed_parts, gate_up_w_grad, down_grad = moe(
-        ffn_in, cot_all, w_router.T, w_gate, w_up, w_down
-    )
-    mixed_sum = lax.psum_scatter(
-        mixed_parts.reshape(16 * ROWS, width), "expert", scatter_dimension=0, tiled=True
-    )
-    mixed_out = (hidden_res + mixed_sum.astype(jnp.float32)).astype(jnp.bfloat16)
-    grad_out = cotangent[0].astype(jnp.float32)
-    gate_grad = returned[:8].reshape(8, 4, ROWS).transpose(1, 0, 2).reshape(EXPERTS, ROWS).T
-    pair_sum = returned[EXTRA:]
-    logit_grad = (
-        gates * (gate_grad - jnp.sum(gates * gate_grad, axis=-1, keepdims=True))
-    ).astype(jnp.bfloat16)
-    router_grad = contract_rows(ffn_in, logit_grad)
-    ffn_in_grad = times_transposed(logit_grad, w_router) + pair_sum
-    res_part, ffn_gain_grad = ffn_pull(ffn_in_grad)
-    hidden_grad = grad_out + res_part
-    branch_grad = hidden_grad.astype(jnp.bfloat16)
-    output_w_grad = contract_rows(attended, branch_grad)
-    attended_grad = times_transposed(branch_grad, w_output).astype(jnp.bfloat16)
-    grad_groups = attended_grad.reshape(tok_count, KV_HEADS, HEADS // KV_HEADS, HEAD_DIM).transpose(
-        1, 0, 2, 3
-    )
-    query_grad_heads, key_grad_heads, value_grad_heads = lax.map(
-        lambda operands: backward_head(operands, key_valid),
-        (query_groups, key_groups, value_groups, grad_groups, log_totals),
-    )
-    query_grad = query_grad_heads.transpose(1, 0, 2, 3).reshape(tok_count, width)
-    key_grad_full = key_grad_heads.transpose(1, 0, 2).reshape(seq_total, kv_width)
-    value_grad_full = value_grad_heads.transpose(1, 0, 2).reshape(seq_total, kv_width)
-    key_grad, value_grad = tuple(
-        (
-            part.astype(jnp.float32)
-            for part in sent_together(
-                (key_grad_full.astype(jnp.bfloat16), value_grad_full.astype(jnp.bfloat16)),
-                "dp",
-                0,
-                1,
-            )
-        )
-    )
-    query_raw_grad, key_raw_grad, query_gain_grad, key_gain_grad = post_pull((query_grad, key_grad))
-    query_raw_low = query_raw_grad.astype(jnp.bfloat16)
-    key_raw_low = key_raw_grad.astype(jnp.bfloat16)
-    value_raw_low = value_grad.astype(jnp.bfloat16)
-    query_w_grad = contract_rows(normed, query_raw_low)
-    key_w_grad = contract_rows(normed, key_raw_low)
-    value_w_grad = contract_rows(normed, value_raw_low)
-    normed_grad = (
-        times_transposed(query_raw_low, w_query)
-        + times_transposed(key_raw_low, w_key)
-        + times_transposed(value_raw_low, w_value)
-    )
-    token_part, attn_gain_grad = attn_pull(normed_grad)
-    token_grad = (hidden_grad + token_part).astype(jnp.bfloat16)
-    weight_parts = [
-        query_w_grad[:, :512],
-        query_w_grad[:, 512:],
-        key_w_grad,
-        value_w_grad,
-        output_w_grad[:, :512],
-        output_w_grad[:, 512:],
-    ]
-    small_parts = [
-        router_grad.reshape(32, 1024),
-        attn_gain_grad.reshape(1, 1024),
-        query_gain_grad.reshape(1, 1024),
-        jnp.pad(key_gain_grad, (0, 512)).reshape(1, 1024),
-        ffn_gain_grad.reshape(1, 1024),
-        jnp.zeros((4, 1024), jnp.float32),
-    ]
-    weight_sums, small_sums = total_everywhere(
-        jnp.concatenate([part.astype(jnp.bfloat16) for part in weight_parts], axis=0),
-        jnp.concatenate(small_parts, axis=0),
-    )
+    weight_sums, small_sums = total_everywhere(late, late_small)
     weight_sums = weight_sums.astype(jnp.float32)
     query_w_sum = jnp.concatenate([weight_sums[:1024], weight_sums[1024:2048]], axis=1)
     key_w_sum, value_w_sum = weight_sums[2048:3072], weight_sums[3072:4096]
-    output_w_sum = jnp.concatenate([weight_sums[4096:5120], weight_sums[5120:]], axis=1)
-    router_sum = small_sums[:32].reshape(1024, 32)
-    attn_gain_sum, query_gain_sum, ffn_gain_sum = small_sums[32], small_sums[33], small_sums[35]
-    key_gain_sum = small_sums[34, :512]
-    gate_up_sum, down_w_sum = lax.psum((gate_up_w_grad, down_grad), "dp")
+    router_sum = early_small[:EXPERTS].T
+    ffn_gain_sum, attn_gain_sum, query_gain_sum = early_small[EXPERTS], small_sums[0], small_sums[1]
+    key_gain_sum = small_sums[2, :512]
     gate_w_sum = gate_up_sum[:, :, :512].astype(jnp.float32)
     up_w_sum = gate_up_sum[:, :, 512:].astype(jnp.float32)
     down_w_sum = down_w_sum.astype(jnp.float32)

time: 549 us -> 394 us (0.72)
  matrix products: 90.9 us -> 0 us
  waiting for transfers between devices: 89 us -> 0.02 us
  Pallas kernels: 266 us -> 348 us
  other arithmetic: 40.8 us -> 12 us
  local copies, waits for them, and re-layouts: 43 us -> 18.3 us
    pallas_call x0 -> x1, Pallas kernels: none -> 103 us  [backward(): pl.pallas_call(backward_kernel, name='backward', out_shape=(shape((ROWS,...]
    dot_general x51 -> x0, matrix products: 90.9 us -> none  [the longest x8 18.6 us: masked_scores(): jnp.einsum('trd,sd->rts', query_pair, key_head, preferred_element_type=jn...]
    reduce_scatter x2 -> x0, waiting for transfers between devices: 88.4 us -> none  [the longest x1 76.3 us: body(): lax.psum_scatter(mixed_parts.reshape(16 * ROWS, width), 'expert', scatter...]
    pallas_call x1, Pallas kernels: 75 us -> 54.3 us  [total_everywhere(): pl.pallas_call(total_kernel, name='total', out_shape=(jax.ShapeDtypeStruc...]
    reshape x7 -> x0, local copies, waits for them, and re-layouts: 8.53 us -> none  [the longest x2 3.61 us: rotate(): heads_view = values.reshape(count_rows, -1, HEAD_DIM)]
    concatenate x2 -> x0, other arithmetic: 7.24 us -> none  [the longest x1 4.82 us: sent_together(): both = jnp.concatenate(arrays, axis=along)]
    slice x6 -> x4, local copies, waits for them, and re-layouts: 15.5 us -> 8.94 us  [the longest x1 4.85 us: body(): key_w_sum, value_w_sum = (weight_sums[2048:3072], weight_sums[3072:4096])]
    convert_element_type x15 -> x1, other arithmetic: 6.56 us -> 0.01 us  [rope_tables(): angles = positions.astype(jnp.float32)[:, None] * inverse[None, :]]
  transfers between devices with their start and end apart: 3 -> 1, of which waited for: 2 -> 0; matrix products, arithmetic and copies ran while one was open for 24% -> 3% of each run, Pallas kernels for 0% -> 40%
where the time goes in v3:
time: 394 us
  Pallas kernels  348 us (88%)
  local copies, waits for them, and re-layouts  18.3 us (5%)
  between operations  14.8 us (4%)
  other arithmetic  12 us (3%)
    pallas_call x1, Pallas kernels, moe(): pl.pallas_call(moe_kernel, name='moe', out_shape=(jax.ShapeDtypeStruct((F...  131 us
    pallas_call x1, Pallas kernels, backward(): pl.pallas_call(backward_kernel, name='backward', out_shape=(shape((ROWS,...  103 us
    pallas_call x1, Pallas kernels, forward(): pl.pallas_call(forward_kernel, name='forward', out_shape=(shape((ROWS, 10...  59.9 us
    pallas_call x1, Pallas kernels, total_everywhere(): pl.pallas_call(total_kernel, name='total', out_shape=(jax.ShapeDtypeStruc...  54.3 us
  transfers between devices with their start and end apart: 1, of which 0 were waited for; matrix products, arithmetic and copies ran while one was open for 3% of the time, Pallas kernels for 40%

profile of v3, /device:TPU:1, one launch (start us, length us, event | category | flops | bytes accessed | tf_op | source)
XLA Modules:
  0.0 393.6 jit_solution(9042343738114235995)
XLA Ops:
  7.2 0.0 all-reduce.3.cloned.1.call-start
  7.9 1.3 reshape.57.key_gain
  9.2 1.3 reshape.55.attn_gain
  10.4 1.3 reshape.56.query_gain
  11.7 1.3 reshape.58.ffn_gain
  13.0 0.8 multiply_sine_fusion
  13.8 59.9 %forward.1 = (bf16[256,1024]{1,0:T(8,128)(2,1)}, f32[256,1024]{1,0:T(8,128)}, bf16[1024,256]{1,0:T(8,128)(2,1)}, bf16[8,64,512]{2,1,0:T(8,128)(2,1)}, f32[8,1,51...) custom-call(bf16[256,1024]{1,0:T(8,128)(2,1)} %bitcast.17, ...), custom_call_target="tpu_custom_call" | custom-call | tf_op jit(solution)/shard_map/forward/pallas_call | solution.py:732
  73.7 130.9 %moe.1 = (f32[272,1024]{1,0:T(8,128)}, bf16[16,256,1024]{2,1,0:T(8,128)(2,1)}, bf16[2,1024,1024]{2,1,0:T(8,128)(2,1)}, bf16[2,512,1024]{2,1,0:T(8,128)(2,1)}) custom-call(bf16[256,1024]{1,0:T(8,128)(2,1)} %get-tuple-element.36.ffn.ffn_in, bf16[4352,1024]{1,0:T(8,128)(2,1)} %get-tuple-element.37.cot, bf16[32,1024]{1,0:T(8,128)(2,1)} %bitcast.29, ...), custom_call_target="tpu_custom_call" | custom-call | flops 49999998976 | bytes 40000000 | tf_op jit(solution)/shard_map/moe/pallas_call | solution.py:431
  204.6 0.0 all-reduce.3.cloned.1.call-update
  204.7 103.3 %backward.1 = (bf16[256,1024]{1,0:T(8,128)(2,1)}, bf16[256,1024]{1,0:T(8,128)(2,1)}, bf16[4096,512]{1,0:T(8,128)(2,1)}, f32[40,1024]{1,0:T(8,128)}, f32[8,1024]{1,0:T(8,128)}, /*index=5*/f32[1024,1024]{1,0:T(8,128)}) custom-call(f32[272,1024]{1,0:T(8,128)} %get-tuple-element.38.returned, f32[256,1024]{1,0:T(8,128)} %get-tuple-element.39.hidden, ...), custom_call_target="tpu_custom_call" | custom-call | flops 99999997952 | bytes 60000000 | tf_op jit(solution)/shard_map/backward/pallas_call | solution.py:1329
  308.0 1.4 slice.40
  309.3 54.3 %total.1 = (bf16[4096,512]{1,0:T(8,128)(2,1)}, f32[8,1024]{1,0:T(8,128)}) custom-call(bf16[4096,512]{1,0:T(8,128)(2,1)} %get-tuple-element.50.parts, f32[8,1024]{1,0:T(8,128)} %get-tuple-element.51.small), custom_call_target="tpu_custom_call" | custom-call | tf_op jit(solution)/shard_map/total/pallas_call | solution.py:963
  363.6 1.3 slice.39
  364.9 4.9 %fusion = (f32[1024,512]{1,0:T(8,128)}, f32[1024,512]{1,0:T(8,128)}, f32[1024,512]{1,0:T(8,128)S(1)}, f32[1024,512]{1,0:T(8,128)S(1)}) fusion(bf16[4096,512]{1,0:T(8,128)(2,1)} %get-tuple-element.53), kind=kLoop, calls=%fused_computation.8 | loop fusion | bytes 16777216 | tf_op jit(solution)/shard_map/slice | solution.py:1431
  369.8 2.3 pad_maximum_fusion
  372.1 1.4 fusion.1
  373.5 0.0 copy-done.4
  373.5 0.7 slice_bitcast_fusion
  374.2 4.2 %convert_element_type.31 = f32[2,512,1024]{2,1,0:T(8,128)} convert(bf16[2,512,1024]{2,1,0:T(8,128)(2,1)} %get-tuple-element.59) | non-fusion elementwise | flops 1048576 | bytes 6291456 | tf_op jit(solution)/shard_map/convert_element_type | solution.py:1437
  378.4 4.7 %slice_convert_fusion = (f32[2,1024,512]{2,1,0:T(8,128)}, f32[2,1024,512]{2,1,0:T(8,128)}) fusion(bf16[2,1024,1024]{2,1,0:T(8,128)(2,1)S(1)} %copy-done), kind=kLoop, calls=%fused_computation.1 | loop fusion | flops 2097152 | bytes 12582912 | tf_op jit(solution)/shard_map/convert_element_type | solution.py:1436
  383.1 0.8 copy.36
  383.9 0.8 copy.37
  384.7 0.0 copy-done.1
  384.7 2.0 copy.38
  (11 shorter events, 0.0 us)
Async XLA Ops:
  7.2 367.0 %all-reduce.3.cloned.1.call-start = ((), (), s32[]{:S(2)}) async-start(), calls=%async_computation | async-start | bytes 12582912 | tf_op jit(solution)/shard_map/psum | solution.py:1420
  369.8 3.8 copy-start.4
  374.2 4.2 %copy-start = (bf16[2,1024,1024]{2,1,0:T(8,128)(2,1)S(1)}, bf16[2,1024,1024]{2,1,0:T(8,128)(2,1)}, u32[]{:S(2)}) copy-start(bf16[2,1024,1024]{2,1,0:T(8,128)(2,1)} %get-tuple-element.58) | copy-start | bytes 12582916
  378.4 4.7 %copy-start.3 = (bf16[256,1024]{1,0:T(8,128)(2,1)S(1)}, bf16[256,1024]{1,0:T(8,128)(2,1)}, u32[]{:S(2)}) copy-start(bf16[256,1024]{1,0:T(8,128)(2,1)} %get-tuple-element.48) | copy-start | bytes 1572868
  378.4 5.5 %copy-start.2 = (bf16[256,1024]{1,0:T(8,128)(2,1)S(1)}, bf16[256,1024]{1,0:T(8,128)(2,1)}, u32[]{:S(2)}) copy-start(bf16[256,1024]{1,0:T(8,128)(2,1)} %get-tuple-element.49) | copy-start | bytes 1572868
  378.4 6.3 %copy-start.1 = (f32[1024,1024]{1,0:T(8,128)S(1)}, f32[1024,1024]{1,0:T(8,128)}, u32[]{:S(2)}) copy-start(f32[1024,1024]{1,0:T(8,128)} %get-tuple-element.92) | copy-start | bytes 12582916
Sparse Core Ops, SparseCore 0:
  204.8 115.6 all-reduce.2

commit v4 on v3

--- a/solution.py
+++ b/solution.py
@@ -157,7 +157,7 @@
         self.add(1, -1)
         self.copy(3).start()
 
-    def third(self, result=None):
+    def third(self, put=None):
         self.copy(2).wait_recv()
         self.copy(3).wait_recv()
         block = self.at(0)
@@ -172,10 +172,10 @@
                 + self.landing[left].astype(jnp.float32)
                 + self.landing[right].astype(jnp.float32)
             )
-            if result is None:
+            if put is None:
                 self.sums[block, here] = total.astype(jnp.bfloat16)
             else:
-                result[here] = total
+                put(here, total)
 
     def drain(self):
         for which in range(4):
@@ -184,9 +184,9 @@
 
 def moe_kernel(
     ffn, cot, wr, w_gate, w_up, w_down,
-    ret, mixed, grad_gu, grad_d,
+    ret, mixed, grad_g, grad_u, grad_d,
     rows, sums, wgu, wd, held, pair, inner, dgu, mixing, back, cotv, before, chosen, gate_rows, grad_rows, stage,
-    ag_send, ag_recv, rs_send, rs_recv, w_sem, cot_sem, stage_sem, credit,
+    ag_send, ag_recv, rs_send, rs_recv, w_sem, cot_sem, stage_sem, half_sem, credit,
 ):
     torus = Torus()
     barrier = pltpu.get_barrier_semaphore()
@@ -242,6 +242,9 @@
 
     def stage_copy(slot, target):
         return pltpu.make_async_copy(stage.at[slot], target, stage_sem.at[slot])
+
+    def half_copy(slot, half, target):
+        return pltpu.make_async_copy(stage.at[slot, :, pl.ds(half * 512, 512)], target, half_sem.at[slot, half])
 
     expert_rows = lax.broadcasted_iota(jnp.int32, (EXPERTS, ROWS), 0)
 
@@ -295,8 +298,8 @@
                 picked.append(jnp.where(slot_at == own, 1.0, 0.0))
             both = jnp.concatenate(picked, axis=0).astype(jnp.bfloat16)
             chosen[j] = both
-            took = dot_nn(both, block).astype(jnp.bfloat16)
-            took_grad = dot_nn(both, cotv[pl.ds(pl.multiple_of(j * FULL + EXTRA, 16), ROWS)]).astype(jnp.bfloat16)
+            grad_block = cotv[pl.ds(pl.multiple_of(j * FULL + EXTRA, 16), ROWS)]
+            took = dot_nn(both, jnp.concatenate([block, grad_block], axis=1)).astype(jnp.bfloat16)
             here = pl.ds(pl.multiple_of(j * CAP, 16), CAP)
             there = pl.ds(pl.multiple_of(g * GROUP + j * CAP, 16), CAP)
             for e in range(2):
@@ -305,8 +308,8 @@
                 )
                 of_rows = jnp.sum(picked[e] * own, axis=1, keepdims=True)
                 gate_rows[e, here] = jnp.broadcast_to(of_rows, (CAP, 128))
-                held[e, there] = took[e * CAP : (e + 1) * CAP]
-                mixing[e, here] = took_grad[e * CAP : (e + 1) * CAP]
+                held[e, there] = took[e * CAP : (e + 1) * CAP, :1024]
+                mixing[e, here] = took[e * CAP : (e + 1) * CAP, 1024:]
 
         @pl.when(g < 3)
         def _():
@@ -345,8 +348,11 @@
             both = chosen[j]
             picked = both.astype(jnp.float32)
             here = pl.ds(pl.multiple_of(j * CAP, 16), CAP)
-            part = dot_tn(both, jnp.concatenate([back[0, here], back[1, here]], axis=0))
-            sums[source, pl.ds(EXTRA, ROWS)] = part.astype(jnp.bfloat16)
+            compact = jnp.concatenate(
+                [jnp.concatenate([back[e, here], mixing[e, here]], axis=1) for e in range(2)], axis=0
+            )
+            spread = dot_tn(both, compact).astype(jnp.bfloat16)
+            sums[source, pl.ds(EXTRA, ROWS)] = spread[:, :1024]
             grads = jnp.zeros((EXPERTS, ROWS), jnp.float32)
             for e in range(2):
                 own = jnp.sum(
@@ -363,8 +369,7 @@
             def _():
                 stage_copy(slot, mixed.at[source]).wait()
 
-            result = dot_tn(both, jnp.concatenate([mixing[0, here], mixing[1, here]], axis=0))
-            stage[slot] = result.astype(jnp.bfloat16)
+            stage[slot] = spread[:, 1024:]
             stage_copy(slot, mixed.at[source]).start()
 
     pl.semaphore_wait(credit, 4)
@@ -382,33 +387,54 @@
     a_last = Scatter(torus, sums, rows, rs_send, rs_recv, 8, 4 * 384, "y", 0, 0, 64, 64)
     b_last = Scatter(torus, sums, rows, rs_send, rs_recv, 9, 1920 + 4 * 432, "z", 0, 128, 80, 64)
 
-    def write_grads(low, high):
+    def write_pair(low, high):
         @pl.loop(low, high)
         def _(k):
             slot = k % 2
-            e, c = k // 6, k % 6
-            stage_copy(slot, grad_d.at[0, pl.ds(0, 256)]).wait()
-
-            @pl.when(c < 4)
+            e, c = k // 4, k % 4
+
+            @pl.when(k < 2)
             def _():
-                columns = pl.ds(pl.multiple_of(c * 256, 256), 256)
-                stage[slot] = dot_tn(held[e, :, columns], dgu[e]).astype(jnp.bfloat16)
-                stage_copy(slot, grad_gu.at[e, columns]).start()
-
-            @pl.when(c >= 4)
+                stage_copy(slot, grad_d.at[0, pl.ds(0, 256)]).wait()
+
+            @pl.when(k >= 2)
             def _():
-                columns = pl.ds(pl.multiple_of((c - 4) * 256, 256), 256)
-                stage[slot] = dot_tn(inner[e, :, columns], pair[e]).astype(jnp.bfloat16)
-                stage_copy(slot, grad_d.at[e, columns]).start()
+                half_copy(slot, 0, grad_g.at[0, pl.ds(0, 256)]).wait()
+                half_copy(slot, 1, grad_u.at[0, pl.ds(0, 256)]).wait()
+
+            columns = pl.ds(pl.multiple_of(c * 256, 256), 256)
+            stage[slot] = dot_tn(held[e, :, columns], dgu[e]).astype(jnp.bfloat16)
+            half_copy(slot, 0, grad_g.at[e, columns]).start()
+            half_copy(slot, 1, grad_u.at[e, columns]).start()
+
+    def write_down():
+        @pl.loop(0, 4)
+        def _(k):
+            slot = k % 2
+            e, c = k // 2, k % 2
+
+            @pl.when(k < 2)
+            def _():
+                half_copy(slot, 0, grad_g.at[0, pl.ds(0, 256)]).wait()
+                half_copy(slot, 1, grad_u.at[0, pl.ds(0, 256)]).wait()
+
+            @pl.when(k >= 2)
+            def _():
+                stage_copy(slot, grad_d.at[0, pl.ds(0, 256)]).wait()
+
+            columns = pl.ds(pl.multiple_of(c * 256, 256), 256)
+            stage[slot] = dot_tn(inner[e, :, columns], pair[e]).astype(jnp.bfloat16)
+            stage_copy(slot, grad_d.at[e, columns]).start()
 
     for d in order:
         b_lead[d].first()
         a_lead[d].first()
-    write_grads(0, 4)
+    write_pair(0, 4)
     for d in order:
         b_lead[d].second()
         a_lead[d].second()
-    write_grads(4, 12)
+    write_pair(4, 8)
+    write_down()
     for slot in range(2):
         stage_copy(slot, grad_d.at[0, pl.ds(0, 256)]).wait()
     for d in order:
@@ -419,8 +445,12 @@
             a_last.first()
     b_last.second()
     a_last.second()
-    b_last.third(ret)
-    a_last.third(ret)
+
+    def put(at, total):
+        ret[at] = total
+
+    b_last.third(put)
+    a_last.third(put)
     for one in [*a_lead.values(), *b_lead.values(), a_last, b_last]:
         one.drain()
 
@@ -434,11 +464,12 @@
         out_shape=(
             jax.ShapeDtypeStruct((FULL, 1024), jnp.float32),
             jax.ShapeDtypeStruct((16, ROWS, 1024), low),
-            jax.ShapeDtypeStruct((2, 1024, 1024), low),
+            jax.ShapeDtypeStruct((2, 1024, 512), low),
+            jax.ShapeDtypeStruct((2, 1024, 512), low),
             jax.ShapeDtypeStruct((2, 512, 1024), low),
         ),
         in_specs=[vmem, hbm, vmem, hbm, hbm, hbm],
-        out_specs=(vmem, hbm, hbm, hbm),
+        out_specs=(vmem, hbm, hbm, hbm, hbm),
         scratch_shapes=[
             pltpu.VMEM((16 * ROWS, 1024), low),
             pltpu.VMEM((16, FULL, 1024), low),
@@ -463,6 +494,7 @@
             pltpu.SemaphoreType.DMA((3,)),
             pltpu.SemaphoreType.DMA,
             pltpu.SemaphoreType.DMA((2,)),
+            pltpu.SemaphoreType.DMA((2, 2)),
             pltpu.SemaphoreType.REGULAR,
         ],
         compiler_params=pltpu.CompilerParams(
@@ -487,6 +519,10 @@
 
 def rms_scale(values):
     return lax.rsqrt(jnp.mean(values * values, axis=-1, keepdims=True) + epsilon)
+
+
+def as_row(gain):
+    return gain[...].astype(jnp.float32).reshape(1, -1)
 
 
 def turned_rows(values, cosine, sine):
@@ -595,7 +631,7 @@
     def _(n):
         at = pl.ds(pl.multiple_of(n * 64, 64), 64)
         rows = tokens[at].astype(jnp.float32)
-        normed[at] = (rows * rms_scale(rows) * attn_gain[...].astype(jnp.float32)).astype(jnp.bfloat16)
+        normed[at] = (rows * rms_scale(rows) * as_row(attn_gain)).astype(jnp.bfloat16)
 
     for load in loads:
         load.wait()
@@ -603,7 +639,7 @@
     keys = Keys(here, device, kv, kv_send, kv_recv)
     key_raw[...] = dot_nn(normed[...], wk[...])
     scaled = key_raw[...]
-    scaled = (scaled * rms_scale(scaled) * key_gain[...].astype(jnp.float32)).T
+    scaled = (scaled * rms_scale(scaled) * as_row(key_gain)).T
     for j in range(KV_HEADS):
         head = turned_rows(scaled[j * 64 : j * 64 + 64], cosine[...], sine[...])
         kv[me, pl.ds(j * 64, 64)] = head.astype(jnp.bfloat16)
@@ -611,12 +647,11 @@
     keys.start(0, 1, 2)
     query_raw[...] = dot_nn(normed[...], wq[...])
     scaled = query_raw[...]
-    turned[...] = (scaled * rms_scale(scaled) * query_gain[...].astype(jnp.float32)).T
-
-    @pl.loop(0, KV_HEADS)
-    def _(j):
+    turned[...] = (scaled * rms_scale(scaled) * as_row(query_gain)).T
+
+    for j in range(KV_HEADS):
         for r in range(2):
-            head = turned[pl.ds(pl.multiple_of(j * 128 + r * 64, 64), 64)]
+            head = turned[j * 128 + r * 64 : j * 128 + r * 64 + 64]
             head = turned_rows(head, cosine[...], sine[...])
             queries[j, :, r * ROWS : (r + 1) * ROWS] = (head * HEAD_DIM**-0.5).astype(jnp.bfloat16)
 
@@ -630,16 +665,20 @@
     query_at = lax.broadcasted_iota(jnp.int32, (ROWS, 2 * ROWS), 1) % ROWS
     valid = (key_at <= query_at) & (key_at + me * ROWS < length[...])
 
-    @pl.loop(0, KV_HEADS)
-    def _(j):
-        key_head = kv[me, pl.ds(pl.multiple_of(j * 64, 64), 64)]
-        value_head = kv[me, pl.ds(pl.multiple_of(512 + j * 64, 64), 64)]
-        scores = jnp.where(valid, dot_tn(key_head, queries[j]), -1e30)
-        top = jnp.max(scores, axis=0, keepdims=True)
-        probs = jnp.exp(scores - top)
-        most[j] = top
-        total[j] = jnp.sum(probs, axis=0, keepdims=True)
-        mixed[j] = dot_nn(value_head, probs.astype(jnp.bfloat16))
+    def heads_of(block):
+        keys_here = [kv[block, j * 64 : j * 64 + 64] for j in range(KV_HEADS)]
+        values_here = [kv[block, 512 + j * 64 : 576 + j * 64] for j in range(KV_HEADS)]
+        return keys_here, values_here
+
+    keys_here, values_here = heads_of(me)
+    scores = [jnp.where(valid, dot_tn(keys_here[j], queries[j]), -1e30) for j in range(KV_HEADS)]
+    tops = [jnp.max(one, axis=0, keepdims=True) for one in scores]
+    probs = [jnp.exp(one - top) for one, top in zip(scores, tops)]
+    parts = [dot_nn(one, prob.astype(jnp.bfloat16)) for one, prob in zip(values_here, probs)]
+    for j in range(KV_HEADS):
+        most[j] = tops[j]
+        total[j] = jnp.sum(probs[j], axis=0, keepdims=True)
+        mixed[j] = parts[j]
 
     @pl.loop(1, 8)
     def _(step):
@@ -683,29 +722,29 @@
 
         @pl.when(block < me)
         def _():
-            @pl.loop(0, KV_HEADS)
-            def _(j):
-                key_head = kv[block, pl.ds(pl.multiple_of(j * 64, 64), 64)]
-                value_head = kv[block, pl.ds(pl.multiple_of(512 + j * 64, 64), 64)]
-                scores = dot_tn(key_head, queries[j])
-                before = most[j]
-                top = jnp.maximum(before, jnp.max(scores, axis=0, keepdims=True))
-                probs = jnp.exp(scores - top)
-                less = jnp.exp(before - top)
-                most[j] = top
-                total[j] = total[j] * less + jnp.sum(probs, axis=0, keepdims=True)
-                mixed[j] = mixed[j] * less + dot_nn(value_head, probs.astype(jnp.bfloat16))
+            keys_here, values_here = heads_of(block)
+            before = [most[j] for j in range(KV_HEADS)]
+            shares = [total[j] for j in range(KV_HEADS)]
+            sums = [mixed[j] for j in range(KV_HEADS)]
+            scores = [dot_tn(keys_here[j], queries[j]) for j in range(KV_HEADS)]
+            tops = [jnp.maximum(old, jnp.max(one, axis=0, keepdims=True)) for old, one in zip(before, scores)]
+            probs = [jnp.exp(one - top) for one, top in zip(scores, tops)]
+            less = [jnp.exp(old - top) for old, top in zip(before, tops)]
+            parts = [dot_nn(one, prob.astype(jnp.bfloat16)) for one, prob in zip(values_here, probs)]
+            for j in range(KV_HEADS):
+                most[j] = tops[j]
+                total[j] = shares[j] * less[j] + jnp.sum(probs[j], axis=0, keepdims=True)
+                mixed[j] = sums[j] * less[j] + parts[j]
 
     save = pltpu.make_async_copy(kv, kv_all, kv_sem)
     save.start()
 
-    @pl.loop(0, KV_HEADS)
-    def _(j):
+    for j in range(KV_HEADS):
         share = total[j]
         log_total[j] = most[j] + jnp.log(share)
-        head = (mixed[j] / share).astype(jnp.bfloat16)
+        head = (mixed[j] * (1.0 / share)).astype(jnp.bfloat16)
         for r in range(2):
-            mixed_t[pl.ds(pl.multiple_of(j * 128 + r * 64, 64), 64), :] = head[:, r * ROWS : (r + 1) * ROWS]
+            mixed_t[j * 128 + r * 64 : j * 128 + r * 64 + 64, :] = head[:, r * ROWS : (r + 1) * ROWS]
 
     hidden[...] = dot_tn(mixed_t[...], wo[...])
 
@@ -714,7 +753,7 @@
         at = pl.ds(pl.multiple_of(n * 64, 64), 64)
         rows = hidden[at] + tokens[at].astype(jnp.float32)
         hidden[at] = rows
-        ffn_in[at] = (rows * rms_scale(rows) * ffn_gain[...].astype(jnp.float32)).astype(jnp.bfloat16)
+        ffn_in[at] = (rows * rms_scale(rows) * as_row(ffn_gain)).astype(jnp.bfloat16)
 
     for d in (0, 1, -1, 2):
         a_second[d].third()
@@ -772,17 +811,21 @@
 
 
 ORDERS = (("x", "y", "z"), ("y", "z", "x"), ("z", "x", "y"))
+STREAMS = ((0, 768), (768, 768), (1536, 512))
 
 
 class Total:
-    def __init__(self, here, device, buffer, final, landing, work, send, recv, number, half, start, rows, base, order):
-        self.here, self.device, self.buffer, self.final = here, device, buffer, final
+    def __init__(self, here, device, buffer, shift, final, landing, work, send, recv, number, stream):
+        self.here, self.device, self.buffer, self.shift, self.final = here, device, buffer, shift, final
         self.landing, self.work = landing, work
-        self.send, self.recv, self.number, self.order = send, recv, number, order
-        self.half, self.start, self.rows, self.base = half, start, rows, base
+        self.send, self.recv, self.number, self.order = send, recv, number, ORDERS[(stream + number // 3) % 3]
+        self.start, self.rows = STREAMS[stream]
+        first = self.start + self.start * 9 // 8
+        r = self.rows
+        self.lands = (first, first + r, first + r + 3 * (r // 4), first + r + 3 * (r // 4) + 3 * (r // 16))
 
     def own(self):
-        return self.here["core"] * self.half + self.start
+        return self.here["core"] * 2048 + self.start
 
     def copy(self, which, source, target, axis, step):
         return pltpu.make_async_remote_copy(
@@ -794,8 +837,14 @@
             device_id_type=MESH,
         )
 
-    def part(self, ref, at, size):
-        return ref.at[pl.ds(pl.multiple_of(at, 16), size)]
+    def held(self, at, size):
+        return self.buffer.at[pl.ds(pl.multiple_of(at + self.shift, 16), size)]
+
+    def ready(self, at, size):
+        return self.final.at[pl.ds(pl.multiple_of(at, 16), size)]
+
+    def land(self, stage, n, size):
+        return self.landing.at[pl.ds(self.lands[stage] + n * size, size)]
 
     def copies(self, stage):
         r, own = self.rows, self.own()
@@ -803,30 +852,25 @@
         ia, ib = self.here[a], self.here[b]
         second = own + ia * (r // 4)
         third = second + ib * (r // 16)
-        land1, land2, land3 = self.base + r, self.base + r + 3 * (r // 4), self.base + r + 3 * (r // 4) + 3 * (r // 16)
         if stage == 0:
-            there = (1 - self.here["core"]) * self.half + self.start
-            return [self.copy(0, self.part(self.buffer, there, r), self.part(self.landing, self.base, r), "core", 1)]
+            there = (1 - self.here["core"]) * 2048 + self.start
+            return [self.copy(0, self.held(there, r), self.land(0, 0, r), "core", 1)]
         if stage == 6:
-            whole = self.part(self.final, own, r)
-            return [self.copy(16, whole, whole, "core", 1)]
+            return [self.copy(16, self.ready(own, r), self.ready(own, r), "core", 1)]
         found = []
         for d in (1, 2, 3):
             if stage == 1:
-                source = self.part(self.buffer, own + (ia + d) % RING * (r // 4), r // 4)
-                target, axis = self.part(self.landing, land1 + (d - 1) * (r // 4), r // 4), a
+                source, target, axis = self.held(own + (ia + d) % RING * (r // 4), r // 4), self.land(1, d - 1, r // 4), a
             elif stage == 2:
-                source = self.part(self.buffer, second + (ib + d) % RING * (r // 16), r // 16)
-                target, axis = self.part(self.landing, land2 + (d - 1) * (r // 16), r // 16), b
+                source = self.held(second + (ib + d) % RING * (r // 16), r // 16)
+                target, axis = self.land(2, d - 1, r // 16), b
             elif stage == 3:
                 source = self.work.at[self.number, pl.ds(0, r // 16)]
-                target, axis = self.part(self.landing, land3 + (d - 1) * (r // 16), r // 16), c
+                target, axis = self.land(3, d - 1, r // 16), c
             elif stage == 4:
-                source = self.part(self.final, third, r // 16)
-                target, axis = source, b
+                source, target, axis = self.ready(third, r // 16), self.ready(third, r // 16), b
             else:
-                source = self.part(self.final, second, r // 4)
-                target, axis = source, a
+                source, target, axis = self.ready(second, r // 4), self.ready(second, r // 4), a
             found.append(self.copy(1 + (stage - 1) * 3 + d - 1, source, target, axis, d))
         return found
 
@@ -834,44 +878,52 @@
         for copy in self.copies(stage):
             copy.start()
 
-    def add(self, target, start, size, lands):
+    def add(self, stage, load, store, size, count):
         step = 64 if size % 64 == 0 else 16
 
         @pl.loop(0, size // step)
         def _(k):
-            here = pl.ds(pl.multiple_of(start + k * step, 16), step)
-            total = self.buffer[here].astype(jnp.float32)
-            for land in lands:
-                total = total + self.landing[pl.ds(pl.multiple_of(land + k * step, 16), step)].astype(jnp.float32)
-            if target is None:
-                self.buffer[here] = total.astype(jnp.bfloat16)
-            else:
-                target[pl.ds(pl.multiple_of(k * step, 16), step)] = total.astype(jnp.bfloat16)
+            at = k * step
+            total = load(at, step).astype(jnp.float32)
+            for n in range(count):
+                land = pl.ds(pl.multiple_of(self.lands[stage] + n * size + at, 16), step)
+                total = total + self.landing[land].astype(jnp.float32)
+            store(at, step, total.astype(jnp.bfloat16))
 
     def finish(self, stage):
         for copy in self.copies(stage):
             copy.wait_recv()
+        if stage > 3:
+            return
         r, own = self.rows, self.own()
         a, b, _ = self.order
         second = own + self.here[a] * (r // 4)
         third = second + self.here[b] * (r // 16)
-        land1, land2, land3 = self.base + r, self.base + r + 3 * (r // 4), self.base + r + 3 * (r // 4) + 3 * (r // 16)
+        first = (own, second, third, third)[stage] + self.shift
+
+        def in_place(at, step, *value):
+            lines = pl.ds(pl.multiple_of(first + at, 16), step)
+            if not value:
+                return self.buffer[lines]
+            self.buffer[lines] = value[0]
+
+        def in_work(at, step, *value):
+            lines = pl.ds(pl.multiple_of(at, 16), step)
+            if not value:
+                return self.work[self.number, lines]
+            self.work[self.number, lines] = value[0]
+
+        def in_final(at, step, value):
+            self.final[pl.ds(pl.multiple_of(third + at, 16), step)] = value
+
         if stage == 0:
-            self.add(None, own, r, [self.base])
+            self.add(0, in_place, in_place, r, 1)
         elif stage == 1:
-            self.add(None, second, r // 4, [land1 + d * (r // 4) for d in range(3)])
+            self.add(1, in_place, in_place, r // 4, 3)
         elif stage == 2:
-            self.add(self.work.at[self.number], third, r // 16, [land2 + d * (r // 16) for d in range(3)])
-        elif stage == 3:
-            r16 = r // 16
-
-            @pl.loop(0, r16 // 16)
-            def _(k):
-                total = self.work[self.number, pl.ds(pl.multiple_of(k * 16, 16), 16)].astype(jnp.float32)
-                for d in range(3):
-                    at = land3 + d * r16 + k * 16
-                    total = total + self.landing[pl.ds(pl.multiple_of(at, 16), 16)].astype(jnp.float32)
-                self.final[pl.ds(pl.multiple_of(third + k * 16, 16), 16)] = total.astype(jnp.bfloat16)
+            self.add(2, in_place, in_work, r // 16, 3)
+        else:
+            self.add(3, in_work, in_final, r // 16, 3)
 
     def drain(self):
         for stage in range(7):
@@ -919,74 +971,6 @@
                 copy.wait_send()
 
 
-def total_kernel(parts, small, whole, small_whole, held, landing, work, values, small_landing, send, recv, small_send, small_recv, load_sem):
-    here, device = everywhere()
-    barrier = pltpu.get_barrier_semaphore()
-    peers = [device("core", 1)] + [device(axis, d) for axis in "xyz" for d in (1, 2, 3)]
-    for peer in peers:
-        pl.semaphore_signal(barrier, inc=1, device_id=peer, device_id_type=MESH)
-    load = pltpu.make_async_copy(parts, held, load_sem)
-    load.start()
-    values[0] = small[...]
-    load.wait()
-    pl.semaphore_wait(barrier, len(peers))
-    half, base, streams = whole.shape[0] // 2, 0, []
-    for s, (start, rows) in enumerate(EARLY):
-        streams.append(
-            Total(here, device, held, whole, landing, work, send, recv, s, half, start, rows, base, ORDERS[s])
-        )
-        base += rows + 3 * (rows // 4) + 6 * (rows // 16)
-    few = Small(device, values, small_landing, small_send, small_recv)
-    for one in streams:
-        one.begin(0)
-    few.begin(0)
-    for stage in range(7):
-        for one in streams:
-            one.finish(stage)
-            if stage < 6:
-                one.begin(stage + 1)
-        if stage < 4:
-            few.finish(stage)
-            if stage < 3:
-                few.begin(stage + 1)
-    small_whole[...] = values[4]
-    for one in streams:
-        one.drain()
-    few.drain()
-
-
-def total_everywhere(parts, small):
-    vmem, hbm = pl.BlockSpec(memory_space=pltpu.VMEM), pl.BlockSpec(memory_space=pl.ANY)
-    low = jnp.bfloat16
-    rows, width = parts.shape
-    room = sum(count + 3 * (count // 4) + 6 * (count // 16) for _, count in EARLY)
-    return pl.pallas_call(
-        total_kernel,
-        name="total",
-        out_shape=(
-            jax.ShapeDtypeStruct(parts.shape, low),
-            jax.ShapeDtypeStruct(small.shape, jnp.float32),
-        ),
-        in_specs=[hbm, vmem],
-        out_specs=(vmem, vmem),
-        scratch_shapes=[
-            pltpu.VMEM((rows, width), low),
-            pltpu.VMEM((room, width), low),
-            pltpu.VMEM((3, 48, width), low),
-            pltpu.VMEM((5, *small.shape), jnp.float32),
-            pltpu.VMEM((10, *small.shape), jnp.float32),
-            pltpu.SemaphoreType.DMA((3, 17)),
-            pltpu.SemaphoreType.DMA((3, 17)),
-            pltpu.SemaphoreType.DMA((10,)),
-            pltpu.SemaphoreType.DMA((10,)),
-            pltpu.SemaphoreType.DMA,
-        ],
-        compiler_params=pltpu.CompilerParams(
-            collective_id=2, has_side_effects=True, vmem_limit_bytes=56 * 2**20
-        ),
-    )(parts, small)
-
-
 class Line:
     def __init__(self, here, device):
         self.here, self.device = here, device
@@ -1012,18 +996,15 @@
     return jnp.concatenate([front * cosine + back * sine, back * cosine - front * sine], axis=0)
 
 
-EARLY = ((0, 768), (768, 768), (1536, 512))
-
-
 def backward_kernel(
-    returned, hidden, ffn_in, cot, tokens, normed, query_raw, key_raw, mixed_t, queries, log_total,
+    hidden, ffn_in, cot, tokens, normed, key_raw, mixed_t, queries, log_total,
     routes_t, length, cosine, sine, attn_gain, query_gain, key_gain, ffn_gain, router_rows,
-    mixed_parts, kv_all, w_query, w_key, w_value, w_output,
-    mixed_out, token_grad, late, early_small, late_small, output_sum,
-    sums, rows, wq, wk, wv, wo, kv, hidden_grad, result, branch, grads, delta, query_grad, turned,
-    for_mate, from_mate, kv_sums, kv_rows, kv_grad, raw_grad, key_low, value_low,
-    held, final, landing, work, values, small_rows,
-    rs_send, rs_recv, mate_send, mate_recv, kv_send, kv_recv, ar_send, ar_recv, small_send, small_recv, load_sem, stage_sem,
+    returned_all, query_raw_all, mixed_parts, kv_all, w_query, w_key, w_value, w_output,
+    mixed_out, token_grad, early_small, late_small, query_sum, key_sum, value_sum, output_sum,
+    sums, rows, returned, square, kv, hidden_grad, result, branch, grads, delta, query_grad, turned,
+    for_mate, from_mate, kv_sums, kv_rows, key_low, value_low,
+    held, finals, landing, work, values, small_rows, late_values, late_rows,
+    rs_send, rs_recv, mate_send, mate_recv, kv_send, kv_recv, ar_send, ar_recv, small_send, small_recv, load_sem, out_sem,
 ):
     torus = Torus()
     here, device = everywhere()
@@ -1035,7 +1016,7 @@
     loads = [
         pltpu.make_async_copy(source, target, load_sem.at[n])
         for n, (source, target) in enumerate(
-            ((w_output, wo), (mixed_parts, sums), (kv_all, kv), (w_query, wq), (w_key, wk), (w_value, wv))
+            ((returned_all, returned), (w_output, square), (mixed_parts, sums), (kv_all, kv))
         )
     ]
     for load in loads:
@@ -1049,6 +1030,7 @@
     logits = jnp.where(named, dot_nt(router_rows[...], ffn_in[...]), -1e30)
     weight = jnp.where(named, jnp.exp(logits - jnp.max(logits, axis=0, keepdims=True)), 0.0)
     gates = weight / jnp.sum(weight, axis=0, keepdims=True)
+    loads[0].wait()
     gate_grad = jnp.concatenate([returned[:8, q * ROWS : (q + 1) * ROWS] for q in range(4)], axis=0)
     logit_grad = (gates * (gate_grad - jnp.sum(gates * gate_grad, axis=0, keepdims=True))).astype(jnp.bfloat16)
     result[...] = dot_tn(logit_grad, router_rows[...])
@@ -1057,7 +1039,7 @@
     def ffn_part(n, gain_grad):
         at = pl.ds(pl.multiple_of(n * 64, 64), 64)
         grad = result[at] + returned[pl.ds(pl.multiple_of(n * 64 + EXTRA, 16), 64)]
-        part, more = rms_back(hidden[at], ffn_gain[...].astype(jnp.float32), grad)
+        part, more = rms_back(hidden[at], as_row(ffn_gain), grad)
         part = part + cot[at].astype(jnp.float32)
         hidden_grad[at] = part
         branch[at] = part.astype(jnp.bfloat16)
@@ -1066,13 +1048,17 @@
     gain_grad = lax.fori_loop(0, 4, ffn_part, jnp.zeros((1, 1024), jnp.float32))
     values[0, EXPERTS:] = jnp.concatenate([gain_grad, jnp.zeros((7, 1024), jnp.float32)], axis=0)
 
-    loads[0].wait()
-    turned[...] = dot_nt(wo[...], branch[...])
-
-    @pl.loop(0, KV_HEADS)
-    def _(j):
+    loads[1].wait()
+    turned[...] = dot_nt(square[...], branch[...])
+    next_load = pltpu.make_async_copy(w_query, square, load_sem.at[6])
+    next_load.start()
+    query_raw = returned.at[pl.ds(0, ROWS)]
+    raw_load = pltpu.make_async_copy(query_raw_all, query_raw, load_sem.at[7])
+    raw_load.start()
+
+    for j in range(KV_HEADS):
         for r in range(2):
-            at = pl.ds(pl.multiple_of(j * 128 + r * 64, 64), 64)
+            at = slice(j * 128 + r * 64, j * 128 + r * 64 + 64)
             low = turned[at].astype(jnp.bfloat16)
             grads[j, :, r * ROWS : (r + 1) * ROWS] = low
             delta[j, :, r * ROWS : (r + 1) * ROWS] = jnp.sum(
@@ -1087,17 +1073,22 @@
         for q in range(4):
             held[pl.ds(pl.multiple_of(q * 1024 + n * 256, 256), 256)] = part[:, q * 256 : (q + 1) * 256]
 
-    for load in loads[1:]:
+    for load in loads[2:]:
         load.wait()
     pl.semaphore_wait(barrier, len(peers))
 
-    half, base, early = 2048, 0, []
-    for s, (start, count) in enumerate(EARLY):
-        early.append(
-            Total(here, device, held, final, landing, work, ar_send, ar_recv, s, half, start, count, base, ORDERS[s])
-        )
-        base += count + 3 * (count // 4) + 6 * (count // 16)
-    few = Small(device, values, small_rows, small_send, small_recv)
+    def reduction(number, buffer, shift):
+        return [
+            Total(
+                here, device, buffer, shift, finals.at[number], landing.at[number], work,
+                ar_send, ar_recv, 3 * number + s, s,
+            )
+            for s in range(3)
+        ]
+
+    early, of_query, of_keys = reduction(0, held, 0), reduction(1, kv, 0), reduction(2, kv, 4096)
+    few = Small(device, values, small_rows, small_send.at[0], small_recv.at[0])
+    late_few = Small(device, late_values, late_rows, small_send.at[1], small_recv.at[1])
     order = (2, 1, -1, 0)
     leads = []
     for n, d in enumerate(order):
@@ -1115,19 +1106,31 @@
     for one in leads:
         one.first()
 
-    def early_step(stage):
-        for one in early:
+    def onward(streams, stage, small=None):
+        for one in streams:
             one.finish(stage)
             if stage < 6:
                 one.begin(stage + 1)
-        if stage < 4:
-            few.finish(stage)
+        if small is not None and stage < 4:
+            small.finish(stage)
             if stage < 3:
-                few.begin(stage + 1)
+                small.begin(stage + 1)
+
+    def early_step(stage):
+        onward(early, stage, few)
+
+    def write_out(number, column, target, at):
+        block = finals.at[number, pl.ds(column * 1024, 1024)]
+        return pltpu.make_async_copy(block, target.at[:, pl.ds(at * 256, 256)], out_sem.at[number, column])
+
+    outs = [write_out(0, q, output_sum, q) for q in range(4)]
+    outs += [write_out(1, q, query_sum, q) for q in range(4)]
+    outs += [write_out(2, q, key_sum, q) for q in range(2)]
+    outs += [write_out(2, 2 + q, value_sum, q) for q in range(2)]
 
     def mate_copy(turn, at):
         return pltpu.make_async_remote_copy(
-            src_ref=for_mate.at[at],
+            src_ref=for_mate.at[turn % 2],
             dst_ref=from_mate.at[at],
             send_sem=mate_send.at[turn],
             recv_sem=mate_recv.at[turn],
@@ -1140,19 +1143,26 @@
     valid = (key_at <= query_at) & (key_at + me * ROWS < length[...])
 
     def block_grads(block, target, at, masked):
-        @pl.loop(0, KV_HEADS)
-        def _(j):
-            key_lines = pl.ds(pl.multiple_of(j * 64, 64), 64)
-            value_lines = pl.ds(pl.multiple_of(512 + j * 64, 64), 64)
-            key_head, value_head = kv[block, key_lines], kv[block, value_lines]
-            probs = jnp.exp(dot_tn(key_head, queries[j]) - log_total[j])
+        for group in range(2):
+            heads = range(4 * group, 4 * group + 4)
+            key_heads = [kv[pl.ds(pl.multiple_of(block * 1024 + j * 64, 64), 64)] for j in heads]
+            value_heads = [kv[pl.ds(pl.multiple_of(block * 1024 + 512 + j * 64, 64), 64)] for j in heads]
+            probs = [jnp.exp(dot_tn(one, queries[j]) - log_total[j]) for one, j in zip(key_heads, heads)]
             if masked:
-                probs = jnp.where(valid, probs, 0.0)
-            probs_grad = dot_tn(value_head, grads[j])
-            score_grad = (probs * (probs_grad - delta[j])).astype(jnp.bfloat16)
-            target[at, key_lines] = dot_nt(queries[j], score_grad).astype(jnp.bfloat16)
-            target[at, value_lines] = dot_nt(grads[j], probs.astype(jnp.bfloat16)).astype(jnp.bfloat16)
-            query_grad[j] += dot_nn(key_head, score_grad)
+                probs = [jnp.where(valid, one, 0.0) for one in probs]
+            probs_grads = [dot_tn(one, grads[j]) for one, j in zip(value_heads, heads)]
+            lows = [
+                (one * (grad - delta[j])).astype(jnp.bfloat16) for one, grad, j in zip(probs, probs_grads, heads)
+            ]
+            key_parts = [dot_nt(queries[j], low).astype(jnp.bfloat16) for low, j in zip(lows, heads)]
+            value_parts = [
+                dot_nt(grads[j], one.astype(jnp.bfloat16)).astype(jnp.bfloat16) for one, j in zip(probs, heads)
+            ]
+            query_parts = [dot_nn(one, low) for one, low in zip(key_heads, lows)]
+            for n, j in enumerate(heads):
+                target[at, j * 64 : j * 64 + 64] = key_parts[n]
+                target[at, 512 + j * 64 : 576 + j * 64] = value_parts[n]
+                query_grad[j] += query_parts[n]
 
     def from_other(turn, at):
         mate_copy(turn, at).wait_recv()
@@ -1190,13 +1200,17 @@
         at = turn_x(turn)
         other = at * 2 + 1 - here["core"]
 
+        @pl.when(turn >= 2)
+        def _():
+            mate_copy(turn - 2, at).wait_send()
+
         @pl.when(other < me)
         def _():
-            block_grads(other, for_mate, at, False)
+            block_grads(other, for_mate, turn % 2, False)
 
         @pl.when(other >= me)
         def _():
-            for_mate[at] = jnp.zeros((1024, ROWS), jnp.bfloat16)
+            for_mate[turn % 2] = jnp.zeros((1024, ROWS), jnp.bfloat16)
 
         mate_copy(turn, at).start()
 
@@ -1240,18 +1254,18 @@
         def _():
             ring.second()
 
-    @pl.loop(0, KV_HEADS)
-    def _(j):
+    for j in range(KV_HEADS):
         for r in range(2):
             head = query_grad[j, :, r * ROWS : (r + 1) * ROWS] * HEAD_DIM**-0.5
-            turned[pl.ds(pl.multiple_of(j * 128 + r * 64, 64), 64)] = turned_back(head, cosine[...], sine[...])
-
+            turned[j * 128 + r * 64 : j * 128 + r * 64 + 64] = turned_back(head, cosine[...], sine[...])
+
+    raw_load.wait()
     result[...] = turned[...].T
 
     def query_part(n, gain_grad):
         at = pl.ds(pl.multiple_of(n * 64, 64), 64)
-        part, more = rms_back(query_raw[at], query_gain[...].astype(jnp.float32), result[at])
-        raw_grad[at] = part.astype(jnp.bfloat16)
+        part, more = rms_back(query_raw[at], as_row(query_gain), result[at])
+        branch[at] = part.astype(jnp.bfloat16)
         return gain_grad + more
 
     query_gain_grad = lax.fori_loop(0, 4, query_part, jnp.zeros((1, 1024), jnp.float32))
@@ -1259,65 +1273,98 @@
     @pl.loop(0, 4)
     def _(n):
         columns = pl.ds(pl.multiple_of(n * 256, 256), 256)
-        part = dot_tn(normed[:, columns], raw_grad[...]).astype(jnp.bfloat16)
-        for q in range(2):
-            late[pl.ds(pl.multiple_of(q * 1024 + n * 256, 256), 256)] = part[:, q * 512 : (q + 1) * 512]
-
-    result[...] = dot_nt(raw_grad[...], wq[...])
+        part = dot_tn(normed[:, columns], branch[...]).astype(jnp.bfloat16)
+        for q in range(4):
+            kv[pl.ds(pl.multiple_of(q * 1024 + n * 256, 256), 256)] = part[:, q * 256 : (q + 1) * 256]
+
+    for one in of_query:
+        one.begin(0)
     early_step(6)
-    ring.third(kv_grad)
-
+    for q in range(4):
+        outs[q].start()
+    early_small[...] = values[4]
+
+    def put(at, total):
+        turned[at] = total
+
+    ring.third(put)
     for j in range(KV_HEADS):
-        turned[j * 64 : j * 64 + 64] = turned_back(kv_grad[j * 64 : j * 64 + 64], cosine[...], sine[...])
-    part, key_gain_grad = rms_back(key_raw[...], key_gain[...].astype(jnp.float32), turned[:512].T)
+        turned[j * 64 : j * 64 + 64] = turned_back(turned[j * 64 : j * 64 + 64], cosine[...], sine[...])
+    part, key_gain_grad = rms_back(key_raw[...], as_row(key_gain), turned[:512].T)
     key_low[...] = part.astype(jnp.bfloat16)
-    value_low[...] = kv_grad[512:].T.astype(jnp.bfloat16)
+    value_low[...] = turned[512:].T.astype(jnp.bfloat16)
 
     @pl.loop(0, 4)
     def _(n):
         columns = pl.ds(pl.multiple_of(n * 256, 256), 256)
-        here_rows = normed[:, columns]
-        late[pl.ds(pl.multiple_of(2048 + n * 256, 256), 256)] = dot_tn(here_rows, key_low[...]).astype(jnp.bfloat16)
-        late[pl.ds(pl.multiple_of(3072 + n * 256, 256), 256)] = dot_tn(here_rows, value_low[...]).astype(jnp.bfloat16)
-
-    result[...] += dot_nt(key_low[...], wk[...]) + dot_nt(value_low[...], wv[...])
+        part = dot_tn(normed[:, columns], jnp.concatenate([key_low[...], value_low[...]], axis=1)).astype(jnp.bfloat16)
+        for q in range(4):
+            kv[pl.ds(pl.multiple_of(4096 + q * 1024 + n * 256, 256), 256)] = part[:, q * 256 : (q + 1) * 256]
+
+    for one in of_keys:
+        one.begin(0)
+    onward(of_query, 0)
+    next_load.wait()
+    result[...] = dot_nt(branch[...], square[...])
+    last_loads = [
+        pltpu.make_async_copy(w_key, square.at[:, pl.ds(0, 512)], load_sem.at[4]),
+        pltpu.make_async_copy(w_value, square.at[:, pl.ds(512, 512)], load_sem.at[5]),
+    ]
+    for load in last_loads:
+        load.start()
+    onward(of_keys, 0)
+    onward(of_query, 1)
+    for load in last_loads:
+        load.wait()
+    result[...] += dot_nt(jnp.concatenate([key_low[...], value_low[...]], axis=1), square[...])
+    onward(of_keys, 1)
+    onward(of_query, 2)
 
     def token_part(n, gain_grad):
         at = pl.ds(pl.multiple_of(n * 64, 64), 64)
-        part, more = rms_back(tokens[at].astype(jnp.float32), attn_gain[...].astype(jnp.float32), result[at])
+        part, more = rms_back(tokens[at].astype(jnp.float32), as_row(attn_gain), result[at])
         token_grad[at] = (hidden_grad[at] + part).astype(jnp.bfloat16)
         return gain_grad + more
 
     attn_gain_grad = lax.fori_loop(0, 4, token_part, jnp.zeros((1, 1024), jnp.float32))
     key_wide = jnp.concatenate([key_gain_grad, jnp.zeros((1, 512), jnp.float32)], axis=1)
-    late_small[...] = jnp.concatenate(
+    late_values[0] = jnp.concatenate(
         [attn_gain_grad, query_gain_grad, key_wide, jnp.zeros((5, 1024), jnp.float32)], axis=0
     )
-
-    stages = (turned, kv_grad)
-    for q in range(4):
-        slot = q % 2
-        out = pltpu.make_async_copy(stages[slot], output_sum.at[:, pl.ds(q * 256, 256)], stage_sem.at[slot])
-        if q >= 2:
-            out.wait()
-        stages[slot][...] = final[q * 1024 : (q + 1) * 1024].astype(jnp.float32)
-        out.start()
-    early_small[...] = values[4]
+    late_few.begin(0)
+    onward(of_keys, 2)
+    onward(of_query, 3, None)
+    late_few.finish(0)
+    late_few.begin(1)
+
+    def put_mixed(at, total):
+        mixed_out[at] = (hidden[at] + total).astype(jnp.bfloat16)
 
     for one in lasts:
-        one.third(result)
-
-    @pl.loop(0, 4)
-    def _(n):
-        at = pl.ds(pl.multiple_of(n * 64, 64), 64)
-        mixed_out[at] = (hidden[at] + result[at]).astype(jnp.bfloat16)
-
-    for slot in range(2):
-        pltpu.make_async_copy(stages[slot], output_sum.at[:, pl.ds(0, 256)], stage_sem.at[slot]).wait()
-    for one in [*leads, *lasts, ring, *early, few]:
+        one.third(put_mixed)
+    onward(of_keys, 3)
+    onward(of_query, 4)
+    late_few.finish(1)
+    late_few.begin(2)
+    onward(of_keys, 4)
+    onward(of_query, 5)
+    late_few.finish(2)
+    late_few.begin(3)
+    onward(of_keys, 5)
+    onward(of_query, 6)
+    for q in range(4, 8):
+        outs[q].start()
+    late_few.finish(3)
+    late_small[...] = late_values[4]
+    onward(of_keys, 6)
+    for q in range(8, 12):
+        outs[q].start()
+    for one in [*leads, *lasts, ring, *early, *of_query, *of_keys, few, late_few]:
         one.drain()
-    for turn in range(4):
+    for turn in (2, 3):
         mate_copy(turn, 0).wait_send()
+    for out in outs:
+        out.wait()
 
 
 def backward(smalls, larges):
@@ -1325,28 +1372,27 @@
     low, wide = jnp.bfloat16, jnp.float32
     shape = jax.ShapeDtypeStruct
     dma = pltpu.SemaphoreType.DMA
-    room = sum(count + 3 * (count // 4) + 6 * (count // 16) for _, count in EARLY)
     return pl.pallas_call(
         backward_kernel,
         name="backward",
         out_shape=(
             shape((ROWS, 1024), low),
             shape((ROWS, 1024), low),
-            shape((4096, 512), low),
             shape((40, 1024), wide),
             shape((8, 1024), wide),
-            shape((1024, 1024), wide),
+            shape((1024, 1024), low),
+            shape((1024, 512), low),
+            shape((1024, 512), low),
+            shape((1024, 1024), low),
         ),
         in_specs=[vmem] * len(smalls) + [hbm] * len(larges),
-        out_specs=(vmem,) * 5 + (hbm,),
+        out_specs=(vmem,) * 4 + (hbm,) * 4,
         scratch_shapes=[
             pltpu.VMEM((16, ROWS, 1024), low),
             pltpu.VMEM((10 * 384, 1024), low),
+            pltpu.VMEM((FULL, 1024), wide),
             pltpu.VMEM((1024, 1024), low),
-            pltpu.VMEM((1024, 512), low),
-            pltpu.VMEM((1024, 512), low),
-            pltpu.VMEM((1024, 1024), low),
-            pltpu.VMEM((8, 1024, ROWS), low),
+            pltpu.VMEM((8 * 1024, ROWS), low),
             pltpu.VMEM((ROWS, 1024), wide),
             pltpu.VMEM((ROWS, 1024), wide),
             pltpu.VMEM((ROWS, 1024), low),
@@ -1354,35 +1400,35 @@
             pltpu.VMEM((KV_HEADS, 1, 2 * ROWS), wide),
             pltpu.VMEM((KV_HEADS, HEAD_DIM, 2 * ROWS), wide),
             pltpu.VMEM((1024, ROWS), wide),
-            pltpu.VMEM((4, 1024, ROWS), low),
+            pltpu.VMEM((2, 1024, ROWS), low),
             pltpu.VMEM((4, 1024, ROWS), low),
             pltpu.VMEM((4, 1024, ROWS), low),
             pltpu.VMEM((3072, ROWS), low),
-            pltpu.VMEM((1024, ROWS), wide),
-            pltpu.VMEM((ROWS, 1024), low),
             pltpu.VMEM((ROWS, 512), low),
             pltpu.VMEM((ROWS, 512), low),
             pltpu.VMEM((4096, 256), low),
-            pltpu.VMEM((4096, 256), low),
-            pltpu.VMEM((room, 256), low),
-            pltpu.VMEM((3, 48, 256), low),
+            pltpu.VMEM((3, 4096, 256), low),
+            pltpu.VMEM((3, 4352, 256), low),
+            pltpu.VMEM((9, 48, 256), low),
             pltpu.VMEM((5, 40, 1024), wide),
             pltpu.VMEM((10, 40, 1024), wide),
+            pltpu.VMEM((5, 8, 1024), wide),
+            pltpu.VMEM((10, 8, 1024), wide),
             dma((10, 4)),
             dma((10, 4)),
             dma((4,)),
             dma((4,)),
             dma((1, 4)),
             dma((1, 4)),
-            dma((3, 17)),
-            dma((3, 17)),
-            dma((10,)),
-            dma((10,)),
-            dma((6,)),
-            dma((2,)),
+            dma((9, 17)),
+            dma((9, 17)),
+            dma((2, 10)),
+            dma((2, 10)),
+            dma((8,)),
+            dma((3, 4)),
         ],
         compiler_params=pltpu.CompilerParams(
-            collective_id=4, has_side_effects=True, vmem_limit_bytes=63 * 2**20
+            collective_id=4, has_side_effects=True, vmem_limit_bytes=66000000
         ),
         cost_estimate=pl.CostEstimate(flops=100 * 10**9, bytes_accessed=60 * 10**6, transcendentals=8 * 10**6),
     )(*smalls, *larges)
@@ -1410,31 +1456,26 @@
     cosine, sine_table = rope_tables(query_pos)
     cosine, sine_table = cosine.T, sine_table.T
     routes_t, length = routes[0].T, lengths.reshape(1, 1)
-    gains = [gain.reshape(1, -1) for gain in (attn_gain, query_gain, key_gain, ffn_gain)]
+    gains = [attn_gain, query_gain, key_gain, ffn_gain]
     weights = (w_query, w_key, w_value, w_output)
     router_rows = w_router.T
     ffn_in, hidden, mixed_t, queries, log_total, normed, query_raw, key_raw, kv_all, cot_all = forward(
         tokens[0], cotangent[0], routes_t, length, cosine, sine_table, gains, weights
     )
-    returned, mixed_parts, gate_up_w_grad, down_grad = moe(ffn_in, cot_all, router_rows, w_gate, w_up, w_down)
-    gate_up_sum, down_w_sum = lax.psum((gate_up_w_grad, down_grad), "dp")
-    mixed_out, token_grad, late, early_small, late_small, output_w_sum = backward(
+    returned, mixed_parts, *expert_grads = moe(ffn_in, cot_all, router_rows, w_gate, w_up, w_down)
+    expert_sums = lax.psum(tuple(expert_grads), "dp")
+    mixed_out, token_grad, early_small, late_small, *weight_sums = backward(
         (
-            returned, hidden, ffn_in, cotangent[0], tokens[0], normed, query_raw, key_raw, mixed_t, queries,
-            log_total, routes_t, length, cosine, sine_table, *gains, router_rows,
+            hidden, ffn_in, cotangent[0], tokens[0], normed, key_raw, mixed_t, queries, log_total, routes_t,
+            length, cosine, sine_table, *gains, router_rows,
         ),
-        (mixed_parts, kv_all, *weights),
+        (returned, query_raw, mixed_parts, kv_all.reshape(8 * 1024, ROWS), *weights),
     )
-    weight_sums, small_sums = total_everywhere(late, late_small)
-    weight_sums = weight_sums.astype(jnp.float32)
-    query_w_sum = jnp.concatenate([weight_sums[:1024], weight_sums[1024:2048]], axis=1)
-    key_w_sum, value_w_sum = weight_sums[2048:3072], weight_sums[3072:4096]
+    query_w_sum, key_w_sum, value_w_sum, output_w_sum = [part.astype(jnp.float32) for part in weight_sums]
+    gate_w_sum, up_w_sum, down_w_sum = [part.astype(jnp.float32) for part in expert_sums]
     router_sum = early_small[:EXPERTS].T
-    ffn_gain_sum, attn_gain_sum, query_gain_sum = early_small[EXPERTS], small_sums[0], small_sums[1]
-    key_gain_sum = small_sums[2, :512]
-    gate_w_sum = gate_up_sum[:, :, :512].astype(jnp.float32)
-    up_w_sum = gate_up_sum[:, :, 512:].astype(jnp.float32)
-    down_w_sum = down_w_sum.astype(jnp.float32)
+    ffn_gain_sum, attn_gain_sum, query_gain_sum = early_small[EXPERTS], late_small[0], late_small[1]
+    key_gain_sum = late_small[2, :512]
     return (
         mixed_out[None],
         token_grad[None],

time: 394 us -> 379 us (0.962)
  local copies, waits for them, and re-layouts: 18.3 us -> 7.18 us
  Pallas kernels: 348 us -> 337 us
  other arithmetic: 12 us -> 19.7 us
    pallas_call x1 -> x0, Pallas kernels: 54.3 us -> none  [total_everywhere(): pl.pallas_call(total_kernel, name='total', out_shape=(jax.ShapeDtypeStruc...]
    pallas_call x1, Pallas kernels: 103 us -> 148 us  [backward(): pl.pallas_call(backward_kernel, name='backward', out_shape=(shape((ROWS,...]
    convert_element_type x2 -> x7, other arithmetic: 8.88 us -> 18.8 us  [body(): part.astype(jnp.float32)]
    reshape x4 -> x0, local copies, waits for them, and re-layouts: 5.09 us -> none  [body(): gain.reshape(1, -1)]
    slice x3 -> x2, local copies, waits for them, and re-layouts: 7.59 us -> 2.82 us  [the longest x1 1.44 us: body(): late_small[1]]
  transfers between devices with their start and end apart: 1 -> 1, of which waited for: 0 -> 0; matrix products, arithmetic and copies ran while one was open for 3% -> 4% of each run, Pallas kernels for 40% -> 39%
where the time goes in v4:
time: 379 us
  Pallas kernels  337 us (89%)
  other arithmetic  19.7 us (5%)
  between operations  14.8 us (4%)
  local copies, waits for them, and re-layouts  7.18 us (2%)
    pallas_call x1, Pallas kernels, backward(): pl.pallas_call(backward_kernel, name='backward', out_shape=(shape((ROWS,...  148 us
    pallas_call x1, Pallas kernels, moe(): pl.pallas_call(moe_kernel, name='moe', out_shape=(jax.ShapeDtypeStruct((F...  129 us
    pallas_call x1, Pallas kernels, forward(): pl.pallas_call(forward_kernel, name='forward', out_shape=(shape((ROWS, 10...  60 us
    convert_element_type x7, other arithmetic, body(): part.astype(jnp.float32)  18.8 us
  transfers between devices with their start and end apart: 1, of which 0 were waited for; matrix products, arithmetic and copies ran while one was open for 4% of the time, Pallas kernels for 39%

profile of v4, /device:TPU:1, one launch (start us, length us, event | category | flops | bytes accessed | tf_op | source)
XLA Modules:
  0.0 378.7 jit_solution(5988390183134582001)
XLA Ops:
  7.2 0.0 all-reduce.3.cloned.1.call-start
  7.9 0.8 multiply_sine_fusion
  8.7 60.0 %forward.1 = (bf16[256,1024]{1,0:T(8,128)(2,1)}, f32[256,1024]{1,0:T(8,128)}, bf16[1024,256]{1,0:T(8,128)(2,1)}, bf16[8,64,512]{2,1,0:T(8,128)(2,1)}, f32[8,1,51...) custom-call(bf16[256,1024]{1,0:T(8,128)(2,1)} %bitcast.18, ...), custom_call_target="tpu_custom_call" | custom-call | tf_op jit(solution)/shard_map/forward/pallas_call | solution.py:771
  68.8 129.4 %moe.1 = (f32[272,1024]{1,0:T(8,128)}, bf16[16,256,1024]{2,1,0:T(8,128)(2,1)}, bf16[2,1024,512]{2,1,0:T(8,128)(2,1)}, bf16[2,1024,512]{2,1,0:T(8,128)(2,1)}, bf16[2,512,1024]{2,1,0:T(8,128)(2,1)}) custom-call(bf16[256,1024]{1,0:T(8,128)(2,1)} %get-tuple-element.38.ffn.ffn_in, bf16[4352,1024]{1,0:T(8,128)(2,1)} %get-tuple-element.44.cot, ...), custom_call_target="tpu_custom_call" | custom-call | flops 49999998976 | bytes 40000000 | tf_op jit(solution)/shard_map/moe/pallas_call | solution.py:461
  198.2 0.0 all-reduce.3.cloned.1.call-update
  198.2 147.6 %backward.1 = (bf16[256,1024]{1,0:T(8,128)(2,1)}, bf16[256,1024]{1,0:T(8,128)(2,1)}, f32[40,1024]{1,0:T(8,128)}, f32[8,1024]{1,0:T(8,128)}, bf16[1024,1024]{1,0:...) custom-call(f32[256,1024]{1,0:T(8,128)} %get-tuple-element.37.hidden, ...), custom_call_target="tpu_custom_call" | custom-call | flops 99999997952 | bytes 60000000 | tf_op jit(solution)/shard_map/backward/pallas_call | solution.py:1375
  345.8 0.0 copy-start.4
  345.8 1.4 slice.17
  347.2 1.4 slice.18
  348.5 2.8 convert_element_type.38
  351.4 0.0 copy-done.4
  351.4 1.6 convert_element_type.39
  353.0 0.7 copy-done.3
  353.7 2.5 convert_element_type.37
  356.2 0.0 copy-done.2
  356.2 2.5 convert_element_type.40
  358.7 1.4 fusion
  360.1 0.0 copy-done.7
  360.1 0.7 slice_bitcast_fusion
  360.8 4.3 %convert_element_type.41 = f32[2,1024,512]{2,1,0:T(8,128)} convert(bf16[2,1024,512]{2,1,0:T(8,128)(2,1)} %get-tuple-element.60) | non-fusion elementwise | flops 1048576 | bytes 6291456 | tf_op jit(solution)/shard_map/convert_element_type | solution.py:1475
  365.1 2.6 convert_element_type.42
  367.7 2.5 convert_element_type.43
  370.2 0.8 copy.36
  371.0 0.8 copy.37
  (14 shorter events, 0.0 us)
Async XLA Ops:
  7.2 353.6 %all-reduce.3.cloned.1.call-start = ((), (), s32[]{:S(2)}) async-start(), calls=%async_computation | async-start | bytes 12582912 | tf_op jit(solution)/shard_map/psum | solution.py:1466
  345.8 5.6 %copy-start.4 = (bf16[1024,512]{1,0:T(8,128)(2,1)S(1)}, bf16[1024,512]{1,0:T(8,128)(2,1)}, u32[]{:S(2)}) copy-start(bf16[1024,512]{1,0:T(8,128)(2,1)} %get-tuple-element.54) | copy-start | bytes 3145732
  351.4 2.3 copy-start.3
  353.7 2.5 copy-start.2
  356.2 3.9 %copy-start.7 = (f32[40,1024]{1,0:T(8,128)S(1)}, f32[40,1024]{1,0:T(8,128)}, u32[]{:S(2)}) copy-start(f32[40,1024]{1,0:T(8,128)} %get-tuple-element.56) | copy-start | bytes 491524
  360.8 4.4 %copy-start.1 = (bf16[2,1024,512]{2,1,0:T(8,128)(2,1)S(1)}, bf16[2,1024,512]{2,1,0:T(8,128)(2,1)}, u32[]{:S(2)}) copy-start(bf16[2,1024,512]{2,1,0:T(8,128)(2,1)} %get-tuple-element.61) | copy-start | bytes 6291460
  365.1 2.6 copy-start
  367.7 2.5 copy-start.6
  367.7 3.3 copy-start.5
Sparse Core Ops, SparseCore 0:
  198.3 136.1 all-reduce.2

commit v5 on v4

--- a/solution.py
+++ b/solution.py
@@ -184,13 +184,16 @@
 
 def moe_kernel(
     ffn, cot, wr, w_gate, w_up, w_down,
-    ret, mixed, grad_g, grad_u, grad_d,
+    ret, mixed, own_gu, own_down,
     rows, sums, wgu, wd, held, pair, inner, dgu, mixing, back, cotv, before, chosen, gate_rows, grad_rows, stage,
-    ag_send, ag_recv, rs_send, rs_recv, w_sem, cot_sem, stage_sem, half_sem, credit,
+    mate_rows, gu_sums, down_sums, ring_rows,
+    ag_send, ag_recv, rs_send, rs_recv, w_sem, cot_sem, stage_sem, mate_send, mate_recv, x_send, x_recv, credit,
 ):
     torus = Torus()
+    place, place_of = everywhere()
     barrier = pltpu.get_barrier_semaphore()
-    for device in torus.neighbours():
+    peers = [*torus.neighbours(), place_of("core", 1), place_of("x", 1), place_of("x", -1)]
+    for device in peers:
         pl.semaphore_signal(barrier, inc=1, device_id=device, device_id_type=MESH)
 
     weights = [
@@ -209,7 +212,7 @@
 
     cot_copy(0).start()
     rows[pl.ds(pl.multiple_of(torus.expert * ROWS, ROWS), ROWS)] = ffn[...]
-    pl.semaphore_wait(barrier, 4)
+    pl.semaphore_wait(barrier, len(peers))
 
     def gather(number, axis, other, low):
         return Gather(torus, rows, ag_send, ag_recv, number, axis, other, low, ROWS // 4, ROWS // 4, ROWS)
@@ -242,9 +245,6 @@
 
     def stage_copy(slot, target):
         return pltpu.make_async_copy(stage.at[slot], target, stage_sem.at[slot])
-
-    def half_copy(slot, half, target):
-        return pltpu.make_async_copy(stage.at[slot, :, pl.ds(half * 512, 512)], target, half_sem.at[slot, half])
 
     expert_rows = lax.broadcasted_iota(jnp.int32, (EXPERTS, ROWS), 0)
 
@@ -387,56 +387,63 @@
     a_last = Scatter(torus, sums, rows, rs_send, rs_recv, 8, 4 * 384, "y", 0, 0, 64, 64)
     b_last = Scatter(torus, sums, rows, rs_send, rs_recv, 9, 1920 + 4 * 432, "z", 0, 128, 80, 64)
 
-    def write_pair(low, high):
-        @pl.loop(low, high)
-        def _(k):
-            slot = k % 2
-            e, c = k // 4, k % 4
-
-            @pl.when(k < 2)
-            def _():
-                stage_copy(slot, grad_d.at[0, pl.ds(0, 256)]).wait()
-
-            @pl.when(k >= 2)
-            def _():
-                half_copy(slot, 0, grad_g.at[0, pl.ds(0, 256)]).wait()
-                half_copy(slot, 1, grad_u.at[0, pl.ds(0, 256)]).wait()
-
-            columns = pl.ds(pl.multiple_of(c * 256, 256), 256)
-            stage[slot] = dot_tn(held[e, :, columns], dgu[e]).astype(jnp.bfloat16)
-            half_copy(slot, 0, grad_g.at[e, columns]).start()
-            half_copy(slot, 1, grad_u.at[e, columns]).start()
-
-    def write_down():
-        @pl.loop(0, 4)
-        def _(k):
-            slot = k % 2
-            e, c = k // 2, k % 2
-
-            @pl.when(k < 2)
-            def _():
-                half_copy(slot, 0, grad_g.at[0, pl.ds(0, 256)]).wait()
-                half_copy(slot, 1, grad_u.at[0, pl.ds(0, 256)]).wait()
-
-            @pl.when(k >= 2)
-            def _():
-                stage_copy(slot, grad_d.at[0, pl.ds(0, 256)]).wait()
-
-            columns = pl.ds(pl.multiple_of(c * 256, 256), 256)
-            stage[slot] = dot_tn(inner[e, :, columns], pair[e]).astype(jnp.bfloat16)
-            stage_copy(slot, grad_d.at[e, columns]).start()
+    def chunk(e, k):
+        if k < 4:
+            return dot_tn(held[e, :, k * 256 : (k + 1) * 256], dgu[e]).astype(jnp.bfloat16)
+        return dot_tn(inner[e, :, (k - 4) * 256 : (k - 3) * 256], pair[e]).astype(jnp.bfloat16)
+
+    def mate_copy(k):
+        return pltpu.make_async_remote_copy(
+            src_ref=stage.at[k % 2],
+            dst_ref=mate_rows.at[pl.ds(k * 256, 256)],
+            send_sem=mate_send.at[k],
+            recv_sem=mate_recv.at[k],
+            device_id=place_of("core", 1),
+            device_id_type=MESH,
+        )
+
+    line = Line(place, place_of)
+    rings = [
+        Scatter(line, gu_sums, ring_rows, x_send, x_recv, 0, 0, "x", 0, 0, 128, 128),
+        Scatter(line, down_sums, ring_rows, x_send, x_recv, 1, 768, "x", 0, 0, 64, 64),
+    ]
 
     for d in order:
         b_lead[d].first()
         a_lead[d].first()
-    write_pair(0, 4)
+    for k in range(6):
+        if k < 2:
+            stage_copy(k, mixed.at[0]).wait()
+        else:
+            mate_copy(k - 2).wait_send()
+        stage[k % 2] = chunk(1 - place["core"], k)
+        mate_copy(k).start()
+        own = chunk(place["core"], k)
+        if k < 4:
+            gu_sums[k] = own
+        else:
+            down_sums[2 * k - 8] = own[:128]
+            down_sums[2 * k - 7] = own[128:]
     for d in order:
         b_lead[d].second()
         a_lead[d].second()
-    write_pair(4, 8)
-    write_down()
-    for slot in range(2):
-        stage_copy(slot, grad_d.at[0, pl.ds(0, 256)]).wait()
+    for k in range(6):
+        mate_copy(k).wait_recv()
+
+        @pl.loop(0, 4)
+        def _(n):
+            other = mate_rows[pl.ds(pl.multiple_of(k * 256 + n * 64, 64), 64)].astype(jnp.float32)
+            if k < 4:
+                at = (k, pl.ds(pl.multiple_of(n * 64, 64), 64))
+                gu_sums[at] = (gu_sums[at].astype(jnp.float32) + other).astype(jnp.bfloat16)
+            else:
+                at = (2 * k - 8 + n // 2, pl.ds(pl.multiple_of(n % 2 * 64, 64), 64))
+                down_sums[at] = (down_sums[at].astype(jnp.float32) + other).astype(jnp.bfloat16)
+
+    for one in rings:
+        one.first()
+    for one in rings:
+        one.second()
     for d in order:
         b_lead[d].third()
         a_lead[d].third()
@@ -451,8 +458,19 @@
 
     b_last.third(put)
     a_last.third(put)
-    for one in [*a_lead.values(), *b_lead.values(), a_last, b_last]:
+
+    def put_gu(at, total):
+        own_gu[at] = total.astype(jnp.bfloat16)
+
+    def put_down(at, total):
+        own_down[at] = total.astype(jnp.bfloat16)
+
+    rings[0].third(put_gu)
+    rings[1].third(put_down)
+    for one in [*a_lead.values(), *b_lead.values(), a_last, b_last, *rings]:
         one.drain()
+    for k in (4, 5):
+        mate_copy(k).wait_send()
 
 
 def moe(ffn_in, cot_all, router_rows, w_gate, w_up, w_down):
@@ -464,12 +482,11 @@
         out_shape=(
             jax.ShapeDtypeStruct((FULL, 1024), jnp.float32),
             jax.ShapeDtypeStruct((16, ROWS, 1024), low),
-            jax.ShapeDtypeStruct((2, 1024, 512), low),
-            jax.ShapeDtypeStruct((2, 1024, 512), low),
-            jax.ShapeDtypeStruct((2, 512, 1024), low),
+            jax.ShapeDtypeStruct((256, 1024), low),
+            jax.ShapeDtypeStruct((128, 1024), low),
         ),
         in_specs=[vmem, hbm, vmem, hbm, hbm, hbm],
-        out_specs=(vmem, hbm, hbm, hbm, hbm),
+        out_specs=(vmem, hbm, vmem, vmem),
         scratch_shapes=[
             pltpu.VMEM((16 * ROWS, 1024), low),
             pltpu.VMEM((16, FULL, 1024), low),
@@ -487,6 +504,10 @@
             pltpu.VMEM((2, GROUP, 128), jnp.float32),
             pltpu.VMEM((2, GROUP, 128), jnp.float32),
             pltpu.VMEM((2, ROWS, 1024), low),
+            pltpu.VMEM((6 * 256, 1024), low),
+            pltpu.VMEM((4, 256, 1024), low),
+            pltpu.VMEM((4, 128, 1024), low),
+            pltpu.VMEM((1152, 1024), low),
             pltpu.SemaphoreType.DMA((10, 4)),
             pltpu.SemaphoreType.DMA((10, 4)),
             pltpu.SemaphoreType.DMA((10, 4)),
@@ -494,7 +515,10 @@
             pltpu.SemaphoreType.DMA((3,)),
             pltpu.SemaphoreType.DMA,
             pltpu.SemaphoreType.DMA((2,)),
-            pltpu.SemaphoreType.DMA((2, 2)),
+            pltpu.SemaphoreType.DMA((6,)),
+            pltpu.SemaphoreType.DMA((6,)),
+            pltpu.SemaphoreType.DMA((2, 4)),
+            pltpu.SemaphoreType.DMA((2, 4)),
             pltpu.SemaphoreType.REGULAR,
         ],
         compiler_params=pltpu.CompilerParams(
@@ -999,12 +1023,12 @@
 def backward_kernel(
     hidden, ffn_in, cot, tokens, normed, key_raw, mixed_t, queries, log_total,
     routes_t, length, cosine, sine, attn_gain, query_gain, key_gain, ffn_gain, router_rows,
-    returned_all, query_raw_all, mixed_parts, kv_all, w_query, w_key, w_value, w_output,
-    mixed_out, token_grad, early_small, late_small, query_sum, key_sum, value_sum, output_sum,
+    returned_all, query_raw_all, mixed_parts, kv_all, w_query, w_key, w_value, w_output, own_gu, own_down,
+    mixed_out, token_grad, early_small, late_small, query_sum, key_sum, value_sum, output_sum, all_gu, all_down,
     sums, rows, returned, square, kv, hidden_grad, result, branch, grads, delta, query_grad, turned,
     for_mate, from_mate, kv_sums, kv_rows, key_low, value_low,
     held, finals, landing, work, values, small_rows, late_values, late_rows,
-    rs_send, rs_recv, mate_send, mate_recv, kv_send, kv_recv, ar_send, ar_recv, small_send, small_recv, load_sem, out_sem,
+    rs_send, rs_recv, mate_send, mate_recv, kv_send, kv_recv, ar_send, ar_recv, small_send, small_recv, load_sem, out_sem, ex_send, ex_recv,
 ):
     torus = Torus()
     here, device = everywhere()
@@ -1021,6 +1045,12 @@
     ]
     for load in loads:
         load.start()
+    owns = [
+        pltpu.make_async_copy(own_gu, all_gu.at[me], load_sem.at[8]),
+        pltpu.make_async_copy(own_down, all_down.at[me], load_sem.at[9]),
+    ]
+    for copy in owns:
+        copy.start()
 
     expert_rows = lax.broadcasted_iota(jnp.int32, (EXPERTS, ROWS), 0)
     member = jnp.zeros((EXPERTS, ROWS), jnp.float32)
@@ -1073,7 +1103,7 @@
         for q in range(4):
             held[pl.ds(pl.multiple_of(q * 1024 + n * 256, 256), 256)] = part[:, q * 256 : (q + 1) * 256]
 
-    for load in loads[2:]:
+    for load in [*loads[2:], *owns]:
         load.wait()
     pl.semaphore_wait(barrier, len(peers))
 
@@ -1100,6 +1130,11 @@
     ]
     ring = Scatter(Line(here, device), kv_sums, kv_rows, kv_send, kv_recv, 0, 0, "x", 0, 0, 512, 512)
 
+    experts = [
+        Keys(here, device, blocks, ex_send.at[n], ex_recv.at[n]) for n, blocks in enumerate((all_gu, all_down))
+    ]
+    for one in experts:
+        one.start(0, 1, 2)
     for one in early:
         one.begin(0)
     few.begin(0)
@@ -1188,6 +1223,11 @@
         @pl.when(turn == 2)
         def _():
             early_step(2)
+            for one in experts:
+                one.arrive(1)
+                one.start(3, 5)
+                one.arrive(2)
+                one.start(4, 6)
 
         @pl.when(turn == 3)
         def _():
@@ -1280,6 +1320,9 @@
     for one in of_query:
         one.begin(0)
     early_step(6)
+    for one in experts:
+        one.arrive(3, 4)
+        one.start(7)
     for q in range(4):
         outs[q].start()
     early_small[...] = values[4]
@@ -1359,7 +1402,9 @@
     onward(of_keys, 6)
     for q in range(8, 12):
         outs[q].start()
-    for one in [*leads, *lasts, ring, *early, *of_query, *of_keys, few, late_few]:
+    for one in experts:
+        one.arrive(0, 5, 6, 7)
+    for one in [*experts, *leads, *lasts, ring, *early, *of_query, *of_keys, few, late_few]:
         one.drain()
     for turn in (2, 3):
         mate_copy(turn, 0).wait_send()
@@ -1384,9 +1429,11 @@
             shape((1024, 512), low),
             shape((1024, 512), low),
             shape((1024, 1024), low),
+            shape((8, 256, 1024), low),
+            shape((8, 128, 1024), low),
         ),
         in_specs=[vmem] * len(smalls) + [hbm] * len(larges),
-        out_specs=(vmem,) * 4 + (hbm,) * 4,
+        out_specs=(vmem,) * 4 + (hbm,) * 6,
         scratch_shapes=[
             pltpu.VMEM((16, ROWS, 1024), low),
             pltpu.VMEM((10 * 384, 1024), low),
@@ -1424,14 +1471,108 @@
             dma((9, 17)),
             dma((2, 10)),
             dma((2, 10)),
-            dma((8,)),
+            dma((10,)),
             dma((3, 4)),
+            dma((2, 8)),
+            dma((2, 8)),
         ],
         compiler_params=pltpu.CompilerParams(
             collective_id=4, has_side_effects=True, vmem_limit_bytes=66000000
         ),
         cost_estimate=pl.CostEstimate(flops=100 * 10**9, bytes_accessed=60 * 10**6, transcendentals=8 * 10**6),
     )(*smalls, *larges)
+
+
+def widen_kernel(
+    early, late, mixed, tokens, query, key, value, output, gate_up, down,
+    ffn_gain, attn_gain, query_gain, key_gain, router,
+    mixed_out, token_out, query_out, key_out, value_out, output_out, gate_out, up_out, down_out,
+    query_in, key_in, value_in, output_in, gate_up_in, down_in,
+    query_wide, key_wide, value_wide, output_wide, gate_up_wide, down_wide,
+    in_sem, out_sem,
+):
+    through = [
+        pltpu.make_async_copy(mixed, mixed_out, out_sem.at[0]),
+        pltpu.make_async_copy(tokens, token_out, out_sem.at[1]),
+    ]
+    for copy in through:
+        copy.start()
+    arrays = (
+        (query, query_in, query_wide, query_out),
+        (output, output_in, output_wide, output_out),
+        (key, key_in, key_wide, key_out),
+        (value, value_in, value_wide, value_out),
+    )
+    parts = []
+    for source, low, wide, target in arrays:
+        for n in range(0, 1024, 512):
+            at = pl.ds(n, 512)
+            parts.append((source.at[at], low.at[at], wide.at[at], [(wide.at[at], target.at[at])]))
+    for block in range(8):
+        rows, e = pl.ds(block // 2 * 256, 256), block % 2
+        wide = gate_up_wide.at[block]
+        targets = [
+            (wide.at[:, pl.ds(0, 512)], gate_out.at[e, rows]),
+            (wide.at[:, pl.ds(512, 512)], up_out.at[e, rows]),
+        ]
+        parts.append((gate_up.at[block], gate_up_in.at[block], wide, targets))
+    for block in range(8):
+        wide = down_wide.at[block]
+        target = down_out.at[block % 2, pl.ds(block // 2 * 128, 128)]
+        parts.append((down.at[block], down_in.at[block], wide, [(wide, target)]))
+    loads = [pltpu.make_async_copy(source, low, in_sem.at[n]) for n, (source, low, _, _) in enumerate(parts)]
+    for load in loads:
+        load.start()
+    ffn_gain[...] = early[EXPERTS]
+    attn_gain[...] = late[0]
+    query_gain[...] = late[1]
+    key_gain[...] = late[2, :512]
+    router[...] = early[:EXPERTS].T
+    stores = []
+    for load, (_, low, wide, targets) in zip(loads, parts):
+        load.wait()
+        wide[...] = low[...].astype(jnp.float32)
+        for source, target in targets:
+            stores.append(pltpu.make_async_copy(source, target, out_sem.at[2 + len(stores)]))
+            stores[-1].start()
+    for copy in [*through, *stores]:
+        copy.wait()
+
+
+def widen(arrays):
+    vmem, hbm = pl.BlockSpec(memory_space=pltpu.VMEM), pl.BlockSpec(memory_space=pl.ANY)
+    low, wide = jnp.bfloat16, jnp.float32
+    shape = jax.ShapeDtypeStruct
+    held = ((1024, 1024), (1024, 512), (1024, 512), (1024, 1024), (8, 256, 1024), (8, 128, 1024))
+    return pl.pallas_call(
+        widen_kernel,
+        name="widen",
+        out_shape=(
+            shape((1024,), wide),
+            shape((1024,), wide),
+            shape((1024,), wide),
+            shape((512,), wide),
+            shape((1024, EXPERTS), wide),
+            shape((ROWS, 1024), low),
+            shape((ROWS, 1024), low),
+            shape((1024, 1024), wide),
+            shape((1024, 512), wide),
+            shape((1024, 512), wide),
+            shape((1024, 1024), wide),
+            shape((2, 1024, 512), wide),
+            shape((2, 1024, 512), wide),
+            shape((2, 512, 1024), wide),
+        ),
+        in_specs=[vmem] * 2 + [hbm] * 8,
+        out_specs=(vmem,) * 5 + (hbm,) * 9,
+        scratch_shapes=[
+            *[pltpu.VMEM(size, low) for size in held],
+            *[pltpu.VMEM(size, wide) for size in held],
+            pltpu.SemaphoreType.DMA((24,)),
+            pltpu.SemaphoreType.DMA((34,)),
+        ],
+        compiler_params=pltpu.CompilerParams(vmem_limit_bytes=56 * 2**20),
+    )(*arrays)
 
 
 def body(
@@ -1462,20 +1603,18 @@
     ffn_in, hidden, mixed_t, queries, log_total, normed, query_raw, key_raw, kv_all, cot_all = forward(
         tokens[0], cotangent[0], routes_t, length, cosine, sine_table, gains, weights
     )
-    returned, mixed_parts, *expert_grads = moe(ffn_in, cot_all, router_rows, w_gate, w_up, w_down)
-    expert_sums = lax.psum(tuple(expert_grads), "dp")
-    mixed_out, token_grad, early_small, late_small, *weight_sums = backward(
+    returned, mixed_parts, own_gu, own_down = moe(ffn_in, cot_all, router_rows, w_gate, w_up, w_down)
+    mixed_low, token_low, early_small, late_small, *sums = backward(
         (
             hidden, ffn_in, cotangent[0], tokens[0], normed, key_raw, mixed_t, queries, log_total, routes_t,
             length, cosine, sine_table, *gains, router_rows,
         ),
-        (returned, query_raw, mixed_parts, kv_all.reshape(8 * 1024, ROWS), *weights),
+        (returned, query_raw, mixed_parts, kv_all.reshape(8 * 1024, ROWS), *weights, own_gu, own_down),
     )
-    query_w_sum, key_w_sum, value_w_sum, output_w_sum = [part.astype(jnp.float32) for part in weight_sums]
-    gate_w_sum, up_w_sum, down_w_sum = [part.astype(jnp.float32) for part in expert_sums]
-    router_sum = early_small[:EXPERTS].T
-    ffn_gain_sum, attn_gain_sum, query_gain_sum = early_small[EXPERTS], late_small[0], late_small[1]
-    key_gain_sum = late_small[2, :512]
+    (
+        ffn_gain_sum, attn_gain_sum, query_gain_sum, key_gain_sum, router_sum, mixed_out, token_grad,
+        query_w_sum, key_w_sum, value_w_sum, output_w_sum, gate_w_sum, up_w_sum, down_w_sum,
+    ) = widen((early_small, late_small, mixed_low, token_low, *sums))
     return (
         mixed_out[None],
         token_grad[None],

time: 379 us -> 396 us (1.045); the launches traced: 379 us -> 388 us
  Pallas kernels: 337 us -> 384 us
  other arithmetic: 19.7 us -> 0.84 us
  between operations: 14.8 us -> 1.78 us
  local copies, waits for them, and re-layouts: 7.18 us -> 1.87 us
    pallas_call x0 -> x1, Pallas kernels: none -> 35.2 us  [widen(): pl.pallas_call(widen_kernel, name='widen', out_shape=(shape((1024,), wide...]
    convert_element_type x7 -> x0, other arithmetic: 18.8 us -> none  [body(): part.astype(jnp.float32)]
    pallas_call x1, Pallas kernels: 148 us -> 158 us  [backward(): pl.pallas_call(backward_kernel, name='backward', out_shape=(shape((ROWS,...]
    slice x3 -> x0, local copies, waits for them, and re-layouts: 4.17 us -> none  [the longest x1 1.44 us: body(): late_small[1]]
  transfers between devices with their start and end apart: 1 -> 0, of which waited for: 0 -> 0; matrix products, arithmetic and copies ran while one was open for 4% -> 0% of each run, Pallas kernels for 39% -> 0%
where the time goes in v5:
time: 396 us; the launch traced here: 388 us
  Pallas kernels  384 us (97%)
    pallas_call x1, Pallas kernels, backward(): pl.pallas_call(backward_kernel, name='backward', out_shape=(shape((ROWS,...  158 us
    pallas_call x1, Pallas kernels, moe(): pl.pallas_call(moe_kernel, name='moe', out_shape=(jax.ShapeDtypeStruct((F...  130 us
    pallas_call x1, Pallas kernels, forward(): pl.pallas_call(forward_kernel, name='forward', out_shape=(shape((ROWS, 10...  59.9 us
    pallas_call x1, Pallas kernels, widen(): pl.pallas_call(widen_kernel, name='widen', out_shape=(shape((1024,), wide...  35.2 us

profile of v5, /device:TPU:1, one launch (start us, length us, event | category | flops | bytes accessed | tf_op | source)
XLA Modules:
  0.0 388.2 jit_solution(17950807650320546754)
XLA Ops:
  1.3 0.8 multiply_sine_fusion
  2.1 59.9 %forward.1 = (bf16[256,1024]{1,0:T(8,128)(2,1)}, f32[256,1024]{1,0:T(8,128)}, bf16[1024,256]{1,0:T(8,128)(2,1)}, bf16[8,64,512]{2,1,0:T(8,128)(2,1)}, f32[8,1,51...) custom-call(bf16[256,1024]{1,0:T(8,128)(2,1)} %bitcast.12, ...), custom_call_target="tpu_custom_call" | custom-call | tf_op jit(solution)/shard_map/forward/pallas_call | solution.py:795
  62.1 130.3 %moe.1 = (f32[272,1024]{1,0:T(8,128)}, bf16[16,256,1024]{2,1,0:T(8,128)(2,1)}, bf16[256,1024]{1,0:T(8,128)(2,1)}, bf16[128,1024]{1,0:T(8,128)(2,1)}) custom-call(bf16[256,1024]{1,0:T(8,128)(2,1)} %get-tuple-element.53.ffn.ffn_in, bf16[4352,1024]{1,0:T(8,128)(2,1)} %get-tuple-element.59.cot, bf16[32,1024]{1,0:T(8,128)(2,1)} %bitcast.21, ...), custom_call_target="tpu_custom_call" | custom-call | flops 49999998976 | bytes 40000000 | tf_op jit(solution)/shard_map/moe/pallas_call | solution.py:479
  192.4 158.2 %backward.1 = (bf16[256,1024]{1,0:T(8,128)(2,1)}, bf16[256,1024]{1,0:T(8,128)(2,1)}, f32[40,1024]{1,0:T(8,128)}, f32[8,1024]{1,0:T(8,128)}, bf16[1024,1024]{1,0:...) custom-call(f32[256,1024]{1,0:T(8,128)} %get-tuple-element.52.hidden, ...), custom_call_target="tpu_custom_call" | custom-call | flops 99999997952 | bytes 60000000 | tf_op jit(solution)/shard_map/backward/pallas_call | solution.py:1420
  350.7 35.2 %widen.1 = (f32[1024]{0:T(1024)}, f32[1024]{0:T(1024)}, f32[1024]{0:T(1024)}, f32[512]{0:T(512)}, f32[1024,32]{1,0:T(8,128)}, /*index=5*/bf16[256,1024]{1,0:T(8,...) custom-call(f32[40,1024]{1,0:T(8,128)} %get-tuple-element.66.early, ...), custom_call_target="tpu_custom_call" | custom-call | tf_op jit(solution)/shard_map/widen/pallas_call | solution.py:1547
  385.9 1.9 copy.30
  (2 shorter events, 0.0 us)
